TPU v7x, 128 devices: a whole 4x4x4 slice. The times are simulated.
128 devices in a mesh: fsdp: 16 (over x_hi, z, core), seq: 8 (over x_lo, y).
Axes of the slice: x: 4 (x_hi: 2, x_lo: 2; x = x_hi * 2 + x_lo), y: 4, z: 4, core: 2. Of those that a mesh axis runs over, the one named last changes fastest.
Arguments:
- tokens: bfloat16 [16384, 1536], P(('fsdp', 'seq')), may hold values from -6 to 6
- gain_one: bfloat16 [1536], P(('fsdp', 'seq')), may hold values from 0.099609375 to 1.8984375
- w_qkv: bfloat16 [1536, 2560], P(('fsdp', 'seq')), may hold values from -0.21875 to 0.21875
- w_out: bfloat16 [1536, 1536], P(('fsdp', 'seq')), may hold values from -0.625 to 0.625
- gain_two: bfloat16 [1536], P(('fsdp', 'seq')), may hold values from 0.099609375 to 1.8984375
- w_router: bfloat16 [1536, 4], P(('fsdp', 'seq')), may hold values from -0.109375 to 0.109375
- w_gate: bfloat16 [4, 1536, 1024], P(None, ('fsdp', 'seq')), may hold values from -0.15625 to 0.15625
- w_up: bfloat16 [4, 1536, 1024], P(None, ('fsdp', 'seq')), may hold values from -0.15625 to 0.15625
- w_down: bfloat16 [4, 1024, 1536], P(None, ('fsdp', 'seq')), may hold values from -0.375 to 0.375
- doc_starts: int32 [34], replicated, may hold values from 0 to 16384, as said below
- routes: int32 [16384, 2], P(('fsdp', 'seq')), may hold values from 0 to 3, all different within a row; in each aligned block of 128 rows (0 to 127, 128 to 255, ...) at most 80 rows name the same one
- cotangent: bfloat16 [16384, 1536], P(('fsdp', 'seq')), may hold values from -6 to 6
Outputs:
- output: bfloat16 [16384, 1536], P(('fsdp', 'seq'))
- grad_input: float32 [16384, 1536], P(('fsdp', 'seq'))
- grad_gain_one: float32 [1536], P(('fsdp', 'seq'))
- grad_w_qkv: float32 [1536, 2560], P(('fsdp', 'seq'))
- grad_w_out: float32 [1536, 1536], P(('fsdp', 'seq'))
- grad_gain_two: float32 [1536], P(('fsdp', 'seq'))
- grad_w_router: float32 [1536, 4], P(('fsdp', 'seq'))
- grad_w_gate: float32 [4, 1536, 1024], P(None, ('fsdp', 'seq'))
- grad_w_up: float32 [4, 1536, 1024], P(None, ('fsdp', 'seq'))
- grad_w_down: float32 [4, 1024, 1536], P(None, ('fsdp', 'seq'))
Inputs may be any that keep to these rules, and one draw needn't show every extreme that they name: Sorted, not falling, with doc_starts[0] = 0; entries equal to 16384 start no document. A document runs from one start to the next larger one, the last to 16384; each has at most 4096 tokens and one has exactly 4096. Outside that one, each group of 8 devices along seq holds one start on its first device and one on its last. `routes`: A token's two experts differ. At most 80 of one device's 128 tokens name one expert, and on some devices one expert is named by exactly 80.
All inputs are finite; a program needn't handle non-finite values.
Results may differ from a plain program's by a relative error of at most 0.02.
The roundings to bfloat16 on the way count: a program that leaves them out, or rounds other values in their place, can miss the bound.
Values may be sent and summed in bfloat16 or wider, within the bound.
A program may use at most 320 MiB of HBM per device.

v0:
```python
import math

import jax
import jax.numpy as jnp
from jax import lax
from jax.sharding import PartitionSpec as P

QUERY_HEADS = 24
KEY_VALUE_HEADS = 8
HEAD_WIDTH = 64
EXPERTS = 4
LOOK = 4
CAP = 80


EPS = 1e-06
NEGATIVE = -1e30
HIGH = lax.Precision.HIGHEST


def side_by_side(arrays, axis, split_dim, concat_dim, along):
    ends, at = ([], 0)
    for a in arrays[:-1]:
        at += a.shape[along]
        ends.append(at)
    both = jnp.concatenate(arrays, axis=along)
    return tuple(
        jnp.split(
            lax.all_to_all(both, axis, split_axis=split_dim, concat_axis=concat_dim, tiled=True),
            ends,
            axis=along,
        )
    )


def side_by_side_2(arrays, axis, dim, along):
    ends, at = ([], 0)
    for a in arrays[:-1]:
        at += a.shape[along]
        ends.append(at)
    both = jnp.concatenate(arrays, axis=along)
    return tuple(jnp.split(lax.all_gather(both, axis, axis=dim, tiled=True), ends, axis=along))


def in_one_piece(arrays, axis, dim, along):
    widths = [math.prod(a.shape[along:]) for a in arrays]
    both = jnp.concatenate(
        [a.reshape(*a.shape[:along], w) for a, w in zip(arrays, widths)], axis=along
    )
    result = lax.all_gather(both, axis, axis=dim, tiled=True)
    blocks = jnp.split(result, [sum(widths[:k]) for k in range(1, len(widths))], axis=along)
    return tuple(
        (b.reshape(*result.shape[:along], *a.shape[along:]) for a, b in zip(arrays, blocks))
    )


def from_behind(x, axis, by):
    peers = lax.axis_size(axis)
    pairs = [(i, i + by) for i in range(peers) if 0 <= i + by < peers]
    return lax.ppermute(x, axis, pairs)


def side_by_side_3(arrays, axis, dim, along):
    ends, at = ([], 0)
    for a in arrays[:-1]:
        at += a.shape[along]
        ends.append(at)
    both = jnp.concatenate(arrays, axis=along)
    return tuple(
        jnp.split(lax.psum_scatter(both, axis, scatter_dimension=dim, tiled=True), ends, axis=along)
    )


def unit_rms(values):
    scale = lax.rsqrt(jnp.mean(values * values, axis=-1, keepdims=True) + EPS)
    return (values * scale, scale)


def rms_back(d_normed, unit, scale, gain):
    d_unit = d_normed * gain
    d_values = scale * (d_unit - unit * jnp.mean(d_unit * unit, axis=-1, keepdims=True))
    return (d_values, jnp.sum(d_normed * unit, axis=0))


def doc_number(doc_starts, positions):
    return jnp.sum((doc_starts[None, :] <= positions[:, None]).astype(jnp.int32), axis=1)


def masked_scores(query_blk, rows_of_keys, query_doc, query_pos, key_doc, key_pos):
    raw = jnp.einsum(
        "qgrh,kgh->grqk", query_blk, rows_of_keys, preferred_element_type=jnp.float32
    ) * HEAD_WIDTH ** (-0.5)
    visible = (query_doc[:, None] == key_doc[None, :]) & (key_pos[None, :] <= query_pos[:, None])
    return jnp.where(visible, raw, NEGATIVE)


def column_order(values, outer, inner):
    experts, rows, width = values.shape
    shaped = values.reshape(experts, rows, outer, inner, width // (outer * inner))
    return jnp.transpose(shaped, (0, 1, 3, 2, 4)).reshape(experts, rows, width)


def fetch_columns(w_gate, w_up, w_down):
    fsdp_count = lax.axis_size("fsdp")
    seq_count = lax.axis_size("seq")
    gate_cols, up_cols = side_by_side(
        (column_order(w_gate, fsdp_count, seq_count), column_order(w_up, fsdp_count, seq_count)),
        "seq",
        2,
        1,
        0,
    )
    return (
        *side_by_side_2((gate_cols, up_cols), "fsdp", 1, 0),
        lax.all_gather(w_down, "fsdp", axis=1, tiled=True),
    )


def gather_slots(values):
    return lax.all_gather(values, "seq", axis=1, tiled=True)


def sum_slots(values):
    return lax.psum_scatter(
        values.astype(jnp.bfloat16), "seq", scatter_dimension=1, tiled=True
    ).astype(jnp.float32)


def on_device(
    tokens,
    gain_one,
    w_qkv,
    w_out,
    gain_two,
    w_router,
    w_gate,
    w_up,
    w_down,
    doc_starts,
    routes,
    cotangent,
):
    gain_first, qkv_weight, out_weight, gain_second, router_weight = in_one_piece(
        (gain_one, w_qkv, w_out, gain_two, w_router), ("fsdp", "seq"), 0, 1
    )
    gate_weight, up_weight, down_weight = fetch_columns(w_gate, w_up, w_down)
    gain_first = gain_first.astype(jnp.float32)
    gain_second = gain_second.astype(jnp.float32)
    inputs = tokens.astype(jnp.float32)
    unit_first, scale_first = unit_rms(inputs)
    normed_one = (unit_first * gain_first).astype(jnp.bfloat16)
    query_key_value_rows = jnp.dot(
        normed_one, qkv_weight, preferred_element_type=jnp.float32
    ).astype(jnp.bfloat16)
    by_heads = lax.all_to_all(query_key_value_rows, "seq", split_axis=1, concat_axis=0, tiled=True)
    group_rows = by_heads.shape[0]
    key_value_heads = KEY_VALUE_HEADS // lax.axis_size("seq")
    heads_per_group = QUERY_HEADS // KEY_VALUE_HEADS
    head_layout = by_heads.reshape(group_rows, key_value_heads, heads_per_group + 2, HEAD_WIDTH)
    query_rows = head_layout[:, :, :heads_per_group, :]
    keyval = head_layout[:, :, heads_per_group:, :].reshape(
        group_rows, key_value_heads * 2 * HEAD_WIDTH
    )
    group_index = lax.axis_index("fsdp")
    earlier = [from_behind(keyval, "fsdp", LOOK - distance) for distance in range(LOOK)]
    window = jnp.concatenate(earlier + [keyval], axis=0)
    window_rows = (LOOK + 1) * group_rows
    window_grid = window.reshape(window_rows, key_value_heads, 2, HEAD_WIDTH)
    rows_of_keys = window_grid[:, :, 0, :]
    rows_of_values = window_grid[:, :, 1, :]
    key_pos = (group_index - LOOK) * group_rows + jnp.arange(window_rows, dtype=jnp.int32)
    key_doc = doc_number(doc_starts, key_pos)
    rows_per_block = min(512, group_rows)
    count_of_blocks = group_rows // rows_per_block
    blocked_queries = query_rows.reshape(
        count_of_blocks, rows_per_block, key_value_heads, heads_per_group, HEAD_WIDTH
    )
    pos_blocks = key_pos[LOOK * group_rows :].reshape(count_of_blocks, rows_per_block)
    doc_blocks = key_doc[LOOK * group_rows :].reshape(count_of_blocks, rows_per_block)

    def forward_block(pieces):
        query_blk, pos_blk, doc_blk = pieces
        scores = masked_scores(query_blk, rows_of_keys, doc_blk, pos_blk, key_doc, key_pos)
        row_peak = jnp.max(scores, axis=-1, keepdims=True)
        exp_scores = jnp.exp(scores - row_peak)
        row_total = jnp.sum(exp_scores, axis=-1, keepdims=True)
        attn_probs = (exp_scores / row_total).astype(jnp.bfloat16)
        attended_blk = jnp.einsum(
            "grqk,kgh->qgrh", attn_probs, rows_of_values, preferred_element_type=jnp.float32
        )
        return (attended_blk, (row_peak + jnp.log(row_total))[..., 0])

    attended_blocks, logsum_blocks = lax.map(
        forward_block, (blocked_queries, pos_blocks, doc_blocks)
    )
    heads_low = attended_blocks.reshape(
        group_rows, key_value_heads * heads_per_group * HEAD_WIDTH
    ).astype(jnp.bfloat16)
    attended_tok = lax.all_to_all(heads_low, "seq", split_axis=0, concat_axis=1, tiled=True)
    branch = jnp.dot(attended_tok, out_weight, preferred_element_type=jnp.float32)
    residual = inputs + branch
    unit_second, scale_second = unit_rms(residual)
    normed_two = (unit_second * gain_second).astype(jnp.bfloat16)
    router_logits = jnp.dot(normed_two, router_weight, preferred_element_type=jnp.float32)
    router_probs = jax.nn.softmax(router_logits, axis=-1)
    expert_ids = jnp.arange(EXPERTS, dtype=jnp.int32)
    picked_mask = (routes[:, :, None] == expert_ids[None, None, :]).astype(jnp.int32)
    flat_pick = picked_mask.reshape(-1, EXPERTS)
    earlier_count = jnp.cumsum(flat_pick, axis=0) - flat_pick
    slot_index = jnp.sum(earlier_count * flat_pick, axis=1).reshape(routes.shape)
    slot_ids = jnp.arange(CAP, dtype=jnp.int32)
    slot_match = (routes[None, None, :, :] == expert_ids[:, None, None, None]) & (
        slot_index[None, None, :, :] == slot_ids[None, :, None, None]
    )
    gate_probs = jnp.take_along_axis(router_probs, routes, axis=1)
    dispatch = jnp.any(slot_match, axis=-1).astype(jnp.bfloat16)
    combine = jnp.sum(jnp.where(slot_match, gate_probs[None, None, :, :], 0.0), axis=-1)
    expert_in = jnp.einsum(
        "ect,td->ecd", dispatch, normed_two, preferred_element_type=jnp.float32
    ).astype(jnp.bfloat16)
    slots_in = gather_slots(expert_in)
    gate_pre = jnp.einsum("ecd,edf->ecf", slots_in, gate_weight, preferred_element_type=jnp.float32)
    up_pre = jnp.einsum("ecd,edf->ecf", slots_in, up_weight, preferred_element_type=jnp.float32)
    sigmoid_gate = jax.nn.sigmoid(gate_pre)
    silu_gate = gate_pre * sigmoid_gate
    hidden = (silu_gate * up_pre).astype(jnp.bfloat16)
    expert_part = jnp.einsum(
        "ecf,efd->ecd", hidden, down_weight, preferred_element_type=jnp.float32
    )
    expert_out = sum_slots(expert_part)
    moe_out = jnp.einsum("ect,ecd->td", combine, expert_out, precision=HIGH)
    output = (residual + moe_out).astype(jnp.bfloat16)
    grad_out = cotangent.astype(jnp.float32)
    d_expert = jnp.einsum("ect,td->ecd", combine, grad_out, precision=HIGH).astype(jnp.bfloat16)
    d_slot_gate = jnp.einsum("ecd,td->ect", expert_out, grad_out, precision=HIGH)
    d_gates = jnp.sum(jnp.where(slot_match, d_slot_gate[..., None], 0.0), axis=(0, 1))
    d_router = jnp.sum(picked_mask.astype(jnp.float32) * d_gates[:, :, None], axis=1)
    d_logits = (
        router_probs * (d_router - jnp.sum(router_probs * d_router, axis=-1, keepdims=True))
    ).astype(jnp.bfloat16)
    d_expert_all = gather_slots(d_expert)
    d_hidden = jnp.einsum(
        "ecd,efd->ecf", d_expert_all, down_weight, preferred_element_type=jnp.float32
    )
    d_gate_pre = (
        d_hidden * up_pre * sigmoid_gate * (1.0 + gate_pre * (1.0 - sigmoid_gate))
    ).astype(jnp.bfloat16)
    d_up_pre = (d_hidden * silu_gate).astype(jnp.bfloat16)
    grad_down = jnp.einsum("ecf,ecd->efd", hidden, d_expert_all, preferred_element_type=jnp.float32)
    grad_gate = jnp.einsum("ecd,ecf->edf", slots_in, d_gate_pre, preferred_element_type=jnp.float32)
    grad_up = jnp.einsum("ecd,ecf->edf", slots_in, d_up_pre, preferred_element_type=jnp.float32)
    grad_router = jnp.einsum("td,te->de", normed_two, d_logits, preferred_element_type=jnp.float32)
    d_in_part = jnp.einsum(
        "ecf,edf->ecd", d_gate_pre, gate_weight, preferred_element_type=jnp.float32
    )
    d_in_part = d_in_part + jnp.einsum(
        "ecf,edf->ecd", d_up_pre, up_weight, preferred_element_type=jnp.float32
    )
    d_expert_in = sum_slots(d_in_part)
    d_normed_two = jnp.einsum(
        "ect,ecd->td", dispatch.astype(jnp.float32), d_expert_in, precision=HIGH
    )
    d_normed_two = d_normed_two + jnp.einsum(
        "te,de->td", d_logits, router_weight, preferred_element_type=jnp.float32
    )
    d_norm_two, grad_gain_second = rms_back(d_normed_two, unit_second, scale_second, gain_second)
    d_resid = grad_out + d_norm_two
    d_branch = d_resid.astype(jnp.bfloat16)
    grad_out_weight = jnp.einsum(
        "tk,td->kd", attended_tok, d_branch, preferred_element_type=jnp.float32
    )
    d_attended_tok = jnp.einsum(
        "td,kd->tk", d_branch, out_weight, preferred_element_type=jnp.float32
    ).astype(jnp.bfloat16)
    d_heads = lax.all_to_all(d_attended_tok, "seq", split_axis=1, concat_axis=0, tiled=True)
    d_out_blocks = d_heads.reshape(
        count_of_blocks, rows_per_block, key_value_heads, heads_per_group, HEAD_WIDTH
    )

    def backward_block(carry, pieces):
        d_keys, d_values = carry
        query_blk, pos_blk, doc_blk, logsum_blk, d_out_blk = pieces
        scores = masked_scores(query_blk, rows_of_keys, doc_blk, pos_blk, key_doc, key_pos)
        attn_probs = jnp.exp(scores - logsum_blk[..., None])
        d_probs = jnp.einsum(
            "qgrh,kgh->grqk", d_out_blk, rows_of_values, preferred_element_type=jnp.float32
        )
        row_delta = jnp.sum(attn_probs * d_probs, axis=-1, keepdims=True)
        d_scores = (attn_probs * (d_probs - row_delta)).astype(jnp.bfloat16)
        d_query = jnp.einsum(
            "grqk,kgh->qgrh", d_scores, rows_of_keys, preferred_element_type=jnp.float32
        ) * HEAD_WIDTH ** (-0.5)
        d_keys = d_keys + jnp.einsum(
            "grqk,qgrh->kgh", d_scores, query_blk, preferred_element_type=jnp.float32
        ) * HEAD_WIDTH ** (-0.5)
        d_values = d_values + jnp.einsum(
            "grqk,qgrh->kgh",
            attn_probs.astype(jnp.bfloat16),
            d_out_blk,
            preferred_element_type=jnp.float32,
        )
        return ((d_keys, d_values), d_query)

    zero_grad = jnp.zeros((window_rows, key_value_heads, HEAD_WIDTH), jnp.float32)
    (d_keys, d_values), d_query_blocks = lax.scan(
        backward_block,
        (zero_grad, zero_grad),
        (blocked_queries, pos_blocks, doc_blocks, logsum_blocks, d_out_blocks),
    )
    d_window = jnp.stack([d_keys, d_values], axis=2).reshape(
        window_rows, key_value_heads * 2 * HEAD_WIDTH
    )
    d_own = d_window[LOOK * group_rows :]
    for distance in range(1, LOOK + 1):
        back_piece = d_window[(LOOK - distance) * group_rows : (LOOK - distance + 1) * group_rows]
        d_own = d_own + from_behind(back_piece.astype(jnp.bfloat16), "fsdp", -distance).astype(
            back_piece.dtype
        )
    d_query_all = d_query_blocks.reshape(group_rows, key_value_heads, heads_per_group, HEAD_WIDTH)
    d_grid = jnp.concatenate(
        [d_query_all, d_own.reshape(group_rows, key_value_heads, 2, HEAD_WIDTH)], axis=2
    )
    d_rows = d_grid.reshape(
        group_rows, key_value_heads * (heads_per_group + 2) * HEAD_WIDTH
    ).astype(jnp.bfloat16)
    d_qkv = lax.all_to_all(d_rows, "seq", split_axis=0, concat_axis=1, tiled=True)
    grad_qkv = jnp.einsum("td,tk->dk", normed_one, d_qkv, preferred_element_type=jnp.float32)
    d_normed_one = jnp.einsum("tk,dk->td", d_qkv, qkv_weight, preferred_element_type=jnp.float32)
    d_norm_one, grad_gain_first = rms_back(d_normed_one, unit_first, scale_first, gain_first)
    grad_input = d_resid + d_norm_one
    shard_gain_one, shard_qkv, shard_out, shard_gain_two, shard_router = (
        lax.psum_scatter(grad_gain_first, ("fsdp", "seq"), scatter_dimension=0, tiled=True),
        lax.psum_scatter(grad_qkv, ("fsdp", "seq"), scatter_dimension=0, tiled=True),
        lax.psum_scatter(grad_out_weight, ("fsdp", "seq"), scatter_dimension=0, tiled=True),
        lax.psum_scatter(grad_gain_second, ("fsdp", "seq"), scatter_dimension=0, tiled=True),
        lax.psum_scatter(grad_router, ("fsdp", "seq"), scatter_dimension=0, tiled=True),
    )
    group_gate, group_up, shard_down = (
        *tuple(
            (
                part.astype(jnp.float32)
                for part in side_by_side_3(
                    (grad_gate.astype(jnp.bfloat16), grad_up.astype(jnp.bfloat16)), "fsdp", 1, 0
                )
            )
        ),
        lax.psum_scatter(
            grad_down.astype(jnp.bfloat16), "fsdp", scatter_dimension=1, tiled=True
        ).astype(jnp.float32),
    )
    back_gate, back_up = tuple(
        (
            part.astype(jnp.float32)
            for part in side_by_side(
                (group_gate.astype(jnp.bfloat16), group_up.astype(jnp.bfloat16)), "seq", 1, 2, 0
            )
        )
    )
    shard_gate = column_order(back_gate, lax.axis_size("seq"), lax.axis_size("fsdp"))
    shard_up = column_order(back_up, lax.axis_size("seq"), lax.axis_size("fsdp"))
    return (
        output,
        grad_input,
        shard_gain_one,
        shard_qkv,
        shard_out,
        shard_gain_two,
        shard_router,
        shard_gate,
        shard_up,
        shard_down,
    )


def solution(mesh):
    in_specs = (
        P(("fsdp", "seq"), None),
        P(("fsdp", "seq")),
        P(("fsdp", "seq"), None),
        P(("fsdp", "seq"), None),
        P(("fsdp", "seq")),
        P(("fsdp", "seq"), None),
        P(None, ("fsdp", "seq"), None),
        P(None, ("fsdp", "seq"), None),
        P(None, ("fsdp", "seq"), None),
        P(),
        P(("fsdp", "seq"), None),
        P(("fsdp", "seq"), None),
    )
    out_specs = (
        P(("fsdp", "seq"), None),
        P(("fsdp", "seq"), None),
        P(("fsdp", "seq")),
        P(("fsdp", "seq"), None),
        P(("fsdp", "seq"), None),
        P(("fsdp", "seq")),
        P(("fsdp", "seq"), None),
        P(None, ("fsdp", "seq"), None),
        P(None, ("fsdp", "seq"), None),
        P(None, ("fsdp", "seq"), None),
    )
    return jax.shard_map(
        on_device, mesh=mesh, in_specs=in_specs, out_specs=out_specs, check_vma=False
    )
```

profile of v0, /device:TPU:3, one launch (start us, length us, event | category | flops | bytes accessed | tf_op | source)
XLA Modules:
  0.0 2067.9 jit_solution(4617276181494960731)
XLA Ops:
  35.4 308.4 %all-gather.15.cloned.1.call-done = bf16[128,12,4102]{2,1,0:T(8,128)(2,1)} async-done(((bf16[1,12,4102]{2,1,0:T(8,128)(2,1)}), bf16[128,12,4102]{2,1,0:T(8,128)(2,1)}) %all-gather.15.cloned.1.call-update) | async-done | bytes 12601360 | tf_op jit(solution)/shard_map/all_gather | solution.py:50
  343.8 20.1 reshape.380
  415.3 91.3 %while.28 = (s32[]{:T(128)}, bf16[2,512,1,3,64]{1,4,3,2,0:T(8,128)(2,1)S(1)}, f32[2,1,3,512]{3,2,1,0:T(4,128)S(1)}, s32[2,512]{1,0:T(2,128)S(1)}, s32[5120]{0:T(...) while((s32[]{:T(128)}, ...), condition=%wide.region_5.6_spmd.clone, body=%wide.region_2.5_spmd.clone.sunk | while | flops 2115505664 | bytes 106891392 | solution.py:193
  431.5 14.9 fusion.188
  446.4 15.0 fusion.189
  477.2 14.6 fusion.188
  491.8 14.7 fusion.189
  525.3 88.5 %all-gather.7.cloned.1.call-done = bf16[4,640,1536]{2,1,0:T(8,128)(2,1)} async-done(((bf16[4,80,1536]{2,1,0:T(8,128)(2,1)}), bf16[4,640,1536]{2,1,0:T(8,128)(2,1)}) %all-gather.7.cloned.1.call-update) | async-done | bytes 7864336 | tf_op jit(solution)/shard_map/all_gather | solution.py:120
  624.2 37.7 %all-gather.11.cloned.1.call-done = bf16[4,128,1536]{2,1,0:T(8,128)(2,1)} async-done(((bf16[4,8,1536]{2,1,0:T(8,128)(2,1)}), bf16[4,128,1536]{2,1,0:T(8,128)(2,1)}) %all-gather.11.cloned.1.call-update) | async-done | bytes 1572880 | tf_op jit(solution)/shard_map/all_gather | solution.py:115
  673.8 80.9 %reduce-scatter.12.cloned.1.call-done = bf16[4,80,1536]{2,1,0:T(8,128)(2,1)} async-done(((bf16[4,640,1536]{2,1,0:T(8,128)(2,1)}), bf16[4,80,1536]{2,1,0:T(8,128)(2,1)}) %reduce-scatter.12.cloned.1.call-update) | async-done | bytes 983056 | tf_op jit(solution)/shard_map/reduce_scatter | solution.py:124
  758.8 85.3 %all-gather.13.cloned.1.call-done = bf16[4,640,1536]{2,1,0:T(8,128)(2,1)} async-done(((bf16[4,80,1536]{2,1,0:T(8,128)(2,1)}), bf16[4,640,1536]{2,1,0:T(8,128)(2,1)}) %all-gather.13.cloned.1.call-update) | async-done | bytes 7864336 | tf_op jit(solution)/shard_map/all_gather | solution.py:120
  877.1 79.1 %reduce-scatter.14.cloned.1.call-done = bf16[4,80,1536]{2,1,0:T(8,128)(2,1)} async-done(((bf16[4,640,1536]{2,1,0:T(8,128)(2,1)}), bf16[4,80,1536]{2,1,0:T(8,128)(2,1)}) %reduce-scatter.14.cloned.1.call-update) | async-done | bytes 983056 | tf_op jit(solution)/shard_map/reduce_scatter | solution.py:124
  979.8 195.2 %while.29 = (s32[]{:T(128)}, f32[5120,1,64]{0,2,1:T(8,128)}, f32[5120,1,64]{0,2,1:T(8,128)}, bf16[2,512,1,3,64]{1,4,3,2,0:T(8,128)(2,1)}, bf16[2,512,1,3,64]{1,4...) while((s32[]{:T(128)}, f32[5120,1,64]{0,2,1:T(8,128)}, ...), condition=%wide.region_22.23_spmd.clone, body=%wide.region_20.22_spmd.clone.sunk | while | flops 5160734208 | bytes 325179712 | solution.py:305
  996.8 15.7 fusion.202
  1012.5 23.1 %fusion.199 = (f32[3,512]{1,0:T(4,128)S(1)}, f32[512,3,5120]{2,0,1:T(8,128)}) fusion(f32[512,3,5120]{2,0,1:T(8,128)} %fusion.198, f32[3,512]{1,0:T(4,128)S(1)} %dynamic-slice_bitcast_fusion.2, pred[512,5120]{1,0:T(8,128)(4,1)S(1)} %compare_and_fusion.5, bf16[5120,1,64]{0,2,1:T(8,128)(2,1)S(1)} %copy-done.3, ...), kind=kOutput, calls=%fused_computation.30.clone.1 | convolution fusion | flops 1045953024 | bytes 66402308 | tf_op jit(solution)/shard_map/while/body/eval_jaxpr/qgrh,kgh->grqk/dot_general | solution.py:285
  1035.5 26.0 %fusion.200 = bf16[3,512,5120]{2,1,0:T(8,128)(2,1)} fusion(f32[512,3,5120]{2,0,1:T(8,128)} %get-tuple-element.586, f32[512,3,5120]{2,0,1:T(8,128)} %fusion.198, f32[3,512]{1,0:T(4,128)S(1)} %get-tuple-element.587, f32[3,512]{1,0:T(4,128)S(1)} %dynamic-slice_bitcast_fusion.2, pred[512,5120]{1,0:T(8,128)(4,1)S(1)} %compare_and_fusion.5), kind=kLoop, calls=%fused_computation.35.clone.1 | loop fusion | flops 47185920 | bytes 81276928 | tf_op jit(solution)/shard_map/reshape.53
  1093.3 15.8 fusion.202
  1109.2 23.0 %fusion.199 = (f32[3,512]{1,0:T(4,128)S(1)}, f32[512,3,5120]{2,0,1:T(8,128)}) fusion(f32[512,3,5120]{2,0,1:T(8,128)} %fusion.198, f32[3,512]{1,0:T(4,128)S(1)} %dynamic-slice_bitcast_fusion.2, pred[512,5120]{1,0:T(8,128)(4,1)S(1)} %compare_and_fusion.5, bf16[5120,1,64]{0,2,1:T(8,128)(2,1)S(1)} %copy-done.3, ...), kind=kOutput, calls=%fused_computation.30.clone.1 | convolution fusion | flops 1045953024 | bytes 66402308 | tf_op jit(solution)/shard_map/while/body/eval_jaxpr/qgrh,kgh->grqk/dot_general | solution.py:285
  1132.2 26.0 %fusion.200 = bf16[3,512,5120]{2,1,0:T(8,128)(2,1)} fusion(f32[512,3,5120]{2,0,1:T(8,128)} %get-tuple-element.586, f32[512,3,5120]{2,0,1:T(8,128)} %fusion.198, f32[3,512]{1,0:T(4,128)S(1)} %get-tuple-element.587, f32[3,512]{1,0:T(4,128)S(1)} %dynamic-slice_bitcast_fusion.2, pred[512,5120]{1,0:T(8,128)(4,1)S(1)} %compare_and_fusion.5), kind=kLoop, calls=%fused_computation.35.clone.1 | loop fusion | flops 47185920 | bytes 81276928 | tf_op jit(solution)/shard_map/reshape.53
  1238.0 377.7 %fusion.130 = (f32[16,2560]{1,0:T(8,128)}, f32[16,1536]{1,0:T(8,128)S(1)}) fusion(f32[1536,2560]{1,0:T(8,128)} %fusion.121, f32[1536,1536]{1,0:T(8,128)} %fusion.118), kind=kCustom, calls=%all-reduce-scatter.2 | all-reduce-scatter fusion | flops 8388609 | bytes 25427968
  1642.5 16.1 collective-permute-start.66
  1879.0 62.9 %all-reduce.7 = (f32[1536]{0:T(1024)S(1)}, f32[1536]{0:T(1024)S(1)}, f32[1536,4]{0,1:T(4,128)S(1)}) all-reduce(f32[1536]{0:T(1024)S(1)} %get-tuple-element.347, f32[1536]{0:T(1024)S(1)} %copy-done.79, f32[1536,4]{0,1:T(4,128)S(1)} %copy-done.52), channel_id=4, replica_groups=mesh['fsdp'=16,'seq'=8] {'fsdp','seq'}, use_global_device_ids=true, to_apply=%region_25.26.clone | all-reduce | flops 9216 | bytes 73728
  1943.7 32.6 %concatenate.43 = f32[524,1536]{1,0:T(8,128)S(1)} concatenate(f32[12,1536]{1,0:T(8,128)} %copy-done.56, f32[16,1536]{1,0:T(8,128)} %copy-done.53, f32[16,1536]{1,0:T(8,128)} %copy-done.54, f32[16,1536]{1,0:T(8,128)} %copy-done.55, f32[16,1536]{1,0:T(8,128)} %copy-done.57, f32[16,1536]{1,0:T(8,128)} %copy-done.58, f32[16,1536]{1,0:T(8,128)} %copy-done.59, f32[16,1536]{1,0:T(8,128)} %copy-done.60, ...), dimensions={0} | concatenate | bytes 6438912
  2001.3 57.3 %concatenate.42 = f32[524,2560]{1,0:T(8,128)} concatenate(f32[12,2560]{1,0:T(8,128)} %copy-done.37, f32[16,2560]{1,0:T(8,128)S(1)} %copy-done.36, f32[16,2560]{1,0:T(8,128)} %copy-done.38, f32[16,2560]{1,0:T(8,128)} %copy-done.39, f32[16,2560]{1,0:T(8,128)} %copy-done.40, f32[16,2560]{1,0:T(8,128)} %copy-done.41, f32[16,2560]{1,0:T(8,128)} %copy-done.42, ...), dimensions={0} | concatenate | bytes 10731520
  (546 shorter events, 612.9 us)
Async XLA Ops:
  8.0 335.8 %all-gather.15.cloned.1.call-start = ((), (), s32[]{:S(2)}) async-start(), calls=%async_computation.17 | async-start | bytes 17436672 | tf_op jit(solution)/shard_map/all_gather | solution.py:50
  29.3 343.8 %all-to-all-start.2 = ((bf16[8,2,6144]{2,1,0:T(2,128)(2,1)}), bf16[8,2,6144]{2,1,0:T(2,128)(2,1)S(1)}, u32[]{:S(2)}, u32[]{:S(2)}) async-start(bf16[8,2,6144]{2,1,0:T(2,128)(2,1)} %reshape.409), calls=%async_computation.2 | async-start | bytes 393216 | tf_op jit(solution)/shard_map/all_to_all | solution.py:29
  378.7 146.5 %all-gather.9.cloned.1.call-start = ((), (), s32[]{:S(2)}) async-start(), calls=%async_computation.11 | async-start | bytes 3342336 | tf_op jit(solution)/shard_map/all_gather | solution.py:42
  512.8 101.0 %all-gather.7.cloned.1.call-start = ((), (), s32[]{:S(2)}) async-start(), calls=%async_computation.10 | async-start | bytes 8847360 | tf_op jit(solution)/shard_map/all_gather | solution.py:120
  524.6 137.3 %all-gather.11.cloned.1.call-start = ((), (), s32[]{:S(2)}) async-start(), calls=%async_computation.12 | async-start | bytes 1671168 | tf_op jit(solution)/shard_map/all_gather | solution.py:115
  525.2 229.6 %reduce-scatter.12.cloned.1.call-start = ((), (), s32[]{:S(2)}) async-start(), calls=%async_computation.13 | async-start | bytes 8847360 | tf_op jit(solution)/shard_map/reduce_scatter | solution.py:124
  668.7 175.4 %all-gather.13.cloned.1.call-start = ((), (), s32[]{:S(2)}) async-start(), calls=%async_computation.14 | async-start | bytes 8847360 | tf_op jit(solution)/shard_map/all_gather | solution.py:120
  758.4 197.9 %reduce-scatter.14.cloned.1.call-start = ((), (), s32[]{:S(2)}) async-start(), calls=%async_computation.15 | async-start | bytes 8847360 | tf_op jit(solution)/shard_map/reduce_scatter | solution.py:124
  869.6 880.3 %reduce-scatter.18.cloned.1.call-start = ((), (), s32[]{:S(2)}) async-start(), calls=%async_computation.18 | async-start | bytes 1671168
  1177.1 33.7 %collective-permute-start.7 = (bf16[1024,128]{0,1:T(8,128)(2,1)S(1)}, bf16[1024,128]{0,1:T(8,128)(2,1)S(1)}, u32[]{:S(2)}, u32[]{:S(2)}) collective-permute-start(bf16[1024,128]{0,1:T(8,128)(2,1)S(1)} %bitcast.446), channel_id=1, source_target_pairs={{32,0},{40,8},{48,16},{56,24},{64,32},{72,40},{80,48},{88,56},{96,... | collective-permute-start | bytes 786440 | tf_op jit(solution)/shard_map/ppermute | solution.py:60
  1218.6 532.3 %reduce-scatter.16.cloned.1.call-start = ((), (), s32[]{:S(2)}) async-start(), calls=%async_computation.16 | async-start | bytes 3342336 | tf_op jit(solution)/shard_map/reduce_scatter | solution.py:70
  1615.7 42.9 %collective-permute-start.70 = (f32[16,1536]{1,0:T(8,128)S(1)}, f32[16,1536]{1,0:T(8,128)S(1)}, u32[]{:S(2)}, u32[]{:S(2)}) collective-permute-start(f32[16,1536]{1,0:T(8,128)S(1)} %get-tuple-element.403), channel_id=1, source_target_pairs={{0,31},{1,32},{2,33},{3,34},{4,35},{5,36},{6,37},{7,38},{8,39},{9,... | collective-permute-start | bytes 294920
  1625.5 38.5 %collective-permute-start.69 = (f32[16,1536]{1,0:T(8,128)S(1)}, f32[16,1536]{1,0:T(8,128)S(1)}, u32[]{:S(2)}, u32[]{:S(2)}) collective-permute-start(f32[16,1536]{1,0:T(8,128)S(1)} %get-tuple-element.403), channel_id=1, source_target_pairs={{0,30},{1,31},{2,32},{3,33},{4,34},{5,35},{6,36},{7,37},{8,38},{9,... | collective-permute-start | bytes 294920
  1631.5 35.8 %collective-permute-start.68 = (f32[16,1536]{1,0:T(8,128)S(1)}, f32[16,1536]{1,0:T(8,128)S(1)}, u32[]{:S(2)}, u32[]{:S(2)}) collective-permute-start(f32[16,1536]{1,0:T(8,128)S(1)} %get-tuple-element.403), channel_id=1, source_target_pairs={{0,29},{1,30},{2,31},{3,32},{4,33},{5,34},{6,35},{7,36},{8,37},{9,... | collective-permute-start | bytes 294920
  1772.6 46.5 %collective-permute-start.32 = (f32[16,2560]{1,0:T(8,128)}, f32[16,2560]{1,0:T(8,128)}, u32[]{:S(2)}, u32[]{:S(2)}) collective-permute-start(f32[16,2560]{1,0:T(8,128)} %get-tuple-element.402), channel_id=1, source_target_pairs={{0,25},{1,26},{2,27},{3,28},{4,29},{5,30},{6,31},{7,32},{8,33},{9,... | collective-permute-start | bytes 491528
  1774.8 45.7 %collective-permute-start.31 = (f32[16,2560]{1,0:T(8,128)}, f32[16,2560]{1,0:T(8,128)}, u32[]{:S(2)}, u32[]{:S(2)}) collective-permute-start(f32[16,2560]{1,0:T(8,128)} %get-tuple-element.402), channel_id=1, source_target_pairs={{0,24},{1,25},{2,26},{3,27},{4,28},{5,29},{6,30},{7,31},{8,32},{9,... | collective-permute-start | bytes 491528
  1778.4 49.9 %collective-permute-start.30 = (f32[16,2560]{1,0:T(8,128)}, f32[16,2560]{1,0:T(8,128)}, u32[]{:S(2)}, u32[]{:S(2)}) collective-permute-start(f32[16,2560]{1,0:T(8,128)} %get-tuple-element.402), channel_id=1, source_target_pairs={{0,23},{1,24},{2,25},{3,26},{4,27},{5,28},{6,29},{7,30},{8,31},{9,... | collective-permute-start | bytes 491528
  1790.1 39.5 %collective-permute-start.29 = (f32[16,2560]{1,0:T(8,128)}, f32[16,2560]{1,0:T(8,128)}, u32[]{:S(2)}, u32[]{:S(2)}) collective-permute-start(f32[16,2560]{1,0:T(8,128)} %get-tuple-element.402), channel_id=1, source_target_pairs={{0,22},{1,23},{2,24},{3,25},{4,26},{5,27},{6,28},{7,29},{8,30},{9,... | collective-permute-start | bytes 491528
  1796.1 34.9 %collective-permute-start.28 = (f32[16,2560]{1,0:T(8,128)}, f32[16,2560]{1,0:T(8,128)}, u32[]{:S(2)}, u32[]{:S(2)}) collective-permute-start(f32[16,2560]{1,0:T(8,128)} %get-tuple-element.402), channel_id=1, source_target_pairs={{0,21},{1,22},{2,23},{3,24},{4,25},{5,26},{6,27},{7,28},{8,29},{9,... | collective-permute-start | bytes 491528
  1857.0 119.3 %collective-permute-start.17 = (f32[16,2560]{1,0:T(8,128)}, f32[16,2560]{1,0:T(8,128)}, u32[]{:S(2)}, u32[]{:S(2)}) collective-permute-start(f32[16,2560]{1,0:T(8,128)} %get-tuple-element.402), channel_id=1, source_target_pairs={{0,10},{1,11},{2,12},{3,13},{4,14},{5,15},{6,16},{7,17},{8,18},{9,... | collective-permute-start | bytes 491528
  1864.9 116.1 %collective-permute-start.16 = (f32[16,2560]{1,0:T(8,128)}, f32[16,2560]{1,0:T(8,128)}, u32[]{:S(2)}, u32[]{:S(2)}) collective-permute-start(f32[16,2560]{1,0:T(8,128)} %get-tuple-element.402), channel_id=1, source_target_pairs={{0,9},{1,10},{2,11},{3,12},{4,13},{5,14},{6,15},{7,16},{8,17},{9,1... | collective-permute-start | bytes 491528
  1866.8 116.1 %collective-permute-start.15 = (f32[16,2560]{1,0:T(8,128)}, f32[16,2560]{1,0:T(8,128)}, u32[]{:S(2)}, u32[]{:S(2)}) collective-permute-start(f32[16,2560]{1,0:T(8,128)} %get-tuple-element.402), channel_id=1, source_target_pairs={{0,8},{1,9},{2,10},{3,11},{4,12},{5,13},{6,14},{7,15},{8,16},{9,17... | collective-permute-start | bytes 491528
  1868.7 117.9 %collective-permute-start.14 = (f32[16,2560]{1,0:T(8,128)}, f32[16,2560]{1,0:T(8,128)}, u32[]{:S(2)}, u32[]{:S(2)}) collective-permute-start(f32[16,2560]{1,0:T(8,128)} %get-tuple-element.402), channel_id=1, source_target_pairs={{0,7},{1,8},{2,9},{3,10},{4,11},{5,12},{6,13},{7,14},{8,15},{9,16}... | collective-permute-start | bytes 491528
  1872.8 117.1 %collective-permute-start.13 = (f32[16,2560]{1,0:T(8,128)}, f32[16,2560]{1,0:T(8,128)}, u32[]{:S(2)}, u32[]{:S(2)}) collective-permute-start(f32[16,2560]{1,0:T(8,128)} %get-tuple-element.402), channel_id=1, source_target_pairs={{0,6},{1,7},{2,8},{3,9},{4,10},{5,11},{6,12},{7,13},{8,14},{9,15},... | collective-permute-start | bytes 491528
  (166 other events, 10216.4 us)
Sparse Core Ops, SparseCore 0:
  12.2 331.5 all-gather.14
Sparse Core Ops, SparseCore 1:
  402.4 50.2 all-gather.8
  524.7 89.1 all-gather.6
  616.2 45.7 all-gather.10
  668.8 85.9 reduce-scatter.11
  758.4 85.6 all-gather.12
  869.7 86.5 reduce-scatter.13
  960.0 66.0 reduce-scatter.17
  1223.6 84.8 reduce-scatter.15
where the time goes:
time: 2080 us; the launch traced here: 2070 us
  waiting for transfers between devices  705 us (34%)
  blocking collectives  441 us (21%)
  starting transfers between devices  309 us (15%)
  matrix products  302 us (15%)
  local copies, waits for them, and re-layouts  185 us (9%)
  other arithmetic  107 us (5%)
    unnamed x2, blocking collectives  441 us
    all_gather x1, waiting for transfers between devices, in_one_piece(): result = lax.all_gather(both, axis, axis=dim, tiled=True)  308 us
    unnamed x65, starting transfers between devices  236 us
    all_gather x2, waiting for transfers between devices, gather_slots(): return lax.all_gather(values, 'seq', axis=1, tiled=True)  174 us
    reduce_scatter x2, waiting for transfers between devices, sum_slots(): lax.psum_scatter(values.astype(jnp.bfloat16), 'seq', scatter_dimension=1,...  160 us
    unnamed x209, local copies, waits for them, and re-layouts  136 us
    another operation x6, other arithmetic  55.4 us
    dot_general x4, matrix products, masked_scores(): jnp.einsum('qgrh,kgh->grqk', query_blk, rows_of_keys, preferred_element_t...  53.8 us
  transfers between devices with their start and end apart: 87, of which 15 were waited for; matrix products, arithmetic and copies ran while one was open for 42% of the time, Pallas kernels for 0%

commit v1 on v0

v1 whole, which is shorter than its diff:
```python
import functools

import jax
import jax.numpy as jnp
import numpy as np
from jax import lax
from jax.experimental import pallas as pl
from jax.experimental.pallas import tpu as pltpu
from jax.sharding import PartitionSpec as P

WIDTH = 64
LOOK = 4
EXPERTS = 4
EPS = 1e-06
NEGATIVE = -1e30
BQ = 256
BK = 512
BOTH = ("fsdp", "seq")


def nt(a, b):
    return lax.dot_general(a, b, (((1,), (1,)), ((), ())), preferred_element_type=jnp.float32)


def tn(a, b):
    return lax.dot_general(a, b, (((0,), (0,)), ((), ())), preferred_element_type=jnp.float32)


def nn(a, b):
    return jnp.dot(a, b, preferred_element_type=jnp.float32)


def stack_heads(rows, low):
    heads = rows.shape[1] // WIDTH
    zero = jnp.zeros((rows.shape[0], WIDTH), rows.dtype)
    parts = []
    for h in range(heads):
        part = rows[:, h * WIDTH : (h + 1) * WIDTH]
        parts.append(jnp.concatenate([part, zero] if low else [zero, part], axis=1))
    return jnp.concatenate(parts, axis=0)


def chunk_loops(bounds_ref, step):
    b = pl.program_id(0)
    first, full, diag, end = (bounds_ref[b, i] for i in range(4))
    pl.loop(first, full)(lambda c: step(c, True))
    pl.loop(full, diag)(lambda c: step(c, False))
    pl.loop(diag, end)(lambda c: step(c, True))


def attention_kernel(bounds_ref, lo_ref, q_ref, kv_ref, out_ref, lse_ref, m_ref, l_ref, acc_ref):
    heads = q_ref.shape[1] // WIDTH
    queries = stack_heads(q_ref[...] * 0.125, True)
    m_ref[...] = jnp.full_like(m_ref, NEGATIVE)
    l_ref[...] = jnp.zeros_like(l_ref)
    acc_ref[...] = jnp.zeros_like(acc_ref)
    base = LOOK * 1024 + pl.program_id(0) * BQ

    def step(c, masked):
        start = pl.multiple_of(c * BK, BK)
        rows = kv_ref[pl.ds(start, BK), :]
        scores = nt(queries, rows)
        if masked:
            key = start + lax.broadcasted_iota(jnp.int32, (BQ, BK), 1)
            query = base + lax.broadcasted_iota(jnp.int32, (BQ, BK), 0)
            seen = (key >= lo_ref[...]) & (key <= query)
            scores = jnp.where(jnp.concatenate([seen] * heads, axis=0), scores, NEGATIVE)
        old = m_ref[...]
        new = jnp.maximum(old, jnp.max(scores, axis=1, keepdims=True))
        probs = jnp.exp(scores - new)
        fade = jnp.exp(old - new)
        m_ref[...] = new
        l_ref[...] = l_ref[...] * fade + jnp.sum(probs, axis=1, keepdims=True)
        acc_ref[...] = acc_ref[...] * fade + nn(probs.astype(jnp.bfloat16), rows)

    chunk_loops(bounds_ref, step)
    total = l_ref[...]
    result = acc_ref[...] / total
    out_ref[...] = jnp.concatenate(
        [result[h * BQ : (h + 1) * BQ, WIDTH:] for h in range(heads)], axis=1
    ).astype(jnp.bfloat16)
    lse = jnp.broadcast_to(m_ref[...] + jnp.log(total), acc_ref.shape)
    lse_ref[...] = jnp.transpose(lse)[:8, :]


def attention(bounds, lo, q, kv):
    rows, width = q.shape
    heads = width // WIDTH
    blocks = rows // BQ
    return pl.pallas_call(
        attention_kernel,
        grid=(blocks,),
        in_specs=[
            pl.BlockSpec(memory_space=pltpu.SMEM),
            pl.BlockSpec((BQ, 1), lambda b: (b, 0)),
            pl.BlockSpec((BQ, width), lambda b: (b, 0)),
            pl.BlockSpec(memory_space=pltpu.VMEM),
        ],
        out_specs=[
            pl.BlockSpec((BQ, width), lambda b: (b, 0)),
            pl.BlockSpec((None, 8, heads * BQ), lambda b: (b, 0, 0)),
        ],
        out_shape=[
            jax.ShapeDtypeStruct((rows, width), jnp.bfloat16),
            jax.ShapeDtypeStruct((blocks, 8, heads * BQ), jnp.float32),
        ],
        scratch_shapes=[
            pltpu.VMEM((heads * BQ, 1), jnp.float32),
            pltpu.VMEM((heads * BQ, 1), jnp.float32),
            pltpu.VMEM((heads * BQ, 2 * WIDTH), jnp.float32),
        ],
        compiler_params=pltpu.CompilerParams(vmem_limit_bytes=48 << 20),
        cost_estimate=pl.CostEstimate(
            flops=4 * rows * 4096 * width, bytes_accessed=4 << 20, transcendentals=rows * 4096 * 3
        ),
        name="attention",
    )(bounds, lo, q, kv)


def attention_back_kernel(
    bounds_ref, lo_ref, q_ref, kv_ref, out_ref, dout_ref, lse_ref, dq_ref, dkv_ref, acc_ref
):
    heads = q_ref.shape[1] // WIDTH
    queries = stack_heads(q_ref[...] * 0.125, True)
    douts = stack_heads(dout_ref[...], False)
    outs = stack_heads(out_ref[...], False)
    delta = jnp.sum(
        jnp.transpose(douts.astype(jnp.float32) * outs.astype(jnp.float32)), axis=0, keepdims=True
    )
    lse = lse_ref[:1, :]
    acc_ref[...] = jnp.zeros_like(acc_ref)
    base = LOOK * 1024 + pl.program_id(0) * BQ

    @pl.when(pl.program_id(0) == 0)
    def _():
        dkv_ref[...] = jnp.zeros_like(dkv_ref)

    def step(c, masked):
        start = pl.multiple_of(c * BK, BK)
        rows = kv_ref[pl.ds(start, BK), :]
        scores = nt(rows, queries)
        if masked:
            key = start + lax.broadcasted_iota(jnp.int32, (BK, BQ), 0)
            query = base + lax.broadcasted_iota(jnp.int32, (BK, BQ), 1)
            seen = (key >= lo_ref[...]) & (key <= query)
            scores = jnp.where(jnp.concatenate([seen] * heads, axis=1), scores, NEGATIVE)
        probs = jnp.exp(scores - lse)
        d_scores = (probs * (nt(rows, douts) - delta)).astype(jnp.bfloat16)
        dkv_ref[pl.ds(start, BK), :] += nn(d_scores, queries) + nn(
            probs.astype(jnp.bfloat16), douts
        )
        acc_ref[...] += tn(d_scores, rows)

    chunk_loops(bounds_ref, step)
    result = acc_ref[...] * 0.125
    dq_ref[...] = jnp.concatenate(
        [result[h * BQ : (h + 1) * BQ, :WIDTH] for h in range(heads)], axis=1
    ).astype(jnp.bfloat16)


def attention_back(bounds, lo_row, q, kv, out, dout, lse):
    rows, width = q.shape
    heads = width // WIDTH
    blocks = rows // BQ
    row_block = pl.BlockSpec((BQ, width), lambda b: (b, 0))
    return pl.pallas_call(
        attention_back_kernel,
        grid=(blocks,),
        in_specs=[
            pl.BlockSpec(memory_space=pltpu.SMEM),
            pl.BlockSpec((1, BQ), lambda b: (0, b)),
            row_block,
            pl.BlockSpec(memory_space=pltpu.VMEM),
            row_block,
            row_block,
            pl.BlockSpec((None, 8, heads * BQ), lambda b: (b, 0, 0)),
        ],
        out_specs=[
            row_block,
            pl.BlockSpec(kv.shape, lambda b: (0, 0)),
        ],
        out_shape=[
            jax.ShapeDtypeStruct((rows, width), jnp.bfloat16),
            jax.ShapeDtypeStruct(kv.shape, jnp.float32),
        ],
        scratch_shapes=[pltpu.VMEM((heads * BQ, 2 * WIDTH), jnp.float32)],
        compiler_params=pltpu.CompilerParams(vmem_limit_bytes=48 << 20),
        cost_estimate=pl.CostEstimate(
            flops=10 * rows * 4096 * width, bytes_accessed=8 << 20, transcendentals=rows * 4096 * 3
        ),
        name="attention_back",
    )(bounds, lo_row, q, kv, out, dout, lse)


def from_behind(x, by):
    peers = lax.axis_size("fsdp")
    pairs = [(i, i + by) for i in range(peers) if 0 <= i + by < peers]
    return lax.ppermute(x, "fsdp", pairs)


def gather_seq(x):
    return lax.all_gather(x, "seq", axis=0, tiled=True)


def scatter_seq(x):
    return lax.psum_scatter(x.astype(jnp.bfloat16), "seq", scatter_dimension=0, tiled=True)


def gather_fsdp(x, dim=0):
    return lax.all_gather(x, "fsdp", axis=dim, tiled=True)


def scatter_fsdp(x, dim=0):
    return lax.psum_scatter(x.astype(jnp.bfloat16), "fsdp", scatter_dimension=dim, tiled=True)


def head_rows_order(fsdp, seq):
    per = fsdp // seq
    return [(f * seq + s, ((f % per) * seq + s) * seq + f // per) for f in range(fsdp) for s in range(seq)]


def columns_by_owner(fsdp, seq, total):
    inner = total // (fsdp * seq)
    place = np.arange(total).reshape(fsdp, seq, inner).transpose(1, 0, 2).reshape(-1)
    one_hot = np.zeros((total, total), np.float32)
    one_hot[place, np.arange(total)] = 1
    return jnp.asarray(one_hot, jnp.bfloat16)


def scale_of(values):
    return lax.rsqrt(jnp.mean(values * values, axis=-1, keepdims=True) + EPS)


def rms_back(d_normed, unit, scale, gain):
    d_unit = d_normed * gain
    return scale * (d_unit - unit * jnp.mean(d_unit * unit, axis=-1, keepdims=True))


def on_device(
    tokens,
    gain_one,
    w_qkv,
    w_out,
    gain_two,
    w_router,
    w_gate,
    w_up,
    w_down,
    doc_starts,
    routes,
    cotangent,
):
    fsdp, seq = lax.axis_size("fsdp"), lax.axis_size("seq")
    group_index = lax.axis_index("fsdp")
    seq_index = lax.axis_index("seq")
    own, model = tokens.shape
    group_rows = own * seq
    experts, own_model, ff = w_gate.shape
    own_ff = ff // seq
    qkv_width = w_qkv.shape[1] // seq
    head_rows = w_out.shape[0] * fsdp
    order = columns_by_owner(fsdp, seq, ff)

    gate_up = nn(
        jnp.concatenate([w_gate, w_up], axis=0).reshape(2 * experts * own_model, ff), order
    ).astype(jnp.bfloat16)
    gate_up = gate_up.reshape(2 * experts, own_model, seq, own_ff)
    to_heads = jnp.concatenate(
        [
            w_qkv.reshape(own_model, seq, qkv_width),
            jnp.transpose(gate_up, (1, 2, 0, 3)).reshape(own_model, seq, 2 * experts * own_ff),
        ],
        axis=2,
    )
    by_heads = lax.all_to_all(to_heads, "seq", split_axis=1, concat_axis=0, tiled=True)
    by_heads = by_heads.reshape(own_model * seq, -1)
    qkv_weight = gather_fsdp(by_heads[:, :qkv_width])
    small = jnp.concatenate([gain_one[:, None], gain_two[:, None], w_router], axis=1)
    small = lax.all_gather(small, BOTH, axis=0, tiled=True)
    gain_first = small[:, 0].astype(jnp.float32)
    gain_second = small[:, 1].astype(jnp.float32)
    router_weight = small[:, 2:]
    out_weight = gather_fsdp(lax.ppermute(w_out, BOTH, head_rows_order(fsdp, seq)))
    expert_weight = gather_fsdp(by_heads[:, qkv_width:])
    gate_weight, up_weight = jnp.split(expert_weight, 2, axis=1)
    down_weight = gather_fsdp(w_down, 1).reshape(experts * own_ff, model)
    grad_all = gather_seq(cotangent)

    tokens_all = gather_seq(tokens).astype(jnp.float32)
    normed_one = (tokens_all * scale_of(tokens_all) * gain_first).astype(jnp.bfloat16)
    qkv = nn(normed_one, qkv_weight).astype(jnp.bfloat16)
    queries, keyval = qkv[:, : 3 * WIDTH], qkv[:, 3 * WIDTH :]
    window = jnp.concatenate([from_behind(keyval, LOOK - i) for i in range(LOOK)] + [keyval], axis=0)
    positions = group_index * group_rows + jnp.arange(group_rows, dtype=jnp.int32)
    begins = jnp.max(
        jnp.where(doc_starts[None, :] <= positions[:, None], doc_starts[None, :], 0), axis=1
    )
    lo = begins - (group_index - LOOK) * group_rows
    blocks = group_rows // BQ
    lo_blocks = lo.reshape(blocks, BQ)
    diag = (LOOK * group_rows + jnp.arange(blocks, dtype=jnp.int32) * BQ) // BK
    end = (LOOK * group_rows + (jnp.arange(blocks, dtype=jnp.int32) + 1) * BQ + BK - 1) // BK
    first = jnp.minimum(lo_blocks[:, 0] // BK, diag)
    full = jnp.minimum((lo_blocks[:, -1] + BK - 1) // BK, diag)
    bounds = jnp.stack([first, full, diag, end], axis=1)
    attended, lse = attention(bounds, lo[:, None], queries, window)
    branch = scatter_seq(nn(attended, out_weight))
    inputs = tokens.astype(jnp.float32)
    residual = inputs + branch.astype(jnp.float32)
    scale_second = scale_of(residual)
    unit_second = residual * scale_second
    normed_two = (unit_second * gain_second).astype(jnp.bfloat16)

    normed_all = gather_seq(normed_two)
    routes_all = gather_seq(routes)
    expert_ids = jnp.arange(experts, dtype=jnp.int32)
    chosen = jnp.sum((routes_all[:, :, None] == expert_ids).astype(jnp.float32), axis=1)
    probs_all = jax.nn.softmax(nn(normed_all, router_weight), axis=-1)
    share = jnp.repeat(probs_all * chosen, own_ff, axis=1)
    gate_pre = nn(normed_all, gate_weight)
    up_pre = nn(normed_all, up_weight)
    sigmoid = jax.nn.sigmoid(gate_pre)
    silu = gate_pre * sigmoid
    hidden = (silu * up_pre).astype(jnp.bfloat16)
    shared = (hidden.astype(jnp.float32) * share).astype(jnp.bfloat16)
    moe_out = scatter_seq(nn(shared, down_weight))
    output = (residual + moe_out.astype(jnp.float32)).astype(jnp.bfloat16)
    d_plain = nt(grad_all, down_weight)
    d_share = jnp.sum(
        (d_plain * hidden.astype(jnp.float32)).reshape(group_rows, experts, own_ff), axis=2
    )
    d_hidden = d_plain * share
    d_gate = (d_hidden * up_pre * sigmoid * (1.0 + gate_pre * (1.0 - sigmoid))).astype(jnp.bfloat16)
    d_up = (d_hidden * silu).astype(jnp.bfloat16)
    d_normed_two = nt(d_gate, gate_weight) + nt(d_up, up_weight)
    d_router = lax.psum_scatter(d_share, "seq", scatter_dimension=0, tiled=True)
    d_normed_two = scatter_seq(d_normed_two).astype(jnp.float32)
    grad_down = tn(shared, grad_all)
    grad_gate_up = jnp.concatenate([tn(normed_all, d_gate), tn(normed_all, d_up)], axis=1)

    chosen_own = jnp.sum((routes[:, :, None] == expert_ids).astype(jnp.float32), axis=1)
    probs_own = jax.nn.softmax(nn(normed_two, router_weight), axis=-1)
    d_router = d_router * chosen_own
    d_logits = (
        probs_own * (d_router - jnp.sum(probs_own * d_router, axis=-1, keepdims=True))
    ).astype(jnp.bfloat16)
    d_normed_two = d_normed_two + nt(d_logits, router_weight)
    grad_out = cotangent.astype(jnp.float32)
    d_resid = grad_out + rms_back(d_normed_two, unit_second, scale_second, gain_second)
    d_branch_all = gather_seq(d_resid.astype(jnp.bfloat16))

    grad_w_out = tn(attended, d_branch_all)
    d_attended = nt(d_branch_all, out_weight).astype(jnp.bfloat16)
    d_queries, d_window = attention_back(
        bounds, lo[None, :], queries, window, attended, d_attended, lse
    )
    d_keyval = d_window[LOOK * group_rows :]
    for distance in range(1, LOOK + 1):
        piece = d_window[(LOOK - distance) * group_rows : (LOOK - distance + 1) * group_rows]
        d_keyval = d_keyval + from_behind(piece.astype(jnp.bfloat16), -distance).astype(jnp.float32)
    d_qkv = jnp.concatenate([d_queries, d_keyval.astype(jnp.bfloat16)], axis=1)
    grad_w_qkv = tn(normed_one, d_qkv)
    d_normed_one = scatter_seq(nt(d_qkv, qkv_weight)).astype(jnp.float32)
    scale_first = scale_of(inputs)
    grad_input = d_resid + rms_back(d_normed_one, inputs * scale_first, scale_first, gain_first)

    shard_down = scatter_fsdp(
        grad_down.reshape(experts, own_ff, model), 1
    ).astype(jnp.float32)
    shard_out = lax.ppermute(
        scatter_fsdp(grad_w_out), BOTH, [(b, a) for a, b in head_rows_order(fsdp, seq)]
    ).astype(jnp.float32)
    grad_cols = jnp.concatenate([grad_w_qkv, grad_gate_up], axis=1)
    grad_cols = scatter_fsdp(grad_cols).reshape(seq, own_model, -1)
    grad_cols = lax.all_to_all(grad_cols, "seq", split_axis=0, concat_axis=0, tiled=True)
    shard_qkv = jnp.transpose(grad_cols[:, :, :qkv_width], (1, 0, 2)).reshape(own_model, -1)
    shard_qkv = shard_qkv.astype(jnp.float32)
    back = grad_cols[:, :, qkv_width:].reshape(seq, own_model, 2 * experts, own_ff)
    back = jnp.transpose(back, (2, 1, 0, 3)).reshape(2 * experts * own_model, ff)
    back = nt(back, order).reshape(2 * experts, own_model, ff)
    shard_gate, shard_up = back[:experts], back[experts:]
    grad_router = tn(normed_two, d_logits)
    shard_router = lax.psum_scatter(grad_router, BOTH, scatter_dimension=0, tiled=True)

    shard_gain_one = jnp.sum(w_qkv.astype(jnp.float32) * shard_qkv, axis=1)
    shard_gain_one = shard_gain_one / gain_one.astype(jnp.float32)
    shard_gain_two = jnp.sum(w_router.astype(jnp.float32) * shard_router, axis=1)
    shard_gain_two += jnp.sum(w_gate.astype(jnp.float32) * shard_gate, axis=(0, 2))
    shard_gain_two += jnp.sum(w_up.astype(jnp.float32) * shard_up, axis=(0, 2))
    shard_gain_two = shard_gain_two / gain_two.astype(jnp.float32)
    return (
        output,
        grad_input,
        shard_gain_one,
        shard_qkv,
        shard_out,
        shard_gain_two,
        shard_router,
        shard_gate,
        shard_up,
        shard_down,
    )


def solution(mesh):
    rows, vector = P(BOTH, None), P(BOTH)
    middle = P(None, BOTH, None)
    in_specs = (
        rows, vector, rows, rows, vector, rows, middle, middle, middle, P(), rows, rows,
    )
    out_specs = (rows, rows, vector, rows, rows, vector, rows, middle, middle, middle)
    return jax.shard_map(
        on_device, mesh=mesh, in_specs=in_specs, out_specs=out_specs, check_vma=False
    )
```

time: 2080 us -> 1100 us (0.53)
  waiting for transfers between devices: 705 us -> 352 us
  starting transfers between devices: 309 us -> 58.2 us
  matrix products: 302 us -> 60.9 us
  local copies, waits for them, and re-layouts: 185 us -> 31.1 us
  other arithmetic: 107 us -> 24.3 us
  blocking collectives: 441 us -> 518 us
  Pallas kernels: 0 us -> 28.6 us
    all_gather x0 -> x4, blocking collectives: none -> 376 us  [the longest x1 288 us: on_device(): small = lax.all_gather(small, BOTH, axis=0, tiled=True)]
    all_gather x5 -> x6, waiting for transfers between devices: 520 us -> 147 us  [the longest x4 104 us: gather_seq(): return lax.all_gather(x, 'seq', axis=0, tiled=True)]
    unnamed x2, blocking collectives: 441 us -> 142 us
    dot_general x37 -> x21, matrix products: 302 us -> 60.9 us  [the longest x8 23.4 us: nn(): return jnp.dot(a, b, preferred_element_type=jnp.float32)]
    unnamed x65 -> x6, starting transfers between devices: 236 us -> 17.2 us
    unnamed x209 -> x111, local copies, waits for them, and re-layouts: 136 us -> 22.9 us
    another operation x7 -> x2, other arithmetic: 55.4 us -> 0.21 us
    pallas_call x0 -> x2, Pallas kernels: none -> 28.6 us  [the longest x1 17.2 us: attention(): pl.pallas_call(attention_kernel, grid=(blocks,), in_specs=[pl.BlockSpec(m...]
  transfers between devices with their start and end apart: 87 -> 29, of which waited for: 15 -> 13; matrix products, arithmetic and copies ran while one was open for 42% -> 12% of each run, Pallas kernels for 0% -> 1%
where the time goes in v1:
time: 1100 us; the launch traced here: 1090 us
  blocking collectives  518 us (47%)
  waiting for transfers between devices  352 us (32%)
  matrix products  60.9 us (6%)
  starting transfers between devices  58.2 us (5%)
  local copies, waits for them, and re-layouts  31.1 us (3%)
  Pallas kernels  28.6 us (3%)
  other arithmetic  24.3 us (2%)
  between operations  17.2 us (2%)
    all_gather x1, blocking collectives, on_device(): small = lax.all_gather(small, BOTH, axis=0, tiled=True)  288 us
    reduce_scatter x4, waiting for transfers between devices, scatter_seq(): lax.psum_scatter(x.astype(jnp.bfloat16), 'seq', scatter_dimension=0, tile...  156 us
    unnamed x2, blocking collectives  142 us
    all_gather x4, waiting for transfers between devices, gather_seq(): return lax.all_gather(x, 'seq', axis=0, tiled=True)  104 us
    all_gather x2, blocking collectives, gather_fsdp(): return lax.all_gather(x, 'fsdp', axis=dim, tiled=True)  74.7 us
    all_gather x2, waiting for transfers between devices, gather_fsdp(): return lax.all_gather(x, 'fsdp', axis=dim, tiled=True)  42.8 us
    unnamed x19, waiting for transfers between devices  23.7 us
    dot_general x8, matrix products, nn(): return jnp.dot(a, b, preferred_element_type=jnp.float32)  23.4 us
  transfers between devices with their start and end apart: 29, of which 13 were waited for; matrix products, arithmetic and copies ran while one was open for 12% of the time, Pallas kernels for 1%

profile of v1, /device:TPU:3, one launch (start us, length us, event | category | flops | bytes accessed | tf_op | source)
XLA Modules:
  0.0 1090.5 jit_solution(14255695558050122346)
XLA Ops:
  8.7 7.0 collective-permute-start.4
  26.7 288.3 %all-gather = bf16[128,12,6]{1,2,0:T(8,128)(2,1)S(1)} all-gather(bf16[1,12,6]{1,2,0:T(8,128)(2,1)S(1)} %maximum_bitcast_fusion), channel_id=1, replica_groups=mesh['fsdp'=16,'seq'=8] {'fsdp','seq'}, dimensions={0}, use_global_device_ids=true | all-gather | bytes 18576 | tf_op jit(solution)/shard_map/all_gather | solution.py:279
  316.5 43.9 %all_gather.32 = bf16[1536,320]{1,0:T(8,128)(2,1)} all-gather(bf16[96,320]{1,0:T(8,128)(2,1)S(1)} %slice.87), channel_id=1, replica_groups=mesh['fsdp'=16,'seq'=8] {'fsdp'}, dimensions={0}, use_global_device_ids=true | all-gather | bytes 1044480 | tf_op jit(solution)/shard_map/all_gather | solution.py:210
  373.0 30.8 %all-gather.1 = bf16[16,12,1536]{2,1,0:T(8,128)(2,1)S(1)} all-gather(bf16[1,12,1536]{2,1,0:T(8,128)(2,1)S(1)} %bitcast.95), channel_id=1, replica_groups=mesh['fsdp'=16,'seq'=8] {'fsdp'}, dimensions={0}, use_global_device_ids=true | all-gather | bytes 626688 | tf_op jit(solution)/shard_map/all_gather | solution.py:210
  411.2 17.2 %attention.1 = (bf16[1024,192]{1,0:T(8,128)(2,1)S(1)}, f32[4,8,768]{2,1,0:T(8,128)S(1)}) custom-call(s32[4,4]{1,0:T(4,128)S(1)} %pad_add_fusion.bounds_ref, s32[1024,1]{1,0:T(8,128)S(1)} %copy.101.lo_ref, bf16[1024,192]{1,0:T(8,128)(2,1)S(1)} %slice.88.q_ref, bf16[5120,128]{1,0:T(8,128)(2,1)S(1)} %constant_dynamic-update-slice_fusion.kv_ref), custom_call_target="tpu_custom_call" | custom-call | flops 3221225472 | bytes 4194304 | tf_op jit(solution)/shard_map/attention/pallas_call | solution.py:90
  432.0 98.6 %reduce-scatter.17.cloned.1.call-done = bf16[128,1536]{1,0:T(8,128)(2,1)} async-done(((bf16[1024,1536]{1,0:T(8,128)(2,1)}), bf16[128,1536]{1,0:T(8,128)(2,1)}) %reduce-scatter.17.cloned.1.call-update) | async-done | bytes 393232 | tf_op jit(solution)/shard_map/reduce_scatter | solution.py:206
  535.2 12.8 %all_gather.36 = s32[1024,2]{0,1:T(2,128)S(1)} all-gather(s32[128,2]{0,1:T(2,128)S(1)} %copy-done.33), channel_id=1, replica_groups=mesh['fsdp'=16,'seq'=8] {'seq'}, dimensions={0}, use_global_device_ids=true | all-gather | bytes 9216 | tf_op jit(solution)/shard_map/all_gather | solution.py:202
  548.1 29.4 %all-gather.11.cloned.1.call-done = bf16[1024,1536]{1,0:T(8,128)(2,1)} async-done(((bf16[128,1536]{1,0:T(8,128)(2,1)}), bf16[1024,1536]{1,0:T(8,128)(2,1)}) %all-gather.11.cloned.1.call-update) | async-done | bytes 3145744 | tf_op jit(solution)/shard_map/all_gather | solution.py:202
  586.4 42.8 %all-gather.15.cloned.1.call-done = bf16[4,128,1536]{2,1,0:T(8,128)(2,1)} async-done(((bf16[4,8,1536]{2,1,0:T(8,128)(2,1)}), bf16[4,128,1536]{2,1,0:T(8,128)(2,1)}) %all-gather.15.cloned.1.call-update) | async-done | bytes 1572880 | tf_op jit(solution)/shard_map/all_gather | solution.py:210
  629.1 41.5 %all-gather.17.cloned.1.call-done = bf16[1024,1536]{1,0:T(8,128)(2,1)} async-done(((bf16[128,1536]{1,0:T(8,128)(2,1)}), bf16[1024,1536]{1,0:T(8,128)(2,1)}) %all-gather.17.cloned.1.call-update) | async-done | bytes 3145744 | tf_op jit(solution)/shard_map/all_gather | solution.py:202
  670.6 7.3 bitcast_reduce_fusion
  693.6 21.0 %reduce-scatter.25.cloned.1.call-done = f32[128,4]{1,0:T(8,128)} async-done(((f32[1024,4]{1,0:T(8,128)}), f32[128,4]{1,0:T(8,128)}) %reduce-scatter.25.cloned.1.call-update) | async-done | bytes 2064
  715.6 47.2 %reduce-scatter.21.cloned.1.call-done = bf16[128,1536]{1,0:T(8,128)(2,1)} async-done(((bf16[1024,1536]{1,0:T(8,128)(2,1)}), bf16[128,1536]{1,0:T(8,128)(2,1)}) %reduce-scatter.21.cloned.1.call-update) | async-done | bytes 393232 | tf_op jit(solution)/shard_map/reduce_scatter | solution.py:206
  778.8 33.2 %all-gather.19.cloned.1.call-done = bf16[1024,1536]{1,0:T(8,128)(2,1)} async-done(((bf16[128,1536]{1,0:T(8,128)(2,1)}), bf16[1024,1536]{1,0:T(8,128)(2,1)}) %all-gather.19.cloned.1.call-update) | async-done | bytes 3145744 | tf_op jit(solution)/shard_map/all_gather | solution.py:202
  815.4 11.4 %attention_back.1 = (bf16[1024,192]{1,0:T(8,128)(2,1)S(1)}, f32[5120,128]{1,0:T(8,128)S(1)}) custom-call(s32[4,4]{1,0:T(4,128)S(1)} %pad_add_fusion.bounds_ref, s32[1,1024]{1,0:T(1,128)S(1)} %bitcast.85, bf16[1024,192]{1,0:T(8,128)(2,1)S(1)} %slice.88.q_ref, bf16[5120,128]{1,0:T(8,128)(2,1)S(1)} %constant_dynamic-update-slice_fusion.kv_ref, ...), custom_call_target="tpu_custom_call" | custom-call | flops 8053063680 | bytes 8388608 | tf_op jit(solution)/shard_map/attention_back/pallas_call | solution.py:166
  839.4 16.6 %collective-permute-done.8 = bf16[1024,128]{1,0:T(8,128)(2,1)S(1)} collective-permute-done((bf16[1024,128]{1,0:T(8,128)(2,1)S(1)}, bf16[1024,128]{1,0:T(8,128)(2,1)S(1)}, u32[]{:S(2)}, u32[]{:S(2)}) %collective-permute-start.8) | collective-permute-done | bytes 262176 | tf_op jit(solution)/shard_map/ppermute | solution.py:198
  860.0 6.4 copy.116
  878.5 99.3 %all-reduce.1 = f32[1536,4]{0,1:T(4,128)S(1)} all-reduce(f32[1536,4]{0,1:T(4,128)S(1)} %fusion.55), channel_id=9, replica_groups=mesh['fsdp'=16,'seq'=8] {'fsdp','seq'}, use_global_device_ids=true, to_apply=%region_22.23.clone | all-reduce | flops 6144 | bytes 49152
  982.1 42.9 %fusion = bf16[16,1536]{1,0:T(8,128)(2,1)S(1)} fusion(bf16[192,1536]{1,0:T(8,128)(2,1)S(1)} %convolution_convert_fusion.7), kind=kCustom, calls=%all-reduce-scatter | all-reduce-scatter fusion | flops 393217 | bytes 639488
  1027.7 6.5 collective-permute-start.10
  1034.2 7.9 collective-permute-start.13
  1046.2 5.9 collective-permute-done.9
  1054.5 8.1 all-to-all-start.1
  1063.9 9.8 reduce-scatter.19.cloned.1.call-done
  (253 shorter events, 137.5 us)
Async XLA Ops:
  8.0 352.4 %all-gather.9.cloned.1.call-start = ((), (), s32[]{:S(2)}) async-start(), calls=%async_computation.9 | async-start | bytes 3538944 | tf_op jit(solution)/shard_map/all_gather | solution.py:202
  8.7 364.3 %collective-permute-start.4 = (bf16[12,1536]{1,0:T(8,128)(2,1)}, bf16[12,1536]{1,0:T(8,128)(2,1)S(1)}, u32[]{:S(2)}, u32[]{:S(2)}) collective-permute-start(bf16[12,1536]{1,0:T(8,128)(2,1)} %param.16), channel_id=1, source_target_pairs={{0,0},{1,8},{2,16},{3,24},{4,32},{5,40},{6,48},{7,56},{8,64},{9,72... | collective-permute-start | bytes 110600 | tf_op jit(solution)/shard_map/ppermute | solution.py:283
  21.2 295.1 %all-to-all-start = ((bf16[12,8,1344]{2,0,1:T(8,128)(2,1)}), bf16[12,8,1344]{2,0,1:T(8,128)(2,1)S(1)}, u32[]{:S(2)}, u32[]{:S(2)}) async-start(bf16[12,8,1344]{2,0,1:T(8,128)(2,1)} %copy.99), calls=%async_computation | async-start | bytes 720896 | tf_op jit(solution)/shard_map/all_to_all | solution.py:275
  26.5 504.1 %reduce-scatter.17.cloned.1.call-start = ((), (), s32[]{:S(2)}) async-start(), calls=%async_computation.10 | async-start | bytes 3538944 | tf_op jit(solution)/shard_map/reduce_scatter | solution.py:206
  366.6 41.5 %collective-permute-start.2 = (bf16[1024,128]{1,0:T(8,128)(2,1)S(1)}, bf16[1024,128]{1,0:T(8,128)(2,1)S(1)}, u32[]{:S(2)}, u32[]{:S(2)}) collective-permute-start(bf16[1024,128]{1,0:T(8,128)(2,1)S(1)} %slice.89), channel_id=1, source_target_pairs={{0,16},{8,24},{16,32},{24,40},{32,48},{40,56},{48,64},{56,72},{64,... | collective-permute-start | bytes 786440 | tf_op jit(solution)/shard_map/ppermute | solution.py:198
  369.4 38.6 %collective-permute-start.1 = (bf16[1024,128]{1,0:T(8,128)(2,1)S(1)}, bf16[1024,128]{1,0:T(8,128)(2,1)S(1)}, u32[]{:S(2)}, u32[]{:S(2)}) collective-permute-start(bf16[1024,128]{1,0:T(8,128)(2,1)S(1)} %slice.89), channel_id=1, source_target_pairs={{0,24},{8,32},{16,40},{24,48},{32,56},{40,64},{48,72},{56,80},{64,... | collective-permute-start | bytes 786440 | tf_op jit(solution)/shard_map/ppermute | solution.py:198
  370.7 36.3 %collective-permute-start = (bf16[1024,128]{1,0:T(8,128)(2,1)S(1)}, bf16[1024,128]{1,0:T(8,128)(2,1)}, u32[]{:S(2)}, u32[]{:S(2)}) collective-permute-start(bf16[1024,128]{1,0:T(8,128)(2,1)S(1)} %slice.89), channel_id=1, source_target_pairs={{0,32},{8,40},{16,48},{24,56},{32,64},{40,72},{48,80},{56,88},{64,... | collective-permute-start | bytes 786440 | tf_op jit(solution)/shard_map/ppermute | solution.py:198
  431.1 117.0 %all-gather.13.cloned.1.call-start = ((), (), s32[]{:S(2)}) async-start(), calls=%async_computation.12 | async-start | bytes 3342336 | tf_op jit(solution)/shard_map/all_gather | solution.py:210
  432.0 145.5 %all-gather.11.cloned.1.call-start = ((), (), s32[]{:S(2)}) async-start(), calls=%async_computation.11 | async-start | bytes 3538944 | tf_op jit(solution)/shard_map/all_gather | solution.py:202
  533.8 95.3 %all-gather.15.cloned.1.call-start = ((), (), s32[]{:S(2)}) async-start(), calls=%async_computation.13 | async-start | bytes 1671168 | tf_op jit(solution)/shard_map/all_gather | solution.py:210
  534.4 136.2 %all-gather.17.cloned.1.call-start = ((), (), s32[]{:S(2)}) async-start(), calls=%async_computation.15 | async-start | bytes 3538944 | tf_op jit(solution)/shard_map/all_gather | solution.py:202
  535.1 179.5 %reduce-scatter.25.cloned.1.call-start = ((), (), s32[]{:S(2)}) async-start(), calls=%async_computation.19 | async-start | bytes 589824
  679.0 83.8 %reduce-scatter.21.cloned.1.call-start = ((), (), s32[]{:S(2)}) async-start(), calls=%async_computation.16 | async-start | bytes 3538944 | tf_op jit(solution)/shard_map/reduce_scatter | solution.py:206
  692.4 119.6 %all-gather.19.cloned.1.call-start = ((), (), s32[]{:S(2)}) async-start(), calls=%async_computation.17 | async-start | bytes 3538944 | tf_op jit(solution)/shard_map/all_gather | solution.py:202
  767.0 211.4 %reduce-scatter.29.cloned.1.call-start = ((), (), s32[]{:S(2)}) async-start(), calls=%async_computation.21 | async-start | bytes 1671168
  773.7 278.9 %reduce-scatter.27.cloned.1.call-start = ((), (), s32[]{:S(2)}) async-start(), calls=%async_computation.20 | async-start | bytes 4595712 | tf_op jit(solution)/shard_map/reduce_scatter | solution.py:214
  831.7 24.3 %collective-permute-start.8 = (bf16[1024,128]{1,0:T(8,128)(2,1)S(1)}, bf16[1024,128]{1,0:T(8,128)(2,1)S(1)}, u32[]{:S(2)}, u32[]{:S(2)}) collective-permute-start(bf16[1024,128]{1,0:T(8,128)(2,1)S(1)} %get-tuple-element.91), channel_id=1, source_target_pairs={{32,0},{40,8},{48,16},{56,24},{64,32},{72,40},{80,48},{88,56},{96,... | collective-permute-start | bytes 786440 | tf_op jit(solution)/shard_map/ppermute | solution.py:198
  833.0 23.0 %collective-permute-start.7 = (bf16[1024,128]{1,0:T(8,128)(2,1)S(1)}, bf16[1024,128]{1,0:T(8,128)(2,1)S(1)}, u32[]{:S(2)}, u32[]{:S(2)}) collective-permute-start(bf16[1024,128]{1,0:T(8,128)(2,1)S(1)} %get-tuple-element.92), channel_id=1, source_target_pairs={{24,0},{32,8},{40,16},{48,24},{56,32},{64,40},{72,48},{80,56},{88,... | collective-permute-start | bytes 786440 | tf_op jit(solution)/shard_map/ppermute | solution.py:198
  834.3 21.7 %collective-permute-start.6 = (bf16[1024,128]{1,0:T(8,128)(2,1)S(1)}, bf16[1024,128]{1,0:T(8,128)(2,1)S(1)}, u32[]{:S(2)}, u32[]{:S(2)}) collective-permute-start(bf16[1024,128]{1,0:T(8,128)(2,1)S(1)} %get-tuple-element.93), channel_id=1, source_target_pairs={{16,0},{24,8},{32,16},{40,24},{48,32},{56,40},{64,48},{72,56},{80,... | collective-permute-start | bytes 786440 | tf_op jit(solution)/shard_map/ppermute | solution.py:198
  866.4 196.2 %reduce-scatter.23.cloned.1.call-start = ((), (), s32[]{:S(2)}) async-start(), calls=%async_computation.18 | async-start | bytes 3538944 | tf_op jit(solution)/shard_map/reduce_scatter | solution.py:206
  871.2 202.5 %reduce-scatter.19.cloned.1.call-start = ((), (), s32[]{:S(2)}) async-start(), calls=%async_computation.14 | async-start | bytes 3538944 | tf_op jit(solution)/shard_map/reduce_scatter | solution.py:206
  1025.0 18.5 %collective-permute-start.12 = (bf16[16,1536]{1,0:T(8,128)(2,1)S(1)}, bf16[16,1536]{1,0:T(8,128)(2,1)S(1)}, u32[]{:S(2)}, u32[]{:S(2)}) collective-permute-start(bf16[16,1536]{1,0:T(8,128)(2,1)S(1)} %fusion), channel_id=1, source_target_pairs={{0,24},{8,32},{16,40},{24,48},{32,56},{40,64},{48,72},{56,80},{64,... | collective-permute-start | bytes 147464
  1026.3 17.2 %collective-permute-start.11 = (bf16[16,1536]{1,0:T(8,128)(2,1)S(1)}, bf16[16,1536]{1,0:T(8,128)(2,1)S(1)}, u32[]{:S(2)}, u32[]{:S(2)}) collective-permute-start(bf16[16,1536]{1,0:T(8,128)(2,1)S(1)} %fusion), channel_id=1, source_target_pairs={{0,16},{8,24},{16,32},{24,40},{32,48},{40,56},{48,64},{56,72},{64,... | collective-permute-start | bytes 147464
  1054.5 22.1 %all-to-all-start.1 = ((bf16[8,12,1344]{2,1,0:T(8,128)(2,1)}), bf16[8,12,1344]{2,1,0:T(8,128)(2,1)}, u32[]{:S(2)}, u32[]{:S(2)}) async-start(bf16[8,12,1344]{2,1,0:T(8,128)(2,1)} %reshape.265), calls=%async_computation.5 | async-start | bytes 720896 | tf_op jit(solution)/shard_map/all_to_all | solution.py:375
  (51 other events, 1083.2 us)
Sparse Core Ops, SparseCore 0:
  10.5 47.3 all-gather.8
  431.2 99.3 reduce-scatter.16
  679.1 35.4 reduce-scatter.24
  716.9 45.8 reduce-scatter.20
  767.1 44.8 all-gather.18
Sparse Core Ops, SparseCore 1:
  434.6 100.1 all-gather.12
  536.9 40.6 all-gather.10
  579.9 49.2 all-gather.14
  630.8 39.7 all-gather.16
  773.8 70.7 reduce-scatter.28
  866.5 110.5 reduce-scatter.26
  979.3 45.5 reduce-scatter.22
  1027.1 46.5 reduce-scatter.18

commit v2 on v1

v2 whole, which is shorter than its diff:
```python
import functools

import jax
import jax.numpy as jnp
import numpy as np
from jax import lax
from jax.experimental import pallas as pl
from jax.experimental.pallas import tpu as pltpu
from jax.sharding import PartitionSpec as P

WIDTH = 64
LOOK = 4
EXPERTS = 4
EPS = 1e-06
NEGATIVE = -1e30
BQ = 256
BK = 512
BOTH = ("fsdp", "seq")


def nt(a, b):
    return lax.dot_general(a, b, (((1,), (1,)), ((), ())), preferred_element_type=jnp.float32)


def tn(a, b):
    return lax.dot_general(a, b, (((0,), (0,)), ((), ())), preferred_element_type=jnp.float32)


def nn(a, b):
    return jnp.dot(a, b, preferred_element_type=jnp.float32)


def stack_heads(rows, low):
    heads = rows.shape[1] // WIDTH
    zero = jnp.zeros((rows.shape[0], WIDTH), rows.dtype)
    parts = []
    for h in range(heads):
        part = rows[:, h * WIDTH : (h + 1) * WIDTH]
        parts.append(jnp.concatenate([part, zero] if low else [zero, part], axis=1))
    return jnp.concatenate(parts, axis=0)


def chunk_loops(bounds_ref, step):
    b = pl.program_id(0)
    first, full, diag, end = (bounds_ref[b, i] for i in range(4))
    pl.loop(first, full)(lambda c: step(c, True))
    pl.loop(full, diag)(lambda c: step(c, False))
    pl.loop(diag, end)(lambda c: step(c, True))


def attention_kernel(bounds_ref, lo_ref, q_ref, kv_ref, out_ref, lse_ref, m_ref, l_ref, acc_ref):
    heads = q_ref.shape[1] // WIDTH
    queries = stack_heads(q_ref[...] * 0.125, True)
    m_ref[...] = jnp.full_like(m_ref, NEGATIVE)
    l_ref[...] = jnp.zeros_like(l_ref)
    acc_ref[...] = jnp.zeros_like(acc_ref)
    base = LOOK * 1024 + pl.program_id(0) * BQ

    def step(c, masked):
        start = pl.multiple_of(c * BK, BK)
        rows = kv_ref[pl.ds(start, BK), :]
        scores = nt(rows, queries)
        if masked:
            key = start + lax.broadcasted_iota(jnp.int32, (BK, BQ), 0)
            query = base + lax.broadcasted_iota(jnp.int32, (BK, BQ), 1)
            seen = (key >= lo_ref[...]) & (key <= query)
            scores = jnp.where(jnp.concatenate([seen] * heads, axis=1), scores, NEGATIVE)
        old = m_ref[...]
        new = jnp.maximum(old, jnp.max(scores, axis=0, keepdims=True))
        probs = jnp.exp(scores - new)
        fade = jnp.exp(old - new)
        m_ref[...] = new
        l_ref[...] = l_ref[...] * fade + jnp.sum(probs, axis=0, keepdims=True)
        acc_ref[...] = acc_ref[...] * fade + tn(rows, probs.astype(jnp.bfloat16))

    chunk_loops(bounds_ref, step)
    total = l_ref[...]
    result = jnp.transpose(acc_ref[...] / total)
    out_ref[...] = jnp.concatenate(
        [result[h * BQ : (h + 1) * BQ, WIDTH:] for h in range(heads)], axis=1
    ).astype(jnp.bfloat16)
    lse_ref[...] = jnp.broadcast_to(m_ref[...] + jnp.log(total), lse_ref.shape)


def attention(bounds, lo, q, kv):
    rows, width = q.shape
    heads = width // WIDTH
    blocks = rows // BQ
    return pl.pallas_call(
        attention_kernel,
        grid=(blocks,),
        in_specs=[
            pl.BlockSpec(memory_space=pltpu.SMEM),
            pl.BlockSpec((1, BQ), lambda b: (0, b)),
            pl.BlockSpec((BQ, width), lambda b: (b, 0)),
            pl.BlockSpec(memory_space=pltpu.VMEM),
        ],
        out_specs=[
            pl.BlockSpec((BQ, width), lambda b: (b, 0)),
            pl.BlockSpec((None, 8, heads * BQ), lambda b: (b, 0, 0)),
        ],
        out_shape=[
            jax.ShapeDtypeStruct((rows, width), jnp.bfloat16),
            jax.ShapeDtypeStruct((blocks, 8, heads * BQ), jnp.float32),
        ],
        scratch_shapes=[
            pltpu.VMEM((1, heads * BQ), jnp.float32),
            pltpu.VMEM((1, heads * BQ), jnp.float32),
            pltpu.VMEM((2 * WIDTH, heads * BQ), jnp.float32),
        ],
        compiler_params=pltpu.CompilerParams(vmem_limit_bytes=48 << 20),
        cost_estimate=pl.CostEstimate(
            flops=4 * rows * 4096 * width, bytes_accessed=4 << 20, transcendentals=rows * 4096 * 3
        ),
        name="attention",
    )(bounds, lo, q, kv)


def attention_back_kernel(
    bounds_ref, lo_ref, q_ref, kv_ref, out_ref, dout_ref, lse_ref, dq_ref, dkv_ref, acc_ref
):
    heads = q_ref.shape[1] // WIDTH
    queries = stack_heads(q_ref[...] * 0.125, True)
    douts = stack_heads(dout_ref[...], False)
    outs = stack_heads(out_ref[...], False)
    delta = jnp.sum(
        jnp.transpose(douts.astype(jnp.float32) * outs.astype(jnp.float32)), axis=0, keepdims=True
    )
    lse = lse_ref[:1, :]
    acc_ref[...] = jnp.zeros_like(acc_ref)
    base = LOOK * 1024 + pl.program_id(0) * BQ

    @pl.when(pl.program_id(0) == 0)
    def _():
        dkv_ref[...] = jnp.zeros_like(dkv_ref)

    def step(c, masked):
        start = pl.multiple_of(c * BK, BK)
        rows = kv_ref[pl.ds(start, BK), :]
        scores = nt(rows, queries)
        if masked:
            key = start + lax.broadcasted_iota(jnp.int32, (BK, BQ), 0)
            query = base + lax.broadcasted_iota(jnp.int32, (BK, BQ), 1)
            seen = (key >= lo_ref[...]) & (key <= query)
            scores = jnp.where(jnp.concatenate([seen] * heads, axis=1), scores, NEGATIVE)
        probs = jnp.exp(scores - lse)
        d_scores = (probs * (nt(rows, douts) - delta)).astype(jnp.bfloat16)
        dkv_ref[pl.ds(start, BK), :] += nn(d_scores, queries) + nn(
            probs.astype(jnp.bfloat16), douts
        )
        acc_ref[...] += tn(d_scores, rows)

    chunk_loops(bounds_ref, step)
    result = acc_ref[...] * 0.125
    dq_ref[...] = jnp.concatenate(
        [result[h * BQ : (h + 1) * BQ, :WIDTH] for h in range(heads)], axis=1
    ).astype(jnp.bfloat16)


def attention_back(bounds, lo_row, q, kv, out, dout, lse):
    rows, width = q.shape
    heads = width // WIDTH
    blocks = rows // BQ
    row_block = pl.BlockSpec((BQ, width), lambda b: (b, 0))
    return pl.pallas_call(
        attention_back_kernel,
        grid=(blocks,),
        in_specs=[
            pl.BlockSpec(memory_space=pltpu.SMEM),
            pl.BlockSpec((1, BQ), lambda b: (0, b)),
            row_block,
            pl.BlockSpec(memory_space=pltpu.VMEM),
            row_block,
            row_block,
            pl.BlockSpec((None, 8, heads * BQ), lambda b: (b, 0, 0)),
        ],
        out_specs=[
            row_block,
            pl.BlockSpec(kv.shape, lambda b: (0, 0)),
        ],
        out_shape=[
            jax.ShapeDtypeStruct((rows, width), jnp.bfloat16),
            jax.ShapeDtypeStruct(kv.shape, jnp.float32),
        ],
        scratch_shapes=[pltpu.VMEM((heads * BQ, 2 * WIDTH), jnp.float32)],
        compiler_params=pltpu.CompilerParams(vmem_limit_bytes=48 << 20),
        cost_estimate=pl.CostEstimate(
            flops=10 * rows * 4096 * width, bytes_accessed=8 << 20, transcendentals=rows * 4096 * 3
        ),
        name="attention_back",
    )(bounds, lo_row, q, kv, out, dout, lse)


RING = 4
MESH = pl.DeviceIdType.MESH
VMEM = pl.BlockSpec(memory_space=pltpu.VMEM)


def at_seq(index):
    return {"seq": index}


def at_fsdp(index):
    return {"fsdp": index}


def ring_places(s):
    x, y = lax.div(s, RING), lax.rem(s, RING)

    def place(dx, dy):
        return lax.rem(x + dx, 2) * RING + lax.rem(y + dy, RING)

    return {
        "up": place(0, 1),
        "down": place(0, 3),
        "far": place(0, 2),
        "over": place(1, 0),
        "over_up": place(1, 1),
        "over_down": place(1, 3),
        "over_far": place(1, 2),
    }


def greet(targets):
    barrier = pltpu.get_barrier_semaphore()
    for target in targets:
        pl.semaphore_signal(barrier, inc=1, device_id=target, device_id_type=MESH)
    pl.semaphore_wait(barrier, len(targets))


def send(src, dst, sems, index, target):
    copy = pltpu.make_async_remote_copy(
        src_ref=src,
        dst_ref=dst,
        send_sem=sems[0].at[index],
        recv_sem=sems[1].at[index],
        device_id=target,
        device_id_type=MESH,
    )
    copy.start()
    return copy


def ring_gather(out, s, sems, base):
    p = ring_places(s)
    half = out.shape[1] // 2
    top, bottom = pl.ds(0, half), pl.ds(half, half)
    up, down, over = at_seq(p["up"]), at_seq(p["down"]), at_seq(p["over"])
    own_up = send(out.at[s], out.at[s], sems, base, up)
    own_down = send(out.at[s], out.at[s], sems, base + 1, down)
    own_over = send(out.at[s], out.at[s], sems, base + 2, over)
    own_up.wait_recv()
    block = out.at[p["down"], top]
    far_up = send(block, block, sems, base + 3, up)
    own_down.wait_recv()
    block = out.at[p["up"], bottom]
    far_down = send(block, block, sems, base + 4, down)
    own_over.wait_recv()
    block = out.at[p["over"]]
    over_up = send(block, block, sems, base + 5, up)
    over_down = send(block, block, sems, base + 6, down)
    far_up.wait_recv()
    far_down.wait_recv()
    block = out.at[p["far"]]
    far_over = send(block, block, sems, base + 7, over)
    over_up.wait_recv()
    over_down.wait_recv()
    far_over.wait_recv()
    for copy in (own_up, own_down, own_over, far_up, far_down, over_up, over_down, far_over):
        copy.wait_send()


def ring_scatter(partial, tx, rx, rx_half, s, sems, base):
    p = ring_places(s)
    half = rx_half.shape[1]
    up, down, over = at_seq(p["up"]), at_seq(p["down"]), at_seq(p["over"])

    def put(slot, value):
        tx[slot] = value.astype(tx.dtype)
        return tx.at[slot]

    def wide(ref):
        return ref[...].astype(jnp.float32)

    first = send(put(0, partial(p["over_far"])), rx.at[0], sems, base, over)
    second = send(put(1, partial(p["over_up"])), rx.at[1], sems, base + 1, up)
    third = send(put(2, partial(p["over_down"])), rx.at[2], sems, base + 2, down)
    far = partial(p["far"])
    first.wait_recv()
    put(3, far + wide(rx.at[0]))
    to_down = send(tx.at[3, pl.ds(0, half)], rx_half.at[0], sems, base + 3, down)
    to_up = send(tx.at[3, pl.ds(half, half)], rx_half.at[1], sems, base + 4, up)
    across = partial(p["over"])
    second.wait_recv()
    third.wait_recv()
    fourth = send(
        put(4, across + wide(rx.at[1]) + wide(rx.at[2])), rx.at[3], sems, base + 5, over
    )
    value = partial(p["down"])
    to_down.wait_recv()
    tx[5, half:] = value[half:].astype(tx.dtype)
    tx[5, :half] = (value[:half] + wide(rx_half.at[0])).astype(tx.dtype)
    fifth = send(tx.at[5], rx.at[4], sems, base + 6, down)
    value = partial(p["up"])
    to_up.wait_recv()
    tx[6, :half] = value[:half].astype(tx.dtype)
    tx[6, half:] = (value[half:] + wide(rx_half.at[1])).astype(tx.dtype)
    sixth = send(tx.at[6], rx.at[5], sems, base + 7, up)
    own = partial(s)
    fourth.wait_recv()
    fifth.wait_recv()
    sixth.wait_recv()
    total = own + wide(rx.at[3]) + wide(rx.at[4]) + wide(rx.at[5])
    for copy in (first, second, third, to_down, to_up, fourth, fifth, sixth):
        copy.wait_send()
    return total


def ring_buffers(rows, width):
    return [
        pltpu.VMEM((7, rows, width), jnp.bfloat16),
        pltpu.VMEM((6, rows, width), jnp.bfloat16),
        pltpu.VMEM((2, rows // 2, width), jnp.bfloat16),
    ]


def sem_pair(count):
    return [pltpu.SemaphoreType.DMA((count,)), pltpu.SemaphoreType.DMA((count,))]


def others(me, count):
    return [lax.rem(me + k, count) for k in range(1, count)]


def exchange(blocks, into, me, peers, at, sems, base):
    return [
        send(blocks.at[p], into.at[me], sems, base + k, at(p)) for k, p in enumerate(peers)
    ]


def spread(block, into, me, peers, at, sems, base):
    return [send(block, into.at[me], sems, base + k, at(p)) for k, p in enumerate(peers)]


def compact(blocks, rows):
    total = blocks.shape[0]
    shape = (total // 16 * rows, total)
    source = lax.broadcasted_iota(jnp.int32, shape, 1)
    place = lax.shift_right_logical(source, 4) * rows + (source & 15)
    keep = (place == lax.broadcasted_iota(jnp.int32, shape, 0)) & ((source & 15) < rows)
    return nn(keep.astype(jnp.bfloat16), blocks).astype(jnp.bfloat16)


def expand(rows_in, rows):
    shape = (rows_in.shape[0] // rows * 16, rows_in.shape[0])
    target = lax.broadcasted_iota(jnp.int32, shape, 0)
    place = lax.shift_right_logical(target, 4) * rows + (target & 15)
    keep = (place == lax.broadcasted_iota(jnp.int32, shape, 1)) & ((target & 15) < rows)
    return nn(keep.astype(jnp.bfloat16), rows_in).astype(jnp.bfloat16)


def scale_of(values):
    return lax.rsqrt(jnp.mean(values * values, axis=-1, keepdims=True) + EPS)


def rms_back(d_normed, unit, scale, gain):
    d_unit = d_normed * gain
    return scale * (d_unit - unit * jnp.mean(d_unit * unit, axis=-1, keepdims=True))


SMALL = 3 * WIDTH
KEYS = 4 * WIDTH


def start_kernel(
    tokens_ref, columns_ref, experts_ref, chosen_ref,
    normed_ref, q_ref, kv_ref, weight_ref, small_ref, rows_ref, chosen_out_ref,
    all_ref, columns_in, experts_in, send_sems, recv_sems,
):
    s, g = lax.axis_index("seq"), lax.axis_index("fsdp")
    peers, groups = others(s, 8), others(g, 16)
    sems = (send_sems, recv_sems)
    greet([at_seq(p) for p in peers] + [at_fsdp(p) for p in groups])
    copies = exchange(columns_ref, columns_in, s, peers, at_seq, sems, 8)
    more = spread(chosen_ref, chosen_out_ref, s, peers, at_seq, sems, 37)
    more += exchange(experts_ref, experts_in, s, peers, at_seq, sems, 15)
    all_ref[s] = tokens_ref[...]
    columns_in[s] = columns_ref[s]
    experts_in[s] = experts_ref[s]
    chosen_out_ref[s] = chosen_ref[...]
    for copy in copies:
        copy.wait_recv()
    mine = pl.ds(pl.multiple_of(g * 96, 32), 96)
    weight_ref[mine, :] = compact(columns_in[...].reshape(128, columns_in.shape[2]), 12)
    wide = [
        send(weight_ref.at[mine], weight_ref.at[mine], sems, 22 + k, at_fsdp(p))
        for k, p in enumerate(groups)
    ]
    ring_gather(all_ref, s, sems, 0)
    for copy in more:
        copy.wait_recv()
    rows_ref[...] = compact(experts_in[...].reshape(128, experts_in.shape[2]), 12)
    for copy in wide:
        copy.wait_recv()
    pick = lax.broadcasted_iota(jnp.int32, (8, 2 * WIDTH), 0) + (SMALL - 2 * WIDTH)
    pick = (pick == lax.broadcasted_iota(jnp.int32, (8, 2 * WIDTH), 1)).astype(jnp.bfloat16)
    small_ref[...] = nt(pick, weight_ref[:, 2 * WIDTH : 4 * WIDTH])
    gain = small_ref[0:1, :]

    @pl.loop(0, 8)
    def _(block):
        place = pl.ds(pl.multiple_of(block * 128, 128), 128)
        values = all_ref[block].astype(jnp.float32)
        normed = (values * scale_of(values) * gain).astype(jnp.bfloat16)
        normed_ref[place, :] = normed
        result = nn(normed, weight_ref[...]).astype(jnp.bfloat16)
        q_ref[place, :] = result[:, :SMALL]
        kv_ref[place, :] = result[:, KEYS:]

    for copy in copies + more + wide:
        copy.wait_send()


def start(tokens, columns, experts, chosen):
    own, model = tokens.shape
    rows = 8 * own
    width = columns.shape[2]
    bf16, f32 = jnp.bfloat16, jnp.float32
    return pl.pallas_call(
        start_kernel,
        in_specs=[VMEM] * 4,
        out_specs=[VMEM] * 7,
        out_shape=[
            jax.ShapeDtypeStruct((rows, model), bf16),
            jax.ShapeDtypeStruct((rows, SMALL), bf16),
            jax.ShapeDtypeStruct((rows, width - KEYS), bf16),
            jax.ShapeDtypeStruct((model, width), bf16),
            jax.ShapeDtypeStruct((8, model), f32),
            jax.ShapeDtypeStruct((96, experts.shape[2]), bf16),
            jax.ShapeDtypeStruct((8,) + chosen.shape, f32),
        ],
        scratch_shapes=[
            pltpu.VMEM((8, own, model), bf16),
            pltpu.VMEM(columns.shape, bf16),
            pltpu.VMEM(experts.shape, bf16),
            *sem_pair(44),
        ],
        compiler_params=pltpu.CompilerParams(
            collective_id=1, has_side_effects=True, vmem_limit_bytes=48 << 20
        ),
        name="start",
    )(tokens, columns, experts, chosen)


def window_kernel(kv_ref, out_ref, send_sems, recv_sems):
    g = lax.axis_index("fsdp")
    core = lax.rem(g, 2)
    after, before, partner = lax.rem(g + 2, 16), lax.rem(g + 14, 16), g + 1 - 2 * core
    sems = (send_sems, recv_sems)
    greet([at_fsdp(after), at_fsdp(before), at_fsdp(partner)])
    out_ref[4] = kv_ref[...]
    first = send(kv_ref, out_ref.at[2], sems, 0, at_fsdp(after))
    first.wait_recv()
    second = send(out_ref.at[2], out_ref.at[0], sems, 1, at_fsdp(after))
    third = send(out_ref.at[4 - 2 * core], out_ref.at[3], sems, 2, at_fsdp(partner))
    second.wait_recv()
    fourth = send(out_ref.at[2 - 2 * core], out_ref.at[1], sems, 3, at_fsdp(partner))
    third.wait_recv()
    fourth.wait_recv()
    for copy in (first, second, third, fourth):
        copy.wait_send()


def window_of(kv):
    return pl.pallas_call(
        window_kernel,
        in_specs=[VMEM],
        out_specs=VMEM,
        out_shape=jax.ShapeDtypeStruct((LOOK + 1,) + kv.shape, kv.dtype),
        scratch_shapes=sem_pair(4),
        compiler_params=pltpu.CompilerParams(
            collective_id=2, has_side_effects=True, vmem_limit_bytes=48 << 20
        ),
        name="window",
    )(kv)


def window_back_kernel(d_ref, out_ref, tx, rx, send_sems, recv_sems):
    g = lax.axis_index("fsdp")
    core = lax.rem(g, 2)
    after, before, partner = lax.rem(g + 2, 16), lax.rem(g + 14, 16), g + 1 - 2 * core
    sems = (send_sems, recv_sems)
    odd = core.astype(jnp.float32)
    even = 1.0 - odd
    greet([at_fsdp(after), at_fsdp(before), at_fsdp(partner)])

    def wide(slot):
        return rx[slot].astype(jnp.float32)

    tx[1] = d_ref[1].astype(jnp.bfloat16)
    one = send(tx.at[1], rx.at[1], sems, 1, at_fsdp(partner))
    tx[2] = d_ref[3].astype(jnp.bfloat16)
    two = send(tx.at[2], rx.at[2], sems, 2, at_fsdp(partner))
    one.wait_recv()
    tx[0] = (d_ref[0] + odd * wide(1)).astype(jnp.bfloat16)
    zero = send(tx.at[0], rx.at[0], sems, 0, at_fsdp(before))
    two.wait_recv()
    zero.wait_recv()
    tx[3] = (d_ref[2] + wide(0) + odd * wide(2) + even * wide(1)).astype(jnp.bfloat16)
    three = send(tx.at[3], rx.at[3], sems, 3, at_fsdp(before))
    three.wait_recv()
    out_ref[...] = (d_ref[4] + wide(3) + even * wide(2)).astype(jnp.bfloat16)
    for copy in (zero, one, two, three):
        copy.wait_send()


def window_back(d_window):
    shape = d_window.shape[1:]
    return pl.pallas_call(
        window_back_kernel,
        in_specs=[VMEM],
        out_specs=VMEM,
        out_shape=jax.ShapeDtypeStruct(shape, jnp.bfloat16),
        scratch_shapes=[
            pltpu.VMEM((4,) + shape, jnp.bfloat16),
            pltpu.VMEM((4,) + shape, jnp.bfloat16),
            *sem_pair(4),
        ],
        compiler_params=pltpu.CompilerParams(
            collective_id=3, has_side_effects=True, vmem_limit_bytes=48 << 20
        ),
        name="window_back",
    )(d_window)


def middle_kernel(
    attended_ref, weight_ref, tokens_ref, small_ref, resid_ref, normed_ref,
    tx, rx, rx_half, send_sems, recv_sems,
):
    s = lax.axis_index("seq")
    p = ring_places(s)
    sems = (send_sems, recv_sems)
    greet([at_seq(p["up"]), at_seq(p["down"]), at_seq(p["over"])])

    def partial(place):
        rows = pl.ds(pl.multiple_of(place * 128, 128), 128)
        return nn(attended_ref[rows, :], weight_ref[...])

    branch = ring_scatter(partial, tx, rx, rx_half, s, sems, 0)
    resid = tokens_ref[...].astype(jnp.float32) + branch
    resid_ref[...] = resid
    normed_ref[s] = (resid * scale_of(resid) * small_ref[1:2, :]).astype(jnp.bfloat16)
    ring_gather(normed_ref, s, sems, 8)


def middle(attended, weight, tokens, small):
    own, model = tokens.shape
    return pl.pallas_call(
        middle_kernel,
        in_specs=[VMEM] * 4,
        out_specs=[VMEM] * 2,
        out_shape=[
            jax.ShapeDtypeStruct((own, model), jnp.float32),
            jax.ShapeDtypeStruct((8, own, model), jnp.bfloat16),
        ],
        scratch_shapes=[*ring_buffers(own, model), *sem_pair(16)],
        compiler_params=pltpu.CompilerParams(
            collective_id=4, has_side_effects=True, vmem_limit_bytes=48 << 20
        ),
        name="middle",
    )(attended, weight, tokens, small)


def turn_kernel(
    d_ref, weight_ref, share_ref, probs_ref, chosen_ref, resid_ref, small_ref, cotangent_ref,
    d_resid_ref, branch_ref, logits_ref,
    share_in, tx, rx, rx_half, send_sems, recv_sems,
):
    s = lax.axis_index("seq")
    peers = others(s, 8)
    sems = (send_sems, recv_sems)
    greet([at_seq(p) for p in peers])
    shares = exchange(share_ref, share_in, s, peers, at_seq, sems, 16)
    share_in[s] = share_ref[s]

    def partial(place):
        rows = pl.ds(pl.multiple_of(place * 128, 128), 128)
        return nt(d_ref[rows, :], weight_ref[...])

    d_normed = ring_scatter(partial, tx, rx, rx_half, s, sems, 0)
    for copy in shares:
        copy.wait_recv()
    d_router = jnp.sum(share_in[...], axis=0) * chosen_ref[...]
    probs = probs_ref[...]
    d_logits = probs * (d_router - jnp.sum(probs * d_router, axis=0, keepdims=True))
    d_logits = d_logits.astype(jnp.bfloat16)
    logits_ref[s] = d_logits.astype(jnp.float32)
    spreads = spread(logits_ref.at[s], logits_ref, s, peers, at_seq, sems, 23)
    router = small_ref[...].astype(jnp.bfloat16)
    padded = jnp.concatenate([jnp.zeros((2, 128), jnp.bfloat16), d_logits[:6]], axis=0)
    d_normed = d_normed + tn(padded, router)
    resid = resid_ref[...]
    scale = scale_of(resid)
    d_resid = cotangent_ref[...].astype(jnp.float32) + rms_back(
        d_normed, resid * scale, scale, small_ref[1:2, :]
    )
    d_resid_ref[...] = d_resid
    branch_ref[s] = d_resid.astype(jnp.bfloat16)
    ring_gather(branch_ref, s, sems, 8)
    for copy in spreads:
        copy.wait_recv()
    for copy in shares + spreads:
        copy.wait_send()


def turn(d_gate_up, weight, d_share, probs, chosen, resid, small, cotangent):
    own, model = resid.shape
    return pl.pallas_call(
        turn_kernel,
        in_specs=[VMEM] * 8,
        out_specs=[VMEM] * 3,
        out_shape=[
            jax.ShapeDtypeStruct((own, model), jnp.float32),
            jax.ShapeDtypeStruct((8, own, model), jnp.bfloat16),
            jax.ShapeDtypeStruct(d_share.shape, jnp.float32),
        ],
        scratch_shapes=[
            pltpu.VMEM(d_share.shape, jnp.float32),
            *ring_buffers(own, model),
            *sem_pair(30),
        ],
        compiler_params=pltpu.CompilerParams(
            collective_id=5, has_side_effects=True, vmem_limit_bytes=48 << 20
        ),
        name="turn",
    )(d_gate_up, weight, d_share, probs, chosen, resid, small, cotangent)


def finish_kernel(
    d_ref, weight_ref, grads_ref, experts_ref, d_resid_ref, tokens_ref, small_ref,
    grad_input_ref, columns_out, experts_out,
    grads_in, columns_tx, tx, rx, rx_half, send_sems, recv_sems,
):
    s, g = lax.axis_index("seq"), lax.axis_index("fsdp")
    peers, groups = others(s, 8), others(g, 16)
    sems = (send_sems, recv_sems)
    greet([at_seq(p) for p in peers] + [at_fsdp(p) for p in groups])
    wide = exchange(grads_ref, grads_in, g, groups, at_fsdp, sems, 8)
    grads_in[g] = grads_ref[g]

    def partial(place):
        rows = pl.ds(pl.multiple_of(place * 128, 128), 128)
        return nt(d_ref[rows, :], weight_ref[...])

    d_normed = ring_scatter(partial, tx, rx, rx_half, s, sems, 0)
    for copy in wide:
        copy.wait_recv()
    total = jnp.sum(grads_in[...].astype(jnp.float32), axis=0).astype(jnp.bfloat16)
    columns_tx[...] = expand(total, 12).reshape(columns_tx.shape)
    copies = exchange(columns_tx, columns_out, s, peers, at_seq, sems, 23)
    copies += exchange(experts_ref, experts_out, s, peers, at_seq, sems, 30)
    columns_out[s] = columns_tx[s]
    experts_out[s] = experts_ref[s]
    values = tokens_ref[...].astype(jnp.float32)
    scale = scale_of(values)
    grad_input_ref[...] = d_resid_ref[...] + rms_back(
        d_normed, values * scale, scale, small_ref[0:1, :]
    )
    for copy in copies:
        copy.wait_recv()
    for copy in wide + copies:
        copy.wait_send()


def finish(d_qkv, weight, grads, experts, d_resid, tokens, small):
    own, model = tokens.shape
    columns = jax.ShapeDtypeStruct((8, 16, grads.shape[2]), jnp.bfloat16)
    return pl.pallas_call(
        finish_kernel,
        in_specs=[VMEM] * 7,
        out_specs=[VMEM] * 3,
        out_shape=[
            jax.ShapeDtypeStruct((own, model), jnp.float32),
            columns,
            jax.ShapeDtypeStruct(experts.shape, jnp.bfloat16),
        ],
        scratch_shapes=[
            pltpu.VMEM(grads.shape, jnp.bfloat16),
            pltpu.VMEM(columns.shape, jnp.bfloat16),
            *ring_buffers(own, model),
            *sem_pair(37),
        ],
        compiler_params=pltpu.CompilerParams(
            collective_id=6, has_side_effects=True, vmem_limit_bytes=48 << 20
        ),
        name="finish",
    )(d_qkv, weight, grads, experts, d_resid, tokens, small)


def gather_seq(x):
    return lax.all_gather(x, "seq", axis=0, tiled=True)


def scatter_seq(x):
    return lax.psum_scatter(x.astype(jnp.bfloat16), "seq", scatter_dimension=0, tiled=True)


def gather_fsdp(x, dim=0):
    return lax.all_gather(x, "fsdp", axis=dim, tiled=True)


def scatter_fsdp(x, dim=0):
    return lax.psum_scatter(x.astype(jnp.bfloat16), "fsdp", scatter_dimension=dim, tiled=True)


def head_rows_order(fsdp, seq):
    per = fsdp // seq
    return [
        (f * seq + s, ((f % per) * seq + s) * seq + f // per)
        for f in range(fsdp)
        for s in range(seq)
    ]


def columns_by_owner(fsdp, seq, total):
    inner = total // (fsdp * seq)
    place = np.arange(total).reshape(fsdp, seq, inner).transpose(1, 0, 2).reshape(-1)
    one_hot = np.zeros((total, total), np.float32)
    one_hot[place, np.arange(total)] = 1
    return jnp.asarray(one_hot, jnp.bfloat16)


def pad_rows(x, axis):
    pads = [(0, 0)] * x.ndim
    pads[axis] = (0, 16 - x.shape[axis])
    return jnp.pad(x, pads)


def on_device(
    tokens,
    gain_one,
    w_qkv,
    w_out,
    gain_two,
    w_router,
    w_gate,
    w_up,
    w_down,
    doc_starts,
    routes,
    cotangent,
):
    fsdp, seq = lax.axis_size("fsdp"), lax.axis_size("seq")
    group_index = lax.axis_index("fsdp")
    own, model = tokens.shape
    group_rows = own * seq
    experts, own_model, ff = w_gate.shape
    own_ff = ff // seq
    order = columns_by_owner(fsdp, seq, ff)
    bf16, f32 = jnp.bfloat16, jnp.float32

    grad_all = gather_seq(cotangent)
    down_weight = gather_fsdp(w_down, 1).reshape(experts * own_ff, model)
    out_weight = gather_fsdp(pad_rows(lax.ppermute(w_out, BOTH, head_rows_order(fsdp, seq)), 0)[None])
    out_weight = out_weight[:, :own_model].reshape(fsdp * own_model, model)
    gate_up = nn(
        jnp.concatenate([w_gate, w_up], axis=0).reshape(2 * experts * own_model, ff), order
    ).astype(bf16)
    gate_up = gate_up.reshape(2 * experts, own_model, seq, own_ff)
    gate_up = jnp.transpose(gate_up, (2, 1, 0, 3)).reshape(seq, own_model, 2 * experts * own_ff)
    qkv_parts = jnp.transpose(w_qkv.reshape(own_model, seq, 5 * WIDTH), (1, 0, 2))
    small = jnp.concatenate([gain_one[:, None], gain_two[:, None], w_router], axis=1)
    small = jnp.pad(small, ((0, 0), (0, WIDTH - small.shape[1])))
    columns = jnp.concatenate(
        [
            qkv_parts[:, :, :SMALL],
            jnp.broadcast_to(small[None], (seq,) + small.shape),
            qkv_parts[:, :, SMALL:],
        ],
        axis=2,
    )
    expert_ids = jnp.arange(8, dtype=jnp.int32)
    chosen_own = jnp.sum((routes[None, :, :] == expert_ids[:, None, None]).astype(f32), axis=2)
    normed_one, queries, keyval, weight, small, rows, chosen = start(
        tokens, pad_rows(columns, 1), pad_rows(gate_up, 1), chosen_own
    )
    expert_weight = gather_fsdp(rows)

    window = window_of(keyval).reshape((LOOK + 1) * group_rows, 2 * WIDTH)
    positions = group_index * group_rows + jnp.arange(group_rows, dtype=jnp.int32)
    begins = jnp.max(
        jnp.where(doc_starts[:, None] <= positions[None, :], doc_starts[:, None], 0), axis=0
    )
    lo = begins - (group_index - LOOK) * group_rows
    blocks = group_rows // BQ
    lo_blocks = lo.reshape(blocks, BQ)
    diag = (LOOK * group_rows + jnp.arange(blocks, dtype=jnp.int32) * BQ) // BK
    end = (LOOK * group_rows + (jnp.arange(blocks, dtype=jnp.int32) + 1) * BQ + BK - 1) // BK
    first = jnp.minimum(lo_blocks[:, 0] // BK, diag)
    full = jnp.minimum((lo_blocks[:, -1] + BK - 1) // BK, diag)
    bounds = jnp.stack([first, full, diag, end], axis=1)
    attended, lse = attention(bounds, lo[None, :], queries, window)
    residual, normed_all = middle(attended, out_weight, tokens, small)
    normed_two = lax.dynamic_index_in_dim(normed_all, lax.axis_index("seq"), 0, False)
    normed_all = normed_all.reshape(group_rows, model)

    router = small[2 : 2 + experts].astype(bf16)
    logits = nt(router, normed_all)
    probs = jax.nn.softmax(logits, axis=0)
    chosen_all = jnp.transpose(chosen, (1, 0, 2)).reshape(8, group_rows)[:experts]
    share = jnp.repeat(jnp.transpose(probs * chosen_all), own_ff, axis=1)
    gate_weight, up_weight = jnp.split(expert_weight, 2, axis=1)
    gate_pre = nn(normed_all, gate_weight)
    up_pre = nn(normed_all, up_weight)
    sigmoid = jax.nn.sigmoid(gate_pre)
    silu = gate_pre * sigmoid
    hidden = (silu * up_pre).astype(bf16)
    shared = (hidden.astype(f32) * share).astype(bf16)
    moe_out = scatter_seq(nn(shared, down_weight))
    output = (residual + moe_out.astype(f32)).astype(bf16)
    d_plain = nt(grad_all, down_weight)
    d_share = jnp.sum((d_plain * hidden.astype(f32)).reshape(group_rows, experts, own_ff), axis=2)
    d_share = jnp.transpose(d_share.reshape(seq, own, experts), (0, 2, 1))
    d_share = jnp.pad(d_share, ((0, 0), (0, 8 - experts), (0, 0)))
    d_hidden = d_plain * share
    d_gate = (d_hidden * up_pre * sigmoid * (1.0 + gate_pre * (1.0 - sigmoid))).astype(bf16)
    d_up = (d_hidden * silu).astype(bf16)
    d_gate_up = jnp.concatenate([d_gate, d_up], axis=1)
    probs_own = jnp.transpose(probs.reshape(experts, seq, own), (1, 0, 2))
    probs_own = lax.dynamic_index_in_dim(probs_own, lax.axis_index("seq"), 0, False)
    probs_own = jnp.pad(probs_own, ((0, 8 - experts), (0, 0)))
    d_resid, d_branch_all, d_logits = turn(
        d_gate_up, expert_weight, d_share, probs_own, chosen_own, residual, small, cotangent
    )
    d_branch_all = d_branch_all.reshape(group_rows, model)
    grad_down = tn(shared, grad_all)
    grad_gate_up = tn(normed_all, d_gate_up)
    part_down = scatter_fsdp(grad_down.reshape(experts, own_ff, model), 1)
    part_gate_up = scatter_fsdp(grad_gate_up)

    d_attended = nt(d_branch_all, out_weight).astype(bf16)
    grad_w_out = tn(attended, d_branch_all)
    part_out = scatter_fsdp(pad_rows(grad_w_out.reshape(fsdp, own_model, model), 1))
    d_queries, d_window = attention_back(
        bounds, lo[None, :], queries, window, attended, d_attended, lse
    )
    d_keyval = window_back(d_window.reshape(LOOK + 1, group_rows, 2 * WIDTH))
    d_qkv = jnp.concatenate(
        [d_queries, jnp.zeros((group_rows, WIDTH), bf16), d_keyval], axis=1
    )
    d_logits = jnp.transpose(d_logits, (1, 0, 2)).reshape(8, group_rows)[:experts]
    grad_router = nn(d_logits.astype(bf16), normed_all)
    grads = tn(normed_one, d_qkv)
    grads = jnp.concatenate(
        [
            grads[:, : SMALL + 2],
            jnp.transpose(grad_router),
            grads[:, SMALL + 2 + experts :],
        ],
        axis=1,
    )
    grads = grads.astype(bf16).reshape(fsdp, model // fsdp, -1)
    grad_input, columns, back = finish(
        d_qkv,
        weight,
        grads,
        pad_rows(part_gate_up.reshape(seq, own_model, -1), 1),
        d_resid,
        tokens,
        small,
    )

    shard_down = part_down.astype(f32)
    shard_out = lax.ppermute(
        part_out[0, :own_model], BOTH, [(b, a) for a, b in head_rows_order(fsdp, seq)]
    ).astype(f32)
    columns = columns[:, :own_model].astype(f32)
    shard_qkv = jnp.concatenate([columns[:, :, :SMALL], columns[:, :, KEYS:]], axis=2)
    shard_qkv = jnp.transpose(shard_qkv, (1, 0, 2)).reshape(own_model, -1)
    shard_router = columns[0, :, SMALL + 2 : SMALL + 2 + experts]
    back = back[:, :own_model].reshape(seq, own_model, 2 * experts, own_ff)
    back = jnp.transpose(back, (2, 1, 0, 3)).reshape(2 * experts * own_model, ff)
    back = nt(back, order).reshape(2 * experts, own_model, ff)
    shard_gate, shard_up = back[:experts], back[experts:]

    shard_gain_one = jnp.sum(w_qkv.astype(f32) * shard_qkv, axis=1)
    shard_gain_one = shard_gain_one / gain_one.astype(f32)
    shard_gain_two = jnp.sum(w_router.astype(f32) * shard_router, axis=1)
    shard_gain_two += jnp.sum(w_gate.astype(f32) * shard_gate, axis=(0, 2))
    shard_gain_two += jnp.sum(w_up.astype(f32) * shard_up, axis=(0, 2))
    shard_gain_two = shard_gain_two / gain_two.astype(f32)
    return (
        output,
        grad_input,
        shard_gain_one,
        shard_qkv,
        shard_out,
        shard_gain_two,
        shard_router,
        shard_gate,
        shard_up,
        shard_down,
    )


def solution(mesh):
    rows, vector = P(BOTH, None), P(BOTH)
    middle = P(None, BOTH, None)
    in_specs = (
        rows, vector, rows, rows, vector, rows, middle, middle, middle, P(), rows, rows,
    )
    out_specs = (rows, rows, vector, rows, rows, vector, rows, middle, middle, middle)
    return jax.shard_map(
        on_device, mesh=mesh, in_specs=in_specs, out_specs=out_specs, check_vma=False
    )
```

time: 1100 us -> 641 us (0.58)
  blocking collectives: 518 us -> 37.3 us
  Pallas kernels: 28.6 us -> 318 us
  waiting for transfers between devices: 352 us -> 110 us
  local copies, waits for them, and re-layouts: 31.1 us -> 53.6 us
  starting transfers between devices: 58.2 us -> 35.8 us
  matrix products: 60.9 us -> 42.1 us
    all_gather x2 -> x0, blocking collectives: 301 us -> none  [the longest x1 288 us: on_device(): small = lax.all_gather(small, BOTH, axis=0, tiled=True)]
    pallas_call x0 -> x6, Pallas kernels: none -> 298 us  [the longest x1 77 us: finish(): pl.pallas_call(finish_kernel, in_specs=[VMEM] * 7, out_specs=[VMEM] * 3,...]
    reduce_scatter x4 -> x1, waiting for transfers between devices: 156 us -> 0.01 us  [scatter_seq(): lax.psum_scatter(x.astype(jnp.bfloat16), 'seq', scatter_dimension=0, tile...]
    unnamed x2 -> x0, blocking collectives: 142 us -> none
    all_gather x4 -> x1, waiting for transfers between devices: 104 us -> 0.01 us  [gather_seq(): return lax.all_gather(x, 'seq', axis=0, tiled=True)]
    reduce_scatter x1 -> x2, waiting for transfers between devices: 0.01 us -> 75.4 us  [scatter_fsdp(): lax.psum_scatter(x.astype(jnp.bfloat16), 'fsdp', scatter_dimension=dim, t...]
    all_gather x2, waiting for transfers between devices: 42.8 us -> 0.01 us  [gather_fsdp(): return lax.all_gather(x, 'fsdp', axis=dim, tiled=True)]
    all_gather x2 -> x1, blocking collectives: 74.7 us -> 37.3 us  [gather_fsdp(): return lax.all_gather(x, 'fsdp', axis=dim, tiled=True)]
  transfers between devices with their start and end apart: 29 -> 9, of which waited for: 13 -> 2; matrix products, arithmetic and copies ran while one was open for 12% -> 11% of each run, Pallas kernels for 1% -> 42%
where the time goes in v2:
time: 641 us; the launch traced here: 629 us
  Pallas kernels  318 us (50%)
  waiting for transfers between devices  110 us (17%)
  local copies, waits for them, and re-layouts  53.6 us (8%)
  matrix products  42.1 us (7%)
  blocking collectives  37.3 us (6%)
  starting transfers between devices  35.8 us (6%)
  other arithmetic  16.4 us (3%)
  between operations  15.2 us (2%)
    pallas_call x1, Pallas kernels, finish(): pl.pallas_call(finish_kernel, in_specs=[VMEM] * 7, out_specs=[VMEM] * 3,...  77 us
    reduce_scatter x2, waiting for transfers between devices, scatter_fsdp(): lax.psum_scatter(x.astype(jnp.bfloat16), 'fsdp', scatter_dimension=dim, t...  75.4 us
    pallas_call x1, Pallas kernels, middle(): pl.pallas_call(middle_kernel, in_specs=[VMEM] * 4, out_specs=[VMEM] * 2,...  57.6 us
    pallas_call x1, Pallas kernels, turn(): pl.pallas_call(turn_kernel, in_specs=[VMEM] * 8, out_specs=[VMEM] * 3, ou...  55.1 us
    pallas_call x1, Pallas kernels, start(): pl.pallas_call(start_kernel, in_specs=[VMEM] * 4, out_specs=[VMEM] * 7, o...  52.6 us
    all_gather x1, blocking collectives, gather_fsdp(): return lax.all_gather(x, 'fsdp', axis=dim, tiled=True)  37.3 us
    unnamed x8, waiting for transfers between devices  34.1 us
    pallas_call x1, Pallas kernels, window_back(): pl.pallas_call(window_back_kernel, in_specs=[VMEM], out_specs=VMEM, out_s...  27.8 us
  transfers between devices with their start and end apart: 9, of which 2 were waited for; matrix products, arithmetic and copies ran while one was open for 11% of the time, Pallas kernels for 42%

profile of v2, /device:TPU:3, one launch (start us, length us, event | category | flops | bytes accessed | tf_op | source)
XLA Modules:
  0.0 628.5 jit_solution(14244817538910370269)
XLA Ops:
  13.0 52.6 %start.1 = (bf16[1024,1536]{1,0:T(8,128)(2,1)S(1)}, bf16[1024,192]{1,0:T(8,128)(2,1)S(1)}, bf16[1024,128]{1,0:T(8,128)(2,1)S(1)}, bf16[1536,384]{1,0:T(8,128)(2,...) custom-call(bf16[128,1536]{1,0:T(8,128)(2,1)S(1)} %copy-done, ...), custom_call_target="tpu_custom_call" | custom-call | tf_op jit(solution)/shard_map/start/pallas_call | solution.py:429
  69.7 3.3 collective-permute-start
  73.2 27.5 %window.1 = bf16[5,1024,128]{2,1,0:T(8,128)(2,1)S(1)} custom-call(bf16[1024,128]{1,0:T(8,128)(2,1)S(1)} %get-tuple-element.30.kv_ref), custom_call_target="tpu_custom_call" | custom-call | tf_op jit(solution)/shard_map/window/pallas_call | solution.py:475
  100.9 9.4 %attention.1 = (bf16[1024,192]{1,0:T(8,128)(2,1)S(1)}, f32[4,8,768]{2,1,0:T(8,128)S(1)}) custom-call(s32[4,4]{1,0:T(4,128)S(1)} %pad_add_fusion.bounds_ref, s32[1,1024]{1,0:T(1,128)S(1)} %bitcast.106, bf16[1024,192]{1,0:T(8,128)(2,1)S(1)} %get-tuple-element.29.q_ref, bf16[5120,128]{1,0:T(8,128)(2,1)S(1)} %bitcast.103), custom_call_target="tpu_custom_call" | custom-call | flops 3221225472 | bytes 4194304 | tf_op jit(solution)/shard_map/attention/pallas_call | solution.py:89
  112.5 37.3 %all-gather = bf16[256,1536]{1,0:T(8,128)(2,1)S(1)} all-gather(bf16[16,1536]{1,0:T(8,128)(2,1)S(1)} %pad.35), channel_id=2, replica_groups=mesh['fsdp'=16,'seq'=8] {'fsdp'}, dimensions={0}, use_global_device_ids=true | all-gather | bytes 835584 | tf_op jit(solution)/shard_map/all_gather | solution.py:709
  153.7 57.6 %middle.1 = (f32[128,1536]{1,0:T(8,128)S(1)}, bf16[8,128,1536]{2,1,0:T(8,128)(2,1)S(1)}) custom-call(bf16[1024,192]{1,0:T(8,128)(2,1)S(1)} %copy-done.8, bf16[192,1536]{1,0:T(8,128)(2,1)S(1)} %copy-done.6, bf16[128,1536]{1,0:T(8,128)(2,1)S(1)} %copy-done, f32[8,1536]{1,0:T(8,128)S(1)} %copy-done.16), custom_call_target="tpu_custom_call" | custom-call | tf_op jit(solution)/shard_map/middle/pallas_call | solution.py:558
  216.2 5.5 fusion.38
  221.8 3.3 fusion.3
  226.7 4.4 multiply_convert_fusion.1
  231.1 2.9 reshape.241
  234.0 3.6 reduce_sum.65
  242.1 55.1 %turn.1 = (f32[128,1536]{1,0:T(8,128)S(1)}, bf16[8,128,1536]{2,1,0:T(8,128)(2,1)}, f32[8,8,128]{2,1,0:T(8,128)S(1)}) custom-call(bf16[1024,1024]{1,0:T(8,128)(2,1)S(1)} %pad_maximum_fusion.d_ref, bf16[1536,1024]{1,0:T(8,128)(2,1)} %all-gather.5.cloned.1.call-done.weight_ref, f32[8,8,128]{2,1,0:T(8,128)S(1)} %pad.36.share_ref, f32[8,128]{1,0:T(8,128)S(1)} %pad.37.probs_ref, ...), custom_call_target="tpu_custom_call" | custom-call | tf_op jit(solution)/shard_map/turn/pallas_call | solution.py:618
  297.3 3.0 convolution_convert_fusion.4
  301.7 10.0 %reduce-scatter.13.cloned.1.call-start = ((), (), s32[]{:S(2)}) async-start(), calls=%async_computation.10 | async-start | bytes 1671168
  311.7 4.7 convolution_convert_fusion.2
  319.1 6.5 %convolution_convert_fusion.1 = bf16[1536,1024]{1,0:T(8,128)(2,1)} fusion(bf16[1024,1536]{1,0:T(8,128)(2,1)S(1)} %bitcast.100, bf16[1024,512]{1,0:T(8,128)(2,1)} %get-tuple-element.101, bf16[1024,512]{1,0:T(8,128)(2,1)} %get-tuple-element.100), kind=kOutput, calls=%fused_computation.1 | convolution fusion | flops 3226992640 | bytes 8388608 | tf_op jit(solution)/shard_map/dot_general | solution.py:26
  325.7 6.0 convolution_convert_fusion
  331.8 3.9 convolution_convert_fusion.5
  343.0 11.3 %attention_back.1 = (bf16[1024,192]{1,0:T(8,128)(2,1)S(1)}, f32[5120,128]{1,0:T(8,128)S(1)}) custom-call(s32[4,4]{1,0:T(4,128)S(1)} %pad_add_fusion.bounds_ref, s32[1,1024]{1,0:T(1,128)S(1)} %bitcast.107, bf16[1024,192]{1,0:T(8,128)(2,1)S(1)} %copy-done.32, bf16[5120,128]{1,0:T(8,128)(2,1)S(1)} %bitcast.104, bf16[1024,192]{1,0:T(8,128)(2,1)S(1)} %copy-done.9, ...), custom_call_target="tpu_custom_call" | custom-call | flops 8053063680 | bytes 8388608 | tf_op jit(solution)/shard_map/attention_back/pallas_call | solution.py:165
  354.4 27.8 %window_back.1 = bf16[1024,128]{1,0:T(8,128)(2,1)S(1)} custom-call(f32[5,1024,128]{2,1,0:T(8,128)S(1)} %bitcast.101), custom_call_target="tpu_custom_call" | custom-call | tf_op jit(solution)/shard_map/window_back/pallas_call | solution.py:519
  393.0 22.2 %collective-permute-start.1 = (bf16[12,1536]{1,0:T(8,128)(2,1)S(1)}, bf16[12,1536]{1,0:T(8,128)(2,1)S(1)}, u32[]{:S(2)}, u32[]{:S(2)}) collective-permute-start(bf16[12,1536]{1,0:T(8,128)(2,1)S(1)} %slice_bitcast_fusion), channel_id=1, source_target_pairs={{0,0},{8,1},{16,2},{24,3},{32,4},{40,5},{48,6},{56,7},{64,8},{72,9... | collective-permute-start | bytes 110600 | tf_op jit(solution)/shard_map/ppermute | solution.py:874
  418.1 32.6 %reduce-scatter.13.cloned.1.call-done = bf16[8,6144]{1,0:T(8,128)(2,1)} async-done(((bf16[128,6144]{1,0:T(8,128)(2,1)}), bf16[8,6144]{1,0:T(8,128)(2,1)}) %reduce-scatter.13.cloned.1.call-update) | async-done | bytes 98320
  453.9 75.4 %reduce-scatter.9.cloned.1.call-done = bf16[96,1024]{1,0:T(8,128)(2,1)} async-done(((bf16[1536,1024]{1,0:T(8,128)(2,1)}), bf16[96,1024]{1,0:T(8,128)(2,1)}) %reduce-scatter.9.cloned.1.call-update) | async-done | bytes 196624 | tf_op jit(solution)/shard_map/reduce_scatter | solution.py:713
  534.0 77.0 %finish.1 = (f32[128,1536]{1,0:T(8,128)S(1)}, bf16[8,16,384]{2,1,0:T(8,128)(2,1)S(1)}, bf16[8,16,1024]{2,1,0:T(8,128)(2,1)S(1)}) custom-call(bf16[1024,384]{1,0:T(8,128)(2,1)S(1)} %copy-done.5, bf16[1536,384]{1,0:T(8,128)(2,1)S(1)} %copy-done.14, bf16[16,96,384]{2,1,0:T(8,128)(2,1)S(1)} %pad_maximum_fusion.1.grads_ref, ...), custom_call_target="tpu_custom_call" | custom-call | tf_op jit(solution)/shard_map/finish/pallas_call | solution.py:678
  (215 shorter events, 70.0 us)
Async XLA Ops:
  7.2 4.7 copy-start.35
  7.2 209.0 %all-gather.7.cloned.1.call-start = ((), (), s32[]{:S(2)}) async-start(), calls=%async_computation.5 | async-start | bytes 1671168 | tf_op jit(solution)/shard_map/all_gather | solution.py:709
  7.9 208.3 %all-gather.9.cloned.1.call-start = ((), (), s32[]{:S(2)}) async-start(), calls=%async_computation.7 | async-start | bytes 3538944 | tf_op jit(solution)/shard_map/all_gather | solution.py:701
  8.7 213.1 %all-gather.5.cloned.1.call-start = ((), (), s32[]{:S(2)}) async-start(), calls=%async_computation.4 | async-start | bytes 3342336 | tf_op jit(solution)/shard_map/all_gather | solution.py:709
  12.4 57.2 %copy-start.52 = (bf16[12,1536]{1,0:T(8,128)(2,1)S(1)}, bf16[12,1536]{1,0:T(8,128)(2,1)}, u32[]{:S(2)}) copy-start(bf16[12,1536]{1,0:T(8,128)(2,1)} %param.16) | copy-start | bytes 110596
  12.4 60.6 %copy-start.50 = (s32[34]{0:T(128)S(1)}, s32[34]{0:T(128)}, u32[]{:S(2)}) copy-start(s32[34]{0:T(128)} %param.22) | copy-start | bytes 412
  69.6 40.7 %copy-start.31 = (bf16[1024,192]{1,0:T(8,128)(2,1)}, bf16[1024,192]{1,0:T(8,128)(2,1)S(1)}, u32[]{:S(2)}) copy-start(bf16[1024,192]{1,0:T(8,128)(2,1)S(1)} %get-tuple-element.29.q_ref) | copy-start | bytes 1179652
  69.6 322.6 %reduce-scatter.11.cloned.1.call-start = ((), (), s32[]{:S(2)}) async-start(), calls=%async_computation.9 | async-start | bytes 835584 | tf_op jit(solution)/shard_map/reduce_scatter | solution.py:713
  69.7 42.8 %collective-permute-start = (bf16[12,1536]{1,0:T(8,128)(2,1)S(1)}, bf16[12,1536]{1,0:T(8,128)(2,1)S(1)}, u32[]{:S(2)}, u32[]{:S(2)}) collective-permute-start(bf16[12,1536]{1,0:T(8,128)(2,1)S(1)} %copy-done.52), channel_id=1, source_target_pairs={{0,0},{1,8},{2,16},{3,24},{4,32},{5,40},{6,48},{7,56},{8,64},{9,72... | collective-permute-start | bytes 110600 | tf_op jit(solution)/shard_map/ppermute | solution.py:764
  111.4 39.4 %copy-start.7 = (bf16[1024,192]{1,0:T(8,128)(2,1)}, bf16[1024,192]{1,0:T(8,128)(2,1)S(1)}, u32[]{:S(2)}) copy-start(bf16[1024,192]{1,0:T(8,128)(2,1)S(1)} %get-tuple-element.31.attended_ref.out_ref) | copy-start | bytes 1179652
  111.4 39.4 %copy-start.33 = (f32[4,8,768]{2,1,0:T(8,128)}, f32[4,8,768]{2,1,0:T(8,128)S(1)}, u32[]{:S(2)}) copy-start(f32[4,8,768]{2,1,0:T(8,128)S(1)} %get-tuple-element.38.lse_ref) | copy-start | bytes 294916
  153.7 59.5 %copy-start.28 = (f32[8,8,128]{2,1,0:T(8,128)S(1)}, f32[8,8,128]{2,1,0:T(8,128)}, u32[]{:S(2)}) copy-start(f32[8,8,128]{2,1,0:T(8,128)} %copy-done.27) | copy-start | bytes 98308
  221.8 4.9 copy-start.37
  226.6 4.5 copy-start.39
  242.1 55.1 %copy-start.42 = (bf16[16,12,1024]{2,1,0:T(8,128)(2,1)S(1)}, bf16[16,12,1024]{2,1,0:T(8,128)(2,1)}, u32[]{:S(2)}) copy-start(bf16[16,12,1024]{2,1,0:T(8,128)(2,1)} %dot_general.54) | copy-start | bytes 1179652
  301.7 149.1 %reduce-scatter.13.cloned.1.call-start = ((), (), s32[]{:S(2)}) async-start(), calls=%async_computation.10 | async-start | bytes 1671168
  319.1 210.3 %reduce-scatter.9.cloned.1.call-start = ((), (), s32[]{:S(2)}) async-start(), calls=%async_computation.8 | async-start | bytes 3342336 | tf_op jit(solution)/shard_map/reduce_scatter | solution.py:713
  325.7 293.1 %reduce-scatter.7.cloned.1.call-start = ((), (), s32[]{:S(2)}) async-start(), calls=%async_computation.6 | async-start | bytes 3538944 | tf_op jit(solution)/shard_map/reduce_scatter | solution.py:705
  354.4 28.0 %copy-start.30 = (bf16[1024,1536]{1,0:T(8,128)(2,1)S(1)}, bf16[1024,1536]{1,0:T(8,128)(2,1)}, u32[]{:S(2)}) copy-start(bf16[1024,1536]{1,0:T(8,128)(2,1)} %copy-done.29) | copy-start | bytes 9437188
  393.0 24.5 %collective-permute-start.1 = (bf16[12,1536]{1,0:T(8,128)(2,1)S(1)}, bf16[12,1536]{1,0:T(8,128)(2,1)S(1)}, u32[]{:S(2)}, u32[]{:S(2)}) collective-permute-start(bf16[12,1536]{1,0:T(8,128)(2,1)S(1)} %slice_bitcast_fusion), channel_id=1, source_target_pairs={{0,0},{8,1},{16,2},{24,3},{32,4},{40,5},{48,6},{56,7},{64,8},{72,9... | collective-permute-start | bytes 110600 | tf_op jit(solution)/shard_map/ppermute | solution.py:874
  415.2 116.9 %copy-start.5 = (bf16[1024,384]{1,0:T(8,128)(2,1)S(1)}, bf16[1024,384]{1,0:T(8,128)(2,1)}, u32[]{:S(2)}) copy-start(bf16[1024,384]{1,0:T(8,128)(2,1)} %copy-done.4) | copy-start | bytes 2359300
  415.2 116.9 %copy-start.14 = (bf16[1536,384]{1,0:T(8,128)(2,1)S(1)}, bf16[1536,384]{1,0:T(8,128)(2,1)}, u32[]{:S(2)}) copy-start(bf16[1536,384]{1,0:T(8,128)(2,1)} %copy-done.13) | copy-start | bytes 3538948
  612.9 4.3 copy-start.46
  615.5 5.1 copy-start.22
  (39 other events, 67.6 us)
Sparse Core Ops, SparseCore 0:
  10.5 60.0 all-gather.6
  72.2 40.2 all-gather.8
  115.1 67.3 all-gather.4
  301.8 71.7 reduce-scatter.10
  377.8 72.8 reduce-scatter.12
  454.7 74.6 reduce-scatter.8
  531.8 70.6 reduce-scatter.6

commit v3 on v2

v3 whole, which is shorter than its diff:
```python
import functools

import jax
import jax.numpy as jnp
import numpy as np
from jax import lax
from jax.experimental import pallas as pl
from jax.experimental.pallas import tpu as pltpu
from jax.sharding import PartitionSpec as P

WIDTH = 64
LOOK = 4
EXPERTS = 4
EPS = 1e-06
NEGATIVE = -1e30
BQ = 256
BK = 512
BOTH = ("fsdp", "seq")


def nt(a, b):
    return lax.dot_general(a, b, (((1,), (1,)), ((), ())), preferred_element_type=jnp.float32)


def tn(a, b):
    return lax.dot_general(a, b, (((0,), (0,)), ((), ())), preferred_element_type=jnp.float32)


def nn(a, b):
    return jnp.dot(a, b, preferred_element_type=jnp.float32)


def stack_heads(rows, low):
    heads = rows.shape[1] // WIDTH
    zero = jnp.zeros((rows.shape[0], WIDTH), rows.dtype)
    parts = []
    for h in range(heads):
        part = rows[:, h * WIDTH : (h + 1) * WIDTH]
        parts.append(jnp.concatenate([part, zero] if low else [zero, part], axis=1))
    return jnp.concatenate(parts, axis=0)


def chunk_loops(bounds_ref, step):
    b = pl.program_id(0)
    first, full, diag, end = (bounds_ref[b, i] for i in range(4))
    pl.loop(first, full)(lambda c: step(c, True))
    pl.loop(full, diag)(lambda c: step(c, False))
    pl.loop(diag, end)(lambda c: step(c, True))


def attention_kernel(bounds_ref, lo_ref, q_ref, kv_ref, out_ref, lse_ref, m_ref, l_ref, acc_ref):
    heads = q_ref.shape[1] // WIDTH
    queries = stack_heads(q_ref[...] * 0.125, True)
    m_ref[...] = jnp.full_like(m_ref, NEGATIVE)
    l_ref[...] = jnp.zeros_like(l_ref)
    acc_ref[...] = jnp.zeros_like(acc_ref)
    base = LOOK * 1024 + pl.program_id(0) * BQ

    def step(c, masked):
        start = pl.multiple_of(c * BK, BK)
        rows = kv_ref[pl.ds(start, BK), :]
        scores = nt(rows, queries)
        if masked:
            key = start + lax.broadcasted_iota(jnp.int32, (BK, BQ), 0)
            query = base + lax.broadcasted_iota(jnp.int32, (BK, BQ), 1)
            seen = (key >= lo_ref[...]) & (key <= query)
            scores = jnp.where(jnp.concatenate([seen] * heads, axis=1), scores, NEGATIVE)
        old = m_ref[...]
        new = jnp.maximum(old, jnp.max(scores, axis=0, keepdims=True))
        probs = jnp.exp(scores - new)
        fade = jnp.exp(old - new)
        m_ref[...] = new
        l_ref[...] = l_ref[...] * fade + jnp.sum(probs, axis=0, keepdims=True)
        acc_ref[...] = acc_ref[...] * fade + tn(rows, probs.astype(jnp.bfloat16))

    chunk_loops(bounds_ref, step)
    total = l_ref[...]
    result = jnp.transpose(acc_ref[...] / total)
    out_ref[...] = jnp.concatenate(
        [result[h * BQ : (h + 1) * BQ, WIDTH:] for h in range(heads)], axis=1
    ).astype(jnp.bfloat16)
    lse_ref[...] = jnp.broadcast_to(m_ref[...] + jnp.log(total), lse_ref.shape)


def attention(bounds, lo, q, kv):
    rows, width = q.shape
    heads = width // WIDTH
    blocks = rows // BQ
    return pl.pallas_call(
        attention_kernel,
        grid=(blocks,),
        in_specs=[
            pl.BlockSpec(memory_space=pltpu.SMEM),
            pl.BlockSpec((1, BQ), lambda b: (0, b)),
            pl.BlockSpec((BQ, width), lambda b: (b, 0)),
            pl.BlockSpec(memory_space=pltpu.VMEM),
        ],
        out_specs=[
            pl.BlockSpec((BQ, width), lambda b: (b, 0)),
            pl.BlockSpec((None, 8, heads * BQ), lambda b: (b, 0, 0)),
        ],
        out_shape=[
            jax.ShapeDtypeStruct((rows, width), jnp.bfloat16),
            jax.ShapeDtypeStruct((blocks, 8, heads * BQ), jnp.float32),
        ],
        scratch_shapes=[
            pltpu.VMEM((1, heads * BQ), jnp.float32),
            pltpu.VMEM((1, heads * BQ), jnp.float32),
            pltpu.VMEM((2 * WIDTH, heads * BQ), jnp.float32),
        ],
        compiler_params=pltpu.CompilerParams(vmem_limit_bytes=48 << 20),
        cost_estimate=pl.CostEstimate(
            flops=4 * rows * 4096 * width, bytes_accessed=4 << 20, transcendentals=rows * 4096 * 3
        ),
        name="attention",
    )(bounds, lo, q, kv)


def attention_back_kernel(
    bounds_ref, lo_ref, q_ref, kv_ref, out_ref, dout_ref, lse_ref, dq_ref, dkv_ref, acc_ref
):
    heads = q_ref.shape[1] // WIDTH
    queries = stack_heads(q_ref[...] * 0.125, True)
    douts = stack_heads(dout_ref[...], False)
    outs = stack_heads(out_ref[...], False)
    delta = jnp.sum(
        jnp.transpose(douts.astype(jnp.float32) * outs.astype(jnp.float32)), axis=0, keepdims=True
    )
    lse = lse_ref[:1, :]
    acc_ref[...] = jnp.zeros_like(acc_ref)
    base = LOOK * 1024 + pl.program_id(0) * BQ

    @pl.when(pl.program_id(0) == 0)
    def _():
        dkv_ref[...] = jnp.zeros_like(dkv_ref)

    def step(c, masked):
        start = pl.multiple_of(c * BK, BK)
        rows = kv_ref[pl.ds(start, BK), :]
        scores = nt(rows, queries)
        if masked:
            key = start + lax.broadcasted_iota(jnp.int32, (BK, BQ), 0)
            query = base + lax.broadcasted_iota(jnp.int32, (BK, BQ), 1)
            seen = (key >= lo_ref[...]) & (key <= query)
            scores = jnp.where(jnp.concatenate([seen] * heads, axis=1), scores, NEGATIVE)
        probs = jnp.exp(scores - lse)
        d_scores = (probs * (nt(rows, douts) - delta)).astype(jnp.bfloat16)
        dkv_ref[pl.ds(start, BK), :] += nn(d_scores, queries) + nn(
            probs.astype(jnp.bfloat16), douts
        )
        acc_ref[...] += tn(d_scores, rows)

    chunk_loops(bounds_ref, step)
    result = acc_ref[...] * 0.125
    dq_ref[...] = jnp.concatenate(
        [result[h * BQ : (h + 1) * BQ, :WIDTH] for h in range(heads)], axis=1
    ).astype(jnp.bfloat16)


def attention_back(bounds, lo_row, q, kv, out, dout, lse):
    rows, width = q.shape
    heads = width // WIDTH
    blocks = rows // BQ
    row_block = pl.BlockSpec((BQ, width), lambda b: (b, 0))
    return pl.pallas_call(
        attention_back_kernel,
        grid=(blocks,),
        in_specs=[
            pl.BlockSpec(memory_space=pltpu.SMEM),
            pl.BlockSpec((1, BQ), lambda b: (0, b)),
            row_block,
            pl.BlockSpec(memory_space=pltpu.VMEM),
            row_block,
            row_block,
            pl.BlockSpec((None, 8, heads * BQ), lambda b: (b, 0, 0)),
        ],
        out_specs=[
            row_block,
            pl.BlockSpec(kv.shape, lambda b: (0, 0)),
        ],
        out_shape=[
            jax.ShapeDtypeStruct((rows, width), jnp.bfloat16),
            jax.ShapeDtypeStruct(kv.shape, jnp.float32),
        ],
        scratch_shapes=[pltpu.VMEM((heads * BQ, 2 * WIDTH), jnp.float32)],
        compiler_params=pltpu.CompilerParams(vmem_limit_bytes=48 << 20),
        cost_estimate=pl.CostEstimate(
            flops=10 * rows * 4096 * width, bytes_accessed=8 << 20, transcendentals=rows * 4096 * 3
        ),
        name="attention_back",
    )(bounds, lo_row, q, kv, out, dout, lse)


RING = 4
MESH = pl.DeviceIdType.MESH
VMEM = pl.BlockSpec(memory_space=pltpu.VMEM)


def at_seq(index):
    return {"seq": index}


def at_fsdp(index):
    return {"fsdp": index}


def ring_places(s):
    x, y = lax.div(s, RING), lax.rem(s, RING)

    def place(dx, dy):
        return lax.rem(x + dx, 2) * RING + lax.rem(y + dy, RING)

    return {
        "up": place(0, 1),
        "down": place(0, 3),
        "far": place(0, 2),
        "over": place(1, 0),
        "over_up": place(1, 1),
        "over_down": place(1, 3),
        "over_far": place(1, 2),
    }


def greet(targets):
    barrier = pltpu.get_barrier_semaphore()
    for target in targets:
        pl.semaphore_signal(barrier, inc=1, device_id=target, device_id_type=MESH)
    pl.semaphore_wait(barrier, len(targets))


def send(src, dst, sems, index, target):
    copy = pltpu.make_async_remote_copy(
        src_ref=src,
        dst_ref=dst,
        send_sem=sems[0].at[index],
        recv_sem=sems[1].at[index],
        device_id=target,
        device_id_type=MESH,
    )
    copy.start()
    return copy


class Task:
    def __init__(self, steps):
        self.steps, self.done, self.value = steps, False, None

    def step(self):
        if not self.done:
            try:
                next(self.steps)
            except StopIteration as end:
                self.done, self.value = True, end.value


def run(task, *beside):
    while not task.done:
        task.step()
        for other in beside:
            other.step()
    return task.value


def run_all(*tasks):
    while not all(task.done for task in tasks):
        for task in tasks:
            task.step()


def ring_gather(out, s, sems, base):
    p = ring_places(s)
    half = out.shape[1] // 2
    top, bottom = pl.ds(0, half), pl.ds(half, half)
    up, down, over = at_seq(p["up"]), at_seq(p["down"]), at_seq(p["over"])
    own_up = send(out.at[s], out.at[s], sems, base, up)
    own_down = send(out.at[s], out.at[s], sems, base + 1, down)
    own_over = send(out.at[s], out.at[s], sems, base + 2, over)
    yield
    own_up.wait_recv()
    block = out.at[p["down"], top]
    far_up = send(block, block, sems, base + 3, up)
    own_down.wait_recv()
    block = out.at[p["up"], bottom]
    far_down = send(block, block, sems, base + 4, down)
    yield
    own_over.wait_recv()
    block = out.at[p["over"]]
    over_up = send(block, block, sems, base + 5, up)
    over_down = send(block, block, sems, base + 6, down)
    yield
    far_up.wait_recv()
    far_down.wait_recv()
    block = out.at[p["far"]]
    far_over = send(block, block, sems, base + 7, over)
    yield
    over_up.wait_recv()
    over_down.wait_recv()
    yield
    far_over.wait_recv()
    for copy in (own_up, own_down, own_over, far_up, far_down, over_up, over_down, far_over):
        copy.wait_send()


def ring_scatter(partial, tx, rx, rx_half, s, sems, base):
    p = ring_places(s)
    half = rx_half.shape[1]
    up, down, over = at_seq(p["up"]), at_seq(p["down"]), at_seq(p["over"])

    def put(slot, value):
        tx[slot] = value.astype(tx.dtype)
        return tx.at[slot]

    def wide(ref):
        return ref[...].astype(jnp.float32)

    first = send(put(0, partial(p["over_far"])), rx.at[0], sems, base, over)
    second = send(put(1, partial(p["over_up"])), rx.at[1], sems, base + 1, up)
    third = send(put(2, partial(p["over_down"])), rx.at[2], sems, base + 2, down)
    far = partial(p["far"])
    yield
    first.wait_recv()
    put(3, far + wide(rx.at[0]))
    to_down = send(tx.at[3, pl.ds(0, half)], rx_half.at[0], sems, base + 3, down)
    to_up = send(tx.at[3, pl.ds(half, half)], rx_half.at[1], sems, base + 4, up)
    across = partial(p["over"])
    yield
    second.wait_recv()
    third.wait_recv()
    fourth = send(
        put(4, across + wide(rx.at[1]) + wide(rx.at[2])), rx.at[3], sems, base + 5, over
    )
    value = partial(p["down"])
    yield
    to_down.wait_recv()
    tx[5, half:] = value[half:].astype(tx.dtype)
    tx[5, :half] = (value[:half] + wide(rx_half.at[0])).astype(tx.dtype)
    fifth = send(tx.at[5], rx.at[4], sems, base + 6, down)
    value = partial(p["up"])
    to_up.wait_recv()
    tx[6, :half] = value[:half].astype(tx.dtype)
    tx[6, half:] = (value[half:] + wide(rx_half.at[1])).astype(tx.dtype)
    sixth = send(tx.at[6], rx.at[5], sems, base + 7, up)
    own = partial(s)
    yield
    fourth.wait_recv()
    fifth.wait_recv()
    sixth.wait_recv()
    total = own + wide(rx.at[3]) + wide(rx.at[4]) + wide(rx.at[5])
    for copy in (first, second, third, to_down, to_up, fourth, fifth, sixth):
        copy.wait_send()
    return total


def ring_buffers(rows, width):
    return [
        pltpu.VMEM((7, rows, width), jnp.bfloat16),
        pltpu.VMEM((6, rows, width), jnp.bfloat16),
        pltpu.VMEM((2, rows // 2, width), jnp.bfloat16),
    ]


def fsdp_place(g):
    x, z, core = lax.div(g, 8), lax.rem(lax.div(g, 2), RING), lax.rem(g, 2)

    def place(dx, dz, dcore):
        return (
            lax.rem(x + dx, 2) * 8 + lax.rem(z + dz, RING) * 2 + lax.rem(core + dcore, 2)
        )

    return place


def fsdp_neighbours(g):
    place = fsdp_place(g)
    return [at_fsdp(place(*d)) for d in ((1, 0, 0), (0, 1, 0), (0, 3, 0), (0, 0, 1))]


def part_of(ref, rows, cut):
    def view(index, half=None):
        first, count = {None: (0, rows), "top": (0, cut), "bottom": (cut, rows - cut)}[half]
        return ref.at[pl.ds(pl.multiple_of(index * rows + first, 16), count)]

    return view


def fsdp_gather(ref, rows, cut, g, sems, base):
    view, place = part_of(ref, rows, cut), fsdp_place(g)
    over, up, down, pal = fsdp_neighbours(g)
    copies = []

    def go(index, half, sem, target):
        copies.append(send(view(index, half), view(index, half), sems, base + sem, target))
        return copies[-1]

    me = place(0, 0, 0)
    to_over = go(me, None, 16, over)
    to_up, to_down = go(me, None, 0, up), go(me, None, 1, down)
    pals = [go(me, None, 8, pal)]
    yield
    to_over.wait_recv()
    side = place(1, 0, 0)
    side_up, side_down = go(side, None, 2, up), go(side, None, 3, down)
    pals.append(go(side, None, 9, pal))
    yield
    to_up.wait_recv()
    far_up = go(place(0, 3, 0), "top", 4, up)
    pals.append(go(place(0, 3, 0), None, 10, pal))
    to_down.wait_recv()
    far_down = go(place(0, 1, 0), "bottom", 5, down) if cut < rows else None
    pals.append(go(place(0, 1, 0), None, 11, pal))
    yield
    side_up.wait_recv()
    side_far_up = go(place(1, 3, 0), "top", 6, up)
    pals.append(go(place(1, 3, 0), None, 12, pal))
    side_down.wait_recv()
    side_far_down = go(place(1, 1, 0), "bottom", 7, down) if cut < rows else None
    pals.append(go(place(1, 1, 0), None, 13, pal))
    yield
    far_up.wait_recv()
    if far_down is not None:
        far_down.wait_recv()
    pals.append(go(place(0, 2, 0), None, 14, pal))
    yield
    side_far_up.wait_recv()
    if side_far_down is not None:
        side_far_down.wait_recv()
    pals.append(go(place(1, 2, 0), None, 15, pal))
    yield
    for copy in pals:
        copy.wait_recv()
    for copy in copies:
        copy.wait_send()


def fsdp_buffers(rows, cut, width):
    return [
        pltpu.VMEM((8 * rows, width), jnp.bfloat16),
        pltpu.VMEM((2, cut, width), jnp.bfloat16),
        pltpu.VMEM((2, max(rows - cut, 16), width), jnp.bfloat16),
        pltpu.VMEM((5, rows, width), jnp.bfloat16),
    ]


def fsdp_scatter(ref, rows, cut, buffers, g, sems, base):
    pair, tops, bottoms, full = buffers
    view, place = part_of(ref, rows, cut), fsdp_place(g)
    over, up, down, pal = fsdp_neighbours(g)
    copies = []

    def go(src, dst, sem, target):
        copies.append(send(src, dst, sems, base + sem, target))
        return copies[-1]

    def wide(part):
        return part[...].astype(jnp.float32)

    def slot(index):
        return pair.at[pl.ds(pl.multiple_of(lax.div(index, 2) * rows, 16), rows)]

    order = [(1, 2), (0, 2), (1, 3), (1, 1), (0, 3), (0, 1), (1, 0), (0, 0)]
    pals = {}
    for k, (dx, dz) in enumerate(order):
        index = place(dx, dz, 1)
        pals[dx, dz] = go(view(index), slot(index), k, pal)
    yield

    def paired(dx, dz):
        pals[dx, dz].wait_recv()
        return wide(view(place(dx, dz, 0))) + wide(slot(place(dx, dz, 0)))

    halves = {}
    for k, dx in enumerate((1, 0)):
        index = place(dx, 2, 0)
        value = paired(dx, 2)
        view(index)[...] = value.astype(jnp.bfloat16)
        halves[dx, "top"] = go(view(index, "top"), tops.at[dx], 8 + 2 * k, down)
        if cut < rows:
            halves[dx, "bottom"] = go(view(index, "bottom"), bottoms.at[dx], 9 + 2 * k, up)
    yield
    fulls = {}
    for k, dx in enumerate((1, 0)):
        index = place(dx, 3, 0)
        value = paired(dx, 3)
        halves[dx, "top"].wait_recv()
        view(index, "top")[...] = (value[:cut] + wide(tops.at[dx])).astype(jnp.bfloat16)
        if cut < rows:
            view(index, "bottom")[...] = value[cut:].astype(jnp.bfloat16)
        fulls[dx, "down"] = go(view(index), full.at[2 * dx], 12 + 2 * k, down)
        index = place(dx, 1, 0)
        value = paired(dx, 1)
        if cut < rows:
            halves[dx, "bottom"].wait_recv()
            view(index, "top")[...] = value[:cut].astype(jnp.bfloat16)
            view(index, "bottom")[...] = (value[cut:] + wide(bottoms.at[dx])).astype(jnp.bfloat16)
        else:
            view(index)[...] = value.astype(jnp.bfloat16)
        fulls[dx, "up"] = go(view(index), full.at[2 * dx + 1], 13 + 2 * k, up)
        yield
    index = place(1, 0, 0)
    value = paired(1, 0)
    fulls[1, "down"].wait_recv()
    fulls[1, "up"].wait_recv()
    view(index)[...] = (value + wide(full.at[2]) + wide(full.at[3])).astype(jnp.bfloat16)
    last = go(view(index), full.at[4], 16, over)
    value = paired(0, 0)
    yield
    fulls[0, "down"].wait_recv()
    fulls[0, "up"].wait_recv()
    value = value + wide(full.at[0]) + wide(full.at[1])
    yield
    last.wait_recv()
    value = value + wide(full.at[4])
    for copy in copies:
        copy.wait_send()
    return value


def sem_pair(count):
    return [pltpu.SemaphoreType.DMA((count,)), pltpu.SemaphoreType.DMA((count,))]


def others(me, count):
    return [lax.rem(me + k, count) for k in range(1, count)]


def exchange(blocks, into, me, peers, at, sems, base):
    return [
        send(blocks.at[p], into.at[me], sems, base + k, at(p)) for k, p in enumerate(peers)
    ]


def spread(block, into, me, peers, at, sems, base):
    return [send(block, into.at[me], sems, base + k, at(p)) for k, p in enumerate(peers)]


def swap_rows(src, dst, sems, index, target, alone):
    away = pltpu.make_async_remote_copy(
        src_ref=src,
        dst_ref=dst,
        send_sem=sems[0].at[index],
        recv_sem=sems[1].at[index],
        device_id=target,
        device_id_type=MESH,
    )
    here = pltpu.make_async_copy(src, dst, sems[0].at[index])
    pl.when(jnp.logical_not(alone))(away.start)
    pl.when(alone)(here.start)

    def wait():
        pl.when(jnp.logical_not(alone))(away.wait)
        pl.when(alone)(here.wait)

    return wait


def head_holder(g, s):
    return {"fsdp": lax.rem(g, 2) * 8 + s, "seq": lax.div(g, 2)}


def head_owner(g, s):
    return {"fsdp": 2 * s + lax.div(g, 8), "seq": lax.rem(g, 8)}


def greet_all(targets, pair, alone):
    barrier = pltpu.get_barrier_semaphore()
    for target in targets:
        pl.semaphore_signal(barrier, inc=1, device_id=target, device_id_type=MESH)

    @pl.when(jnp.logical_not(alone))
    def _():
        for target in pair:
            pl.semaphore_signal(barrier, inc=1, device_id=target, device_id_type=MESH)

    pl.semaphore_wait(barrier, len(targets) + jnp.where(alone, 0, 2))


def compact(blocks, rows):
    total = blocks.shape[0]
    shape = (total // 16 * rows, total)
    source = lax.broadcasted_iota(jnp.int32, shape, 1)
    place = lax.shift_right_logical(source, 4) * rows + (source & 15)
    keep = (place == lax.broadcasted_iota(jnp.int32, shape, 0)) & ((source & 15) < rows)
    return nn(keep.astype(jnp.bfloat16), blocks).astype(jnp.bfloat16)


def expand(rows_in, rows):
    shape = (rows_in.shape[0] // rows * 16, rows_in.shape[0])
    target = lax.broadcasted_iota(jnp.int32, shape, 0)
    place = lax.shift_right_logical(target, 4) * rows + (target & 15)
    keep = (place == lax.broadcasted_iota(jnp.int32, shape, 1)) & ((target & 15) < rows)
    return nn(keep.astype(jnp.bfloat16), rows_in).astype(jnp.bfloat16)


def unit_order(row_axis):
    mixed = lax.broadcasted_iota(jnp.int32, (512, 512), 1 - row_axis)
    plain = lax.broadcasted_iota(jnp.int32, (512, 512), row_axis)
    f = lax.shift_right_logical(mixed, 5)
    e = lax.shift_right_logical(mixed, 3) & 3
    return (e * 128 + f * 8 + (mixed & 7) == plain).astype(jnp.bfloat16)


def scale_of(values):
    return lax.rsqrt(jnp.mean(values * values, axis=-1, keepdims=True) + EPS)


def rms_back(d_normed, unit, scale, gain):
    d_unit = d_normed * gain
    return scale * (d_unit - unit * jnp.mean(d_unit * unit, axis=-1, keepdims=True))


def rows_at(place, count=128):
    return pl.ds(pl.multiple_of(place * count, count), count)


def kernel_params(collective_id):
    return pltpu.CompilerParams(
        collective_id=collective_id, has_side_effects=True, vmem_limit_bytes=52 << 20
    )


def array(shape, dtype=jnp.bfloat16):
    return jax.ShapeDtypeStruct(shape, dtype)


SMALL = 3 * WIDTH
KEYS = 4 * WIDTH


def start_kernel(
    tokens_ref, columns_ref, experts_ref, down_ref, wout_ref, chosen_ref,
    normed_ref, q_ref, kv_ref, weight_ref, small_ref, gate_up_ref, down_all_ref, wout_all_ref,
    chosen_out_ref,
    all_ref, columns_in, experts_in, mixed, send_sems, recv_sems,
):
    s, g = lax.axis_index("seq"), lax.axis_index("fsdp")
    peers = others(s, 8)
    sems = (send_sems, recv_sems)
    holder, owner = head_holder(g, s), head_owner(g, s)
    alone = (holder["fsdp"] == g) & (holder["seq"] == s)
    greet_all([at_seq(p) for p in peers] + fsdp_neighbours(g), (holder, owner), alone)
    copies = exchange(columns_ref, columns_in, s, peers, at_seq, sems, 8)
    wait_rows = swap_rows(
        wout_ref,
        mixed.at[pl.ds(pl.multiple_of(holder["fsdp"] * 48 + 32, 16), 16)],
        sems, 22, holder, alone,
    )
    copies += exchange(experts_ref, experts_in, s, peers, at_seq, sems, 15)
    all_ref[s] = tokens_ref[...]
    tokens_in = Task(ring_gather(all_ref, s, sems, 0))
    tokens_in.step()
    chosen_copies = spread(chosen_ref, chosen_out_ref, s, peers, at_seq, sems, 23)
    columns_in[s] = columns_ref[s]
    experts_in[s] = experts_ref[s]
    chosen_out_ref[s] = chosen_ref[...]
    mixed[pl.ds(pl.multiple_of(g * 48, 16), 32), :] = down_ref[...]
    for copy in copies[:7]:
        copy.wait_recv()
    weight_ref[rows_at(g, 96), :] = compact(columns_in[...].reshape(128, columns_in.shape[2]), 12)
    columns_gather = Task(fsdp_gather(weight_ref, 96, 48, g, sems, 30))
    columns_gather.step()
    for copy in copies[7:]:
        copy.wait_recv()
    gate_up_ref[rows_at(g, 96), :] = compact(experts_in[...].reshape(128, experts_in.shape[2]), 12)
    gate_up_gather = Task(fsdp_gather(gate_up_ref, 96, 48, g, sems, 47))
    gate_up_gather.step()
    wait_rows()
    mixed_gather = Task(fsdp_gather(mixed, 48, 32, g, sems, 64))
    run(columns_gather, tokens_in, gate_up_gather, mixed_gather)
    pick = lax.broadcasted_iota(jnp.int32, (8, 2 * WIDTH), 0) + (SMALL - 2 * WIDTH)
    pick = (pick == lax.broadcasted_iota(jnp.int32, (8, 2 * WIDTH), 1)).astype(jnp.bfloat16)
    small_ref[...] = nt(pick, weight_ref[:, 2 * WIDTH : 4 * WIDTH])
    gain = small_ref[0:1, :]
    run_all(tokens_in, gate_up_gather, mixed_gather)

    @pl.loop(0, 8)
    def _(block):
        values = all_ref[block].astype(jnp.float32)
        normed = (values * scale_of(values) * gain).astype(jnp.bfloat16)
        normed_ref[rows_at(block), :] = normed
        result = nn(normed, weight_ref[...]).astype(jnp.bfloat16)
        q_ref[rows_at(block), :] = result[:, :SMALL]
        kv_ref[rows_at(block), :] = result[:, KEYS:]

    parts = mixed[...].reshape(16, 48, mixed.shape[1])
    down_all_ref[...] = nn(unit_order(0), parts[:, :32].reshape(512, -1)).astype(jnp.bfloat16)
    wout_all_ref[...] = compact(parts[:, 32:].reshape(256, -1), 12)
    for copy in chosen_copies:
        copy.wait_recv()
    for copy in copies + chosen_copies:
        copy.wait_send()


def start(tokens, columns, experts, down, wout, chosen):
    own, model = tokens.shape
    rows = 8 * own
    width = columns.shape[2]
    return pl.pallas_call(
        start_kernel,
        in_specs=[VMEM] * 6,
        out_specs=[VMEM] * 9,
        out_shape=[
            array((rows, model)),
            array((rows, SMALL)),
            array((rows, width - KEYS)),
            array((model, width)),
            array((8, model), jnp.float32),
            array((model, experts.shape[2])),
            array((512, model)),
            array((192, model)),
            array((8,) + chosen.shape, jnp.float32),
        ],
        scratch_shapes=[
            pltpu.VMEM((8, own, model), jnp.bfloat16),
            pltpu.VMEM(columns.shape, jnp.bfloat16),
            pltpu.VMEM(experts.shape, jnp.bfloat16),
            pltpu.VMEM((16 * 48, model), jnp.bfloat16),
            *sem_pair(81),
        ],
        compiler_params=kernel_params(1),
        name="start",
    )(tokens, columns, experts, down, wout, chosen)


def window_steps(kv_ref, out_ref, g, sems, base):
    core = lax.rem(g, 2)
    after, partner = at_fsdp(lax.rem(g + 2, 16)), at_fsdp(g + 1 - 2 * core)
    out_ref[4] = kv_ref[...]
    first = send(kv_ref, out_ref.at[2], sems, base, after)
    yield
    first.wait_recv()
    second = send(out_ref.at[2], out_ref.at[0], sems, base + 1, after)
    third = send(out_ref.at[4 - 2 * core], out_ref.at[3], sems, base + 2, partner)
    yield
    second.wait_recv()
    fourth = send(out_ref.at[2 - 2 * core], out_ref.at[1], sems, base + 3, partner)
    yield
    third.wait_recv()
    fourth.wait_recv()
    for copy in (first, second, third, fourth):
        copy.wait_send()


def window_greeting(g):
    core = lax.rem(g, 2)
    return [at_fsdp(i) for i in (lax.rem(g + 2, 16), lax.rem(g + 14, 16), g + 1 - 2 * core)]


def ring_greeting(s):
    p = ring_places(s)
    return [at_seq(p["up"]), at_seq(p["down"]), at_seq(p["over"])]


def window_kernel(kv_ref, cotangent_ref, out_ref, all_ref, send_sems, recv_sems):
    s, g = lax.axis_index("seq"), lax.axis_index("fsdp")
    sems = (send_sems, recv_sems)
    greet(window_greeting(g) + ring_greeting(s))
    window = Task(window_steps(kv_ref, out_ref, g, sems, 0))
    window.step()
    all_ref[s] = cotangent_ref[...]
    run_all(window, Task(ring_gather(all_ref, s, sems, 4)))


def window_of(kv, cotangent):
    return pl.pallas_call(
        window_kernel,
        in_specs=[VMEM] * 2,
        out_specs=[VMEM] * 2,
        out_shape=[array((LOOK + 1,) + kv.shape), array((8,) + cotangent.shape)],
        scratch_shapes=sem_pair(12),
        compiler_params=kernel_params(2),
        name="window",
    )(kv, cotangent)


def window_back_steps(d_ref, out_ref, tx, rx, g, sems, base):
    core = lax.rem(g, 2)
    before, partner = at_fsdp(lax.rem(g + 14, 16)), at_fsdp(g + 1 - 2 * core)
    odd = core.astype(jnp.float32)
    even = 1.0 - odd

    def wide(slot):
        return rx[slot].astype(jnp.float32)

    tx[1] = d_ref[1].astype(jnp.bfloat16)
    one = send(tx.at[1], rx.at[1], sems, base + 1, partner)
    tx[2] = d_ref[3].astype(jnp.bfloat16)
    two = send(tx.at[2], rx.at[2], sems, base + 2, partner)
    yield
    one.wait_recv()
    tx[0] = (d_ref[0] + odd * wide(1)).astype(jnp.bfloat16)
    zero = send(tx.at[0], rx.at[0], sems, base, before)
    yield
    two.wait_recv()
    zero.wait_recv()
    tx[3] = (d_ref[2] + wide(0) + odd * wide(2) + even * wide(1)).astype(jnp.bfloat16)
    three = send(tx.at[3], rx.at[3], sems, base + 3, before)
    yield
    three.wait_recv()
    out_ref[...] = (d_ref[4] + wide(3) + even * wide(2)).astype(jnp.bfloat16)
    for copy in (zero, one, two, three):
        copy.wait_send()


def window_back_kernel(
    d_ref, shared_ref, down_ref, resid_ref, out_ref, output_ref,
    wtx, wrx, tx, rx, rx_half, send_sems, recv_sems,
):
    s, g = lax.axis_index("seq"), lax.axis_index("fsdp")
    sems = (send_sems, recv_sems)
    greet(window_greeting(g) + ring_greeting(s))
    window = Task(window_back_steps(d_ref, out_ref, wtx, wrx, g, sems, 8))
    window.step()

    def partial(place):
        return nn(shared_ref[rows_at(place), :], down_ref[...])

    total = run(Task(ring_scatter(partial, tx, rx, rx_half, s, sems, 0)), window)
    output_ref[...] = (resid_ref[...] + total).astype(jnp.bfloat16)
    run(window)


def window_back(d_window, shared, down, resid):
    shape = d_window.shape[1:]
    own, model = resid.shape
    return pl.pallas_call(
        window_back_kernel,
        in_specs=[VMEM] * 4,
        out_specs=[VMEM] * 2,
        out_shape=[array(shape), array((own, model))],
        scratch_shapes=[
            pltpu.VMEM((4,) + shape, jnp.bfloat16),
            pltpu.VMEM((4,) + shape, jnp.bfloat16),
            *ring_buffers(own, model),
            *sem_pair(12),
        ],
        compiler_params=kernel_params(3),
        name="window_back",
    )(d_window, shared, down, resid)


def moe_kernel(
    attended_ref, wout_ref, tokens_ref, small_ref, gate_up_ref, down_ref, cotangent_ref, chosen_ref,
    resid_ref, shared_ref, d_resid_ref, branch_ref, router_ref, part_gate_up_ref, part_down_ref,
    normed_ref, d_ref, grad_gate_up, grad_down, probs_ref, share_tx, share_in, logits_ref,
    tx_a, rx_a, half_a, tx_b, rx_b, half_b,
    pair_a, tops_a, bottoms_a, full_a, pair_b, tops_b, bottoms_b, full_b,
    send_sems, recv_sems,
):
    s, g = lax.axis_index("seq"), lax.axis_index("fsdp")
    p = ring_places(s)
    peers = others(s, 8)
    sems = (send_sems, recv_sems)
    greet([at_seq(q) for q in peers] + fsdp_neighbours(g))
    model = tokens_ref.shape[1]
    units = down_ref.shape[0]
    per = units // EXPERTS

    def branch_part(place):
        return nn(attended_ref[rows_at(place), :], wout_ref[...])

    branch = run(Task(ring_scatter(branch_part, tx_a, rx_a, half_a, s, sems, 0)))
    resid = tokens_ref[...].astype(jnp.float32) + branch
    resid_ref[...] = resid
    gain = small_ref[1:2, :]
    router = small_ref[...].astype(jnp.bfloat16)
    normed_ref[s] = (resid * scale_of(resid) * gain).astype(jnp.bfloat16)
    gather = Task(ring_gather(normed_ref, s, sems, 8))
    gather.step()

    def block(place):
        x = normed_ref[place]
        logits = nt(router, x)
        logits = jnp.concatenate([logits[2 : 2 + EXPERTS], jnp.full((4, 128), NEGATIVE)], axis=0)
        probs = jnp.exp(logits - jnp.max(logits, axis=0, keepdims=True))
        probs = probs / jnp.sum(probs, axis=0, keepdims=True)
        probs_ref[place] = probs
        share = jnp.concatenate([probs * chosen_ref[place], jnp.zeros((120, 128))], axis=0)
        share = jnp.transpose(share)
        plain = nt(cotangent_ref[place], down_ref[...])
        both = nn(x, gate_up_ref[...])
        sums = []
        for e in range(EXPERTS):
            at = slice(e * per, (e + 1) * per)
            gate, up = both[:, at], both[:, units + e * per : units + (e + 1) * per]
            wide = jnp.broadcast_to(share[:, e : e + 1], gate.shape)
            sigmoid = 1.0 / (1.0 + jnp.exp(-gate))
            silu = gate * sigmoid
            hidden = (silu * up).astype(jnp.bfloat16).astype(jnp.float32)
            shared_ref[rows_at(place), at] = (hidden * wide).astype(jnp.bfloat16)
            sums.append(jnp.sum(plain[:, at] * hidden, axis=1, keepdims=True))
            d_hidden = plain[:, at] * wide
            d_gate = d_hidden * up * sigmoid * (1.0 + gate * (1.0 - sigmoid))
            d_ref[rows_at(place), at] = d_gate.astype(jnp.bfloat16)
            d_ref[rows_at(place), units + e * per : units + (e + 1) * per] = (
                d_hidden * silu
            ).astype(jnp.bfloat16)
        sums = jnp.concatenate(sums + [jnp.zeros((128, 128 - EXPERTS))], axis=1)
        share_tx[place] = jnp.transpose(sums)[:8]

    block(s)
    gather.step()
    gather.step()
    block(p["down"])
    block(p["up"])
    gather.step()
    block(p["over"])
    gather.step()
    block(p["far"])
    block(p["over_up"])
    block(p["over_down"])
    run(gather)
    block(p["over_far"])
    shares = exchange(share_tx, share_in, s, peers, at_seq, sems, 24)
    share_in[s] = share_tx[s]

    def weight_grads():
        shared, grad = shared_ref[...], cotangent_ref[...].reshape(8 * 128, model)
        value = tn(shared, grad).astype(jnp.bfloat16)
        yield
        grad_down[...] = nn(unit_order(1), value).astype(jnp.bfloat16)
        down_sum = Task(
            fsdp_scatter(
                grad_down, 32, 16, (pair_b, tops_b, bottoms_b, full_b), g, sems, 55
            )
        )
        down_sum.step()
        yield
        for third in range(3):

            @pl.loop(0, 4)
            def _(j, third=third):
                at = rows_at(third * 4 + j)
                normed = normed_ref[:, :, at].reshape(8 * 128, 128)
                grad_gate_up[at, :] = tn(normed, d_ref[...]).astype(jnp.bfloat16)

            yield
        gate_up_sum = Task(
            fsdp_scatter(
                grad_gate_up, 96, 48, (pair_a, tops_a, bottoms_a, full_a), g, sems, 38
            )
        )
        while not (down_sum.done and gate_up_sum.done):
            gate_up_sum.step()
            down_sum.step()
            yield
        part_gate_up_ref[...] = gate_up_sum.value.astype(jnp.bfloat16)
        part_down_ref[...] = down_sum.value.astype(jnp.bfloat16)

    grads = Task(weight_grads())

    def normed_part(place):
        return nt(d_ref[rows_at(place), :], gate_up_ref[...])

    d_normed = run(Task(ring_scatter(normed_part, tx_b, rx_b, half_b, s, sems, 16)), grads)
    for copy in shares:
        copy.wait_recv()

    d_router = jnp.sum(share_in[...], axis=0) * chosen_ref[s]
    probs = probs_ref[s]
    d_logits = probs * (d_router - jnp.sum(probs * d_router, axis=0, keepdims=True))
    d_logits = d_logits.astype(jnp.bfloat16)
    logits_ref[s] = d_logits.astype(jnp.float32)
    spreads = spread(logits_ref.at[s], logits_ref, s, peers, at_seq, sems, 31)
    padded = jnp.concatenate([jnp.zeros((2, 128), jnp.bfloat16), d_logits[:6]], axis=0)
    d_normed = d_normed + tn(padded, router)
    resid = resid_ref[...]
    scale = scale_of(resid)
    d_resid = cotangent_ref[s].astype(jnp.float32) + rms_back(
        d_normed, resid * scale, scale, gain
    )
    d_resid_ref[...] = d_resid
    branch_ref[s] = d_resid.astype(jnp.bfloat16)
    run_all(Task(ring_gather(branch_ref, s, sems, 72)), grads)
    for copy in spreads:
        copy.wait_recv()
    total = jnp.zeros((8, model), jnp.float32)
    for q in range(8):
        total += nn(logits_ref[q].astype(jnp.bfloat16), normed_ref[q])
    router_ref[...] = total
    for copy in shares + spreads:
        copy.wait_send()


def moe(attended, wout, tokens, small, gate_up, down, cotangent, chosen):
    own, model = tokens.shape
    rows = 8 * own
    width, units = gate_up.shape[1], down.shape[0]
    f32 = jnp.float32
    tiny = pltpu.VMEM((8, 8, own), f32)
    return pl.pallas_call(
        moe_kernel,
        in_specs=[VMEM] * 8,
        out_specs=[VMEM] * 7,
        out_shape=[
            array((own, model), f32),
            array((rows, units)),
            array((own, model), f32),
            array((8, own, model)),
            array((8, model), f32),
            array((model // 16, width)),
            array((units // 16, model)),
        ],
        scratch_shapes=[
            pltpu.VMEM((8, own, model), jnp.bfloat16),
            pltpu.VMEM((rows, width), jnp.bfloat16),
            pltpu.VMEM((model, width), jnp.bfloat16),
            pltpu.VMEM((units, model), jnp.bfloat16),
            tiny,
            tiny,
            tiny,
            tiny,
            *ring_buffers(own, model),
            *ring_buffers(own, model),
            *fsdp_buffers(model // 16, 48, width),
            *fsdp_buffers(units // 16, 16, model),
            *sem_pair(80),
        ],
        compiler_params=kernel_params(4),
        name="moe",
    )(attended, wout, tokens, small, gate_up, down, cotangent, chosen)


def finish_kernel(
    dq_ref, dkv_ref, weight_ref, normed_ref, attended_ref, branch_ref, router_ref, experts_ref,
    d_resid_ref, tokens_ref, small_ref,
    grad_input_ref, columns_out, experts_out, wout_out,
    d_ref, grads, grads_wout, columns_tx, experts_tx, wout_tx, tx, rx, rx_half,
    pair_a, tops_a, bottoms_a, full_a, pair_b, tops_b, bottoms_b, full_b,
    send_sems, recv_sems,
):
    s, g = lax.axis_index("seq"), lax.axis_index("fsdp")
    peers = others(s, 8)
    sems = (send_sems, recv_sems)
    holder, owner = head_holder(g, s), head_owner(g, s)
    alone = (holder["fsdp"] == g) & (holder["seq"] == s)
    greet_all([at_seq(q) for q in peers] + fsdp_neighbours(g), (holder, owner), alone)
    experts_tx[...] = expand(experts_ref[...], 12).reshape(experts_tx.shape)
    copies = exchange(experts_tx, experts_out, s, peers, at_seq, sems, 8)
    experts_out[s] = experts_tx[s]
    d_ref[:, :SMALL] = dq_ref[...]
    d_ref[:, SMALL:KEYS] = jnp.zeros((d_ref.shape[0], WIDTH), jnp.bfloat16)
    d_ref[:, KEYS:] = dkv_ref[...]

    def partial(place):
        return nt(d_ref[rows_at(place), :], weight_ref[...])

    def weight_grads():
        d = d_ref[...]
        lane = lax.broadcasted_iota(jnp.int32, (128, KEYS - 2 * WIDTH), 1)

        @pl.loop(0, normed_ref.shape[1] // 128)
        def _(j):
            at = rows_at(j)
            value = tn(normed_ref[:, at], d)
            router = jnp.concatenate(
                [jnp.zeros((WIDTH + 2, 128)), router_ref[:, at], jnp.zeros((54, 128))], axis=0
            )
            router = jnp.transpose(router)
            grads[at, : 2 * WIDTH] = value[:, : 2 * WIDTH].astype(jnp.bfloat16)
            grads[at, 2 * WIDTH : KEYS] = jnp.where(
                lane < WIDTH, value[:, 2 * WIDTH : KEYS], router
            ).astype(jnp.bfloat16)
            grads[at, KEYS:] = value[:, KEYS:].astype(jnp.bfloat16)

        main = Task(
            fsdp_scatter(grads, 96, 48, (pair_a, tops_a, bottoms_a, full_a), g, sems, 15)
        )
        main.step()
        yield
        value = tn(attended_ref[...], branch_ref[...].reshape(d.shape[0], -1)).astype(jnp.bfloat16)
        grads_wout[...] = expand(value, 12)
        wout = Task(
            fsdp_scatter(grads_wout, 16, 16, (pair_b, tops_b, bottoms_b, full_b), g, sems, 32)
        )
        while not main.done:
            main.step()
            wout.step()
            yield
        columns_tx[...] = expand(main.value.astype(jnp.bfloat16), 12).reshape(columns_tx.shape)
        copies.extend(exchange(columns_tx, columns_out, s, peers, at_seq, sems, 49))
        columns_out[s] = columns_tx[s]
        yield
        while not wout.done:
            wout.step()
            yield
        wout_tx[...] = wout.value.astype(jnp.bfloat16)
        return swap_rows(wout_tx, wout_out, sems, 56, owner, alone)

    weights = Task(weight_grads())
    d_normed = run(Task(ring_scatter(partial, tx, rx, rx_half, s, sems, 0)), weights)
    values = tokens_ref[...].astype(jnp.float32)
    scale = scale_of(values)
    grad_input_ref[...] = d_resid_ref[...] + rms_back(
        d_normed, values * scale, scale, small_ref[0:1, :]
    )
    wait_rows = run(weights)
    wait_rows()
    for copy in copies:
        copy.wait_recv()
    for copy in copies:
        copy.wait_send()


def finish(dq, dkv, weight, normed, attended, branch, router, experts, d_resid, tokens, small):
    own, model = tokens.shape
    rows = dq.shape[0]
    width = weight.shape[1]
    columns = (8, 16, width)
    blocks = (8, 16, experts.shape[1])
    bf16 = jnp.bfloat16
    return pl.pallas_call(
        finish_kernel,
        in_specs=[VMEM] * 11,
        out_specs=[VMEM] * 4,
        out_shape=[
            array((own, model), jnp.float32),
            array(columns),
            array(blocks),
            array((16, model)),
        ],
        scratch_shapes=[
            pltpu.VMEM((rows, width), bf16),
            pltpu.VMEM((model, width), bf16),
            pltpu.VMEM((256, model), bf16),
            pltpu.VMEM(columns, bf16),
            pltpu.VMEM(blocks, bf16),
            pltpu.VMEM((16, model), bf16),
            *ring_buffers(own, model),
            *fsdp_buffers(model // 16, 48, width),
            *fsdp_buffers(16, 16, model),
            *sem_pair(57),
        ],
        compiler_params=kernel_params(5),
        name="finish",
    )(dq, dkv, weight, normed, attended, branch, router, experts, d_resid, tokens, small)


def columns_by_owner(fsdp, seq, total):
    inner = total // (fsdp * seq)
    place = np.arange(total).reshape(fsdp, seq, inner).transpose(1, 0, 2).reshape(-1)
    one_hot = np.zeros((total, total), np.float32)
    one_hot[place, np.arange(total)] = 1
    return jnp.asarray(one_hot, jnp.bfloat16)


def pad_rows(x, axis):
    pads = [(0, 0)] * x.ndim
    pads[axis] = (0, 16 - x.shape[axis])
    return jnp.pad(x, pads)


def on_device(
    tokens,
    gain_one,
    w_qkv,
    w_out,
    gain_two,
    w_router,
    w_gate,
    w_up,
    w_down,
    doc_starts,
    routes,
    cotangent,
):
    seq = lax.axis_size("seq")
    fsdp = lax.axis_size("fsdp")
    group_index = lax.axis_index("fsdp")
    own, model = tokens.shape
    group_rows = own * seq
    experts, own_model, ff = w_gate.shape
    own_ff = ff // seq
    order = columns_by_owner(fsdp, seq, ff)
    bf16, f32 = jnp.bfloat16, jnp.float32

    gate_up = nn(
        jnp.concatenate([w_gate, w_up], axis=0).reshape(2 * experts * own_model, ff), order
    ).astype(bf16)
    gate_up = gate_up.reshape(2 * experts, own_model, seq, own_ff)
    gate_up = jnp.transpose(gate_up, (2, 1, 0, 3)).reshape(seq, own_model, 2 * experts * own_ff)
    qkv_parts = jnp.transpose(w_qkv.reshape(own_model, seq, 5 * WIDTH), (1, 0, 2))
    small = jnp.concatenate([gain_one[:, None], gain_two[:, None], w_router], axis=1)
    small = jnp.pad(small, ((0, 0), (0, WIDTH - small.shape[1])))
    columns = jnp.concatenate(
        [
            qkv_parts[:, :, :SMALL],
            jnp.broadcast_to(small[None], (seq,) + small.shape),
            qkv_parts[:, :, SMALL:],
        ],
        axis=2,
    )
    expert_ids = jnp.arange(8, dtype=jnp.int32)
    chosen = jnp.sum((routes[None, :, :] == expert_ids[:, None, None]).astype(f32), axis=2)
    normed_one, queries, keyval, weight, small, gate_up, down, out_weight, chosen = start(
        tokens,
        pad_rows(columns, 1),
        pad_rows(gate_up, 1),
        w_down.reshape(-1, model),
        pad_rows(w_out, 0),
        chosen,
    )

    window, cotangent_all = window_of(keyval, cotangent)
    window = window.reshape((LOOK + 1) * group_rows, 2 * WIDTH)
    positions = group_index * group_rows + jnp.arange(group_rows, dtype=jnp.int32)
    begins = jnp.max(
        jnp.where(doc_starts[:, None] <= positions[None, :], doc_starts[:, None], 0), axis=0
    )
    lo = begins - (group_index - LOOK) * group_rows
    blocks = group_rows // BQ
    lo_blocks = lo.reshape(blocks, BQ)
    diag = (LOOK * group_rows + jnp.arange(blocks, dtype=jnp.int32) * BQ) // BK
    end = (LOOK * group_rows + (jnp.arange(blocks, dtype=jnp.int32) + 1) * BQ + BK - 1) // BK
    first = jnp.minimum(lo_blocks[:, 0] // BK, diag)
    full = jnp.minimum((lo_blocks[:, -1] + BK - 1) // BK, diag)
    bounds = jnp.stack([first, full, diag, end], axis=1)
    attended, lse = attention(bounds, lo[None, :], queries, window)

    residual, shared, d_resid, d_branch, grad_router, part_gate_up, part_down = moe(
        attended, out_weight, tokens, small, gate_up, down, cotangent_all, chosen
    )

    d_attended = nt(d_branch.reshape(group_rows, model), out_weight).astype(bf16)
    d_queries, d_window = attention_back(
        bounds, lo[None, :], queries, window, attended, d_attended, lse
    )
    d_keyval, output = window_back(
        d_window.reshape(LOOK + 1, group_rows, 2 * WIDTH), shared, down, residual
    )
    grad_input, columns, back, shard_out = finish(
        d_queries, d_keyval, weight, normed_one, attended, d_branch, grad_router, part_gate_up,
        d_resid, tokens, small,
    )

    shard_down = part_down.astype(f32).reshape(experts, -1, model)
    shard_out = shard_out[:own_model].astype(f32)
    columns = columns[:, :own_model].astype(f32)
    shard_qkv = jnp.concatenate([columns[:, :, :SMALL], columns[:, :, KEYS:]], axis=2)
    shard_qkv = jnp.transpose(shard_qkv, (1, 0, 2)).reshape(own_model, -1)
    shard_router = columns[0, :, SMALL + 2 : SMALL + 2 + experts]
    back = back[:, :own_model].reshape(seq, own_model, 2 * experts, own_ff)
    back = jnp.transpose(back, (2, 1, 0, 3)).reshape(2 * experts * own_model, ff)
    back = nt(back, order).reshape(2 * experts, own_model, ff)
    shard_gate, shard_up = back[:experts], back[experts:]

    shard_gain_one = jnp.sum(w_qkv.astype(f32) * shard_qkv, axis=1)
    shard_gain_one = shard_gain_one / gain_one.astype(f32)
    shard_gain_two = jnp.sum(w_router.astype(f32) * shard_router, axis=1)
    shard_gain_two += jnp.sum(w_gate.astype(f32) * shard_gate, axis=(0, 2))
    shard_gain_two += jnp.sum(w_up.astype(f32) * shard_up, axis=(0, 2))
    shard_gain_two = shard_gain_two / gain_two.astype(f32)
    return (
        output,
        grad_input,
        shard_gain_one,
        shard_qkv,
        shard_out,
        shard_gain_two,
        shard_router,
        shard_gate,
        shard_up,
        shard_down,
    )


def solution(mesh):
    rows, vector = P(BOTH, None), P(BOTH)
    middle = P(None, BOTH, None)
    in_specs = (
        rows, vector, rows, rows, vector, rows, middle, middle, middle, P(), rows, rows,
    )
    out_specs = (rows, rows, vector, rows, rows, vector, rows, middle, middle, middle)
    return jax.shard_map(
        on_device, mesh=mesh, in_specs=in_specs, out_specs=out_specs, check_vma=False
    )
```

time: 641 us -> 410 us (0.64)
  waiting for transfers between devices: 110 us -> 0 us
  Pallas kernels: 318 us -> 379 us
  local copies, waits for them, and re-layouts: 53.6 us -> 10.4 us
  blocking collectives: 37.3 us -> 0 us
  matrix products: 42.1 us -> 5.06 us
  starting transfers between devices: 35.8 us -> 0 us
  between operations: 15.2 us -> 1.3 us
  other arithmetic: 16.4 us -> 6.62 us
    reduce_scatter x3 -> x0, waiting for transfers between devices: 75.4 us -> none  [the longest x2 75.4 us: scatter_fsdp(): lax.psum_scatter(x.astype(jnp.bfloat16), 'fsdp', scatter_dimension=dim, t...]
    pallas_call x6 -> x5, Pallas kernels: 298 us -> 358 us  [the longest x1 145 us: moe(): pl.pallas_call(moe_kernel, in_specs=[VMEM] * 8, out_specs=[VMEM] * 7, out...]
    all_gather x1 -> x0, blocking collectives: 37.3 us -> none  [gather_fsdp(): return lax.all_gather(x, 'fsdp', axis=dim, tiled=True)]
    unnamed x8 -> x0, waiting for transfers between devices: 34.1 us -> none
    ppermute x2 -> x0, starting transfers between devices: 25.5 us -> none  [the longest x1 22.2 us: on_device(): lax.ppermute(part_out[0, :own_model], BOTH, [(b, a) for a, b in head_rows...]
    unnamed x117 -> x46, local copies, waits for them, and re-layouts: 25.2 us -> 6.18 us
    dot_general x4 -> x0, matrix products: 15.7 us -> none  [tn(): lax.dot_general(a, b, (((0,), (0,)), ((), ())), preferred_element_type=jn...]
    dot_general x5 -> x1, matrix products: 15.3 us -> 0.48 us  [nn(): return jnp.dot(a, b, preferred_element_type=jnp.float32)]
  transfers between devices with their start and end apart: 9 -> 0, of which waited for: 2 -> 0; matrix products, arithmetic and copies ran while one was open for 11% -> 0% of each run, Pallas kernels for 42% -> 0%
where the time goes in v3:
time: 410 us; the launch traced here: 402 us
  Pallas kernels  379 us (92%)
  local copies, waits for them, and re-layouts  10.4 us (3%)
  other arithmetic  6.62 us (2%)
  matrix products  5.06 us (1%)
    pallas_call x1, Pallas kernels, moe(): pl.pallas_call(moe_kernel, in_specs=[VMEM] * 8, out_specs=[VMEM] * 7, out...  145 us
    pallas_call x1, Pallas kernels, finish(): pl.pallas_call(finish_kernel, in_specs=[VMEM] * 11, out_specs=[VMEM] * 4,...  76.1 us
    pallas_call x1, Pallas kernels, start(): pl.pallas_call(start_kernel, in_specs=[VMEM] * 6, out_specs=[VMEM] * 9, o...  61.1 us
    pallas_call x1, Pallas kernels, window_back(): pl.pallas_call(window_back_kernel, in_specs=[VMEM] * 4, out_specs=[VMEM]...  39.6 us
    pallas_call x1, Pallas kernels, window_of(): pl.pallas_call(window_kernel, in_specs=[VMEM] * 2, out_specs=[VMEM] * 2,...  35.7 us
    pallas_call x1, Pallas kernels, attention_back(): pl.pallas_call(attention_back_kernel, grid=(blocks,), in_specs=[pl.BlockS...  11.7 us
    pallas_call x1, Pallas kernels, attention(): pl.pallas_call(attention_kernel, grid=(blocks,), in_specs=[pl.BlockSpec(m...  9.55 us

profile of v3, /device:TPU:3, one launch (start us, length us, event | category | flops | bytes accessed | tf_op | source)
XLA Modules:
  0.0 402.4 jit_solution(17747142176084664344)
XLA Ops:
  0.7 0.9 pad_maximum_fusion.1
  1.6 0.8 select_reduce_fusion
  2.5 0.7 convert_reduce_fusion.chosen_ref
  3.3 0.8 pad.19.wout_ref
  4.1 1.0 reshape.197
  5.3 1.0 pad_maximum_fusion
  7.6 61.1 %start.1 = (bf16[1024,1536]{1,0:T(8,128)(2,1)}, bf16[1024,192]{1,0:T(8,128)(2,1)S(1)}, bf16[1024,128]{1,0:T(8,128)(2,1)S(1)}, bf16[1536,384]{1,0:T(8,128)(2,1)},...) custom-call(bf16[128,1536]{1,0:T(8,128)(2,1)S(1)} %copy-done, ...), custom_call_target="tpu_custom_call" | custom-call | tf_op jit(solution)/shard_map/start/pallas_call | solution.py:697
  68.7 35.7 %window.1 = (bf16[5,1024,128]{2,1,0:T(8,128)(2,1)S(1)}, bf16[8,128,1536]{2,1,0:T(8,128)(2,1)}) custom-call(bf16[1024,128]{1,0:T(8,128)(2,1)S(1)} %get-tuple-element.39.kv_ref, bf16[128,1536]{1,0:T(8,128)(2,1)S(1)} %copy-done.5), custom_call_target="tpu_custom_call" | custom-call | tf_op jit(solution)/shard_map/window/pallas_call | solution.py:764
  104.5 9.5 %attention.1 = (bf16[1024,192]{1,0:T(8,128)(2,1)S(1)}, f32[4,8,768]{2,1,0:T(8,128)S(1)}) custom-call(s32[4,4]{1,0:T(4,128)S(1)} %pad_add_fusion.bounds_ref, s32[1,1024]{1,0:T(1,128)S(1)} %bitcast.44, bf16[1024,192]{1,0:T(8,128)(2,1)S(1)} %get-tuple-element.38.q_ref, bf16[5120,128]{1,0:T(8,128)(2,1)S(1)} %bitcast.46), custom_call_target="tpu_custom_call" | custom-call | flops 3221225472 | bytes 4194304 | tf_op jit(solution)/shard_map/attention/pallas_call | solution.py:89
  114.0 145.3 %moe.1 = (f32[128,1536]{1,0:T(8,128)}, bf16[1024,512]{1,0:T(8,128)(2,1)}, f32[128,1536]{1,0:T(8,128)}, bf16[8,128,1536]{2,1,0:T(8,128)(2,1)}, f32[8,1536]{1,0:T(...) custom-call(bf16[1024,192]{1,0:T(8,128)(2,1)S(1)} %get-tuple-element.41.attended_ref.out_ref, ...), custom_call_target="tpu_custom_call" | custom-call | tf_op jit(solution)/shard_map/moe/pallas_call | solution.py:990
  259.3 3.8 convolution_convert_fusion
  263.1 1.2 copy.66.dout_ref
  264.3 0.7 bitcast_convert_fusion
  265.0 1.0 copy-done.8
  266.1 11.7 %attention_back.1 = (bf16[1024,192]{1,0:T(8,128)(2,1)S(1)}, f32[5120,128]{1,0:T(8,128)S(1)}) custom-call(s32[4,4]{1,0:T(4,128)S(1)} %pad_add_fusion.bounds_ref, s32[1,1024]{1,0:T(1,128)S(1)} %bitcast.45, bf16[1024,192]{1,0:T(8,128)(2,1)S(1)} %copy-done.8, bf16[5120,128]{1,0:T(8,128)(2,1)S(1)} %bitcast.47, ...), custom_call_target="tpu_custom_call" | custom-call | flops 8053063680 | bytes 8388608 | tf_op jit(solution)/shard_map/attention_back/pallas_call | solution.py:165
  277.8 1.5 copy-done.1
  279.4 39.6 %window_back.1 = (bf16[1024,128]{1,0:T(8,128)(2,1)S(1)}, bf16[128,1536]{1,0:T(8,128)(2,1)S(1)}) custom-call(f32[5,1024,128]{2,1,0:T(8,128)} %bitcast.41, bf16[1024,512]{1,0:T(8,128)(2,1)} %get-tuple-element.51.shared_ref, bf16[512,1536]{1,0:T(8,128)(2,1)} %get-tuple-element.45.down_ref, f32[128,1536]{1,0:T(8,128)S(1)} %copy-done.3), custom_call_target="tpu_custom_call" | custom-call | tf_op jit(solution)/shard_map/window_back/pallas_call | solution.py:825
  319.0 76.1 %finish.1 = (f32[128,1536]{1,0:T(8,128)}, bf16[8,16,384]{2,1,0:T(8,128)(2,1)S(1)}, bf16[8,16,1024]{2,1,0:T(8,128)(2,1)S(1)}, bf16[16,1536]{1,0:T(8,128)(2,1)S(1)}) custom-call(bf16[1024,192]{1,0:T(8,128)(2,1)S(1)} %get-tuple-element.54.dq_ref, bf16[1024,128]{1,0:T(8,128)(2,1)S(1)} %get-tuple-element.55.dkv_ref, ...), custom_call_target="tpu_custom_call" | custom-call | tf_op jit(solution)/shard_map/finish/pallas_call | solution.py:1111
  395.1 0.6 slice_convert_fusion.1
  397.2 0.8 fusion.4
  398.3 0.8 copy.73
  399.3 0.8 copy.74
  400.6 0.7 copy.90
  401.4 0.9 copy.91
  (78 shorter events, 4.0 us)
Async XLA Ops:
  0.6 5.9 %copy-start.9 = (bf16[1024,1024]{1,0:T(8,128)(2,1)S(1)}, bf16[1024,1024]{1,0:T(8,128)(2,1)}, u32[]{:S(2)}) copy-start(bf16[1024,1024]{1,0:T(8,128)(2,1)} %constant.69.clone) | copy-start | bytes 6291460
  6.6 1.0 copy-start
  6.6 1.0 copy-start.6
  7.1 61.6 %copy-start.5 = (bf16[128,1536]{1,0:T(8,128)(2,1)S(1)}, bf16[128,1536]{1,0:T(8,128)(2,1)}, u32[]{:S(2)}) copy-start(bf16[128,1536]{1,0:T(8,128)(2,1)} %cotangent_ref.1) | copy-start | bytes 1179652
  68.7 45.3 %copy-start.7 = (bf16[1024,192]{1,0:T(8,128)(2,1)}, bf16[1024,192]{1,0:T(8,128)(2,1)S(1)}, u32[]{:S(2)}) copy-start(bf16[1024,192]{1,0:T(8,128)(2,1)S(1)} %get-tuple-element.38.q_ref) | copy-start | bytes 1179652
  104.4 9.6 %copy-start.4 = (bf16[192,1536]{1,0:T(8,128)(2,1)S(1)}, bf16[192,1536]{1,0:T(8,128)(2,1)}, u32[]{:S(2)}) copy-start(bf16[192,1536]{1,0:T(8,128)(2,1)} %get-tuple-element.42.wout_ref) | copy-start | bytes 1769476
  114.0 151.0 %copy-start.2 = (bf16[1024,192]{1,0:T(8,128)(2,1)}, bf16[1024,192]{1,0:T(8,128)(2,1)S(1)}, u32[]{:S(2)}) copy-start(bf16[1024,192]{1,0:T(8,128)(2,1)S(1)} %get-tuple-element.41.attended_ref.out_ref) | copy-start | bytes 1179652
  265.0 1.0 copy-start.8
  266.1 13.3 %copy-start.3 = (f32[128,1536]{1,0:T(8,128)S(1)}, f32[128,1536]{1,0:T(8,128)}, u32[]{:S(2)}) copy-start(f32[128,1536]{1,0:T(8,128)} %get-tuple-element.52.resid_ref) | copy-start | bytes 2359300
  277.8 1.6 copy-start.1
  319.0 77.0 %copy-start.17 = (bf16[12,4]{0,1:T(4,128)(2,1)S(1)}, bf16[12,4]{0,1:T(4,128)(2,1)}, u32[]{:S(2)}) copy-start(bf16[12,4]{0,1:T(4,128)(2,1)} %param.18) | copy-start | bytes 292
  319.0 77.3 %copy-start.15 = (bf16[12,2560]{1,0:T(8,128)(2,1)S(1)}, bf16[12,2560]{1,0:T(8,128)(2,1)}, u32[]{:S(2)}) copy-start(bf16[12,2560]{1,0:T(8,128)(2,1)} %param.15) | copy-start | bytes 184324
  395.1 1.3 copy-start.19
  395.1 2.1 copy-start.10
  395.9 2.0 copy-start.16
  396.3 1.8 copy-start.12
  397.1 1.0 copy-start.13
  397.2 1.9 copy-start.14
  398.0 2.1 copy-start.18
  398.0 3.4 copy-start.11
